TPU v7x, 512 devices: a whole 4x4x16 slice. The times are simulated.
512 devices in a mesh: rep: 64 (over z_lo, y, core), tp: 8 (over x, z_hi).
Axes of the slice: x: 4, y: 4, z: 16 (z_hi: 2, z_lo: 8; z = z_hi * 8 + z_lo), core: 2. Of those that a mesh axis runs over, the one named last changes fastest.
Arguments:
- context: bfloat16 [2, 32768, 2048], P(None, 'rep', 'tp'), may hold values from -6 to 6
- residual: bfloat16 [2, 32768, 2304], P(None, 'rep', 'tp'), may hold values from -40 to 40, as said below
- targets: bfloat16 [2, 32768, 2304], P(None, 'rep', 'tp'), may hold values from -6 to 6
- gain: float32 [2304], P('tp'), may hold values from 0.1 to 1.9
- slow_weight: bfloat16 [2048, 2304], P(None, 'tp'), may hold values from -0.125 to 0.125
- momentum: float32 [2048, 2304], P('rep', 'tp'), may hold values from -4 to 4
- shares: float32 [2, 64], P(None, 'rep'), may hold values from 0.3 to 0.7
Outputs:
- new_weight: float32 [2048, 2304], P('rep', 'tp')
- new_momentum: float32 [2048, 2304], P('rep', 'tp')
- push_mass: float32 [64], P('rep')
Inputs may be any that keep to these rules, and one draw needn't show every extreme that they name: `residual`: Real-valued.
All inputs are finite; a program needn't handle non-finite values.
Results may differ from a plain program's by a relative error of at most 0.0045.
Values may be sent and summed in bfloat16 or wider, within the bound.
No kernel may reach another device: no remote copies, remote signals or barrier semaphores. Data moves between devices by JAX's collectives and lax.ppermute only.
A program may use at most 64 MiB of HBM per device.

v0:
```python
import jax
import jax.numpy as jnp
from jax import lax
from jax.sharding import PartitionSpec as P

D = 2304
STEPS = 2
TOK = 512


LR = 0.005
BETA = 0.7
ALPHA = 1.0
EPS = 1e-06


def passed_along(value, axis, steps):
    count = lax.axis_size(axis)
    pairs = [(source, (source + steps) % count) for source in range(count)]
    return lax.ppermute(value, axis, pairs)


def contract_rows(left, right):
    return lax.dot_general(
        left, right, (((0,), (0,)), ((), ())), preferred_element_type=jnp.float32
    )


def body(context, residual, targets, gain, slow_weight, momentum, shares):
    anchor = slow_weight.astype(jnp.float32)
    numerator = anchor
    push_mass = jnp.ones((1,), jnp.float32)
    scale = TOK ** (-0.5)
    for step in range(STEPS):
        quotient = (numerator / push_mass).astype(jnp.bfloat16)
        context_step = context[step]
        residual_step = residual[step].astype(jnp.float32)
        target_step = targets[step].astype(jnp.float32)
        gathered = lax.all_gather(context_step, "tp", axis=1, tiled=True)
        output = residual_step + jnp.dot(gathered, quotient, preferred_element_type=jnp.float32)
        total_sq = lax.psum(jnp.sum(output * output, axis=1), "tp")
        root_mean = jnp.sqrt(total_sq / D + EPS)
        normed = output / root_mean[:, None]
        normed_grad = scale * gain * (gain * normed - target_step)
        projection = lax.psum(jnp.sum(normed_grad * normed, axis=1), "tp") / D
        output_grad = ((normed_grad - normed * projection[:, None]) / root_mean[:, None]).astype(
            jnp.bfloat16
        )
        weight_grad = contract_rows(gathered, output_grad)
        stepped = numerator - LR * weight_grad
        kept_share = shares[step, 0]
        outgoing = ((1.0 - kept_share) * stepped).astype(jnp.bfloat16)
        incoming_mass = passed_along((1.0 - kept_share) * push_mass, "rep", step + 1)
        push_mass = kept_share * push_mass + incoming_mass
        incoming = passed_along(outgoing, "rep", step + 1)
        numerator = kept_share * stepped + incoming.astype(jnp.float32)
    debiased = numerator / push_mass
    replicas = lax.axis_size("rep")
    row_count = debiased.shape[0] // replicas
    offset = lax.axis_index("rep") * row_count
    summed = lax.psum(debiased, "rep")
    own_sum = lax.dynamic_slice_in_dim(summed, offset, row_count, 0)
    average = own_sum / replicas
    anchor_rows = lax.dynamic_slice_in_dim(anchor, offset, row_count, 0)
    new_momentum = BETA * momentum + (anchor_rows - average) / LR
    new_weight = anchor_rows - ALPHA * LR * new_momentum
    return (new_weight, new_momentum, push_mass)


def solution(mesh):
    return jax.shard_map(
        body,
        mesh=mesh,
        in_specs=(
            P(None, "rep", "tp"),
            P(None, "rep", "tp"),
            P(None, "rep", "tp"),
            P("tp"),
            P(None, "tp"),
            P("rep", "tp"),
            P(None, "rep"),
        ),
        out_specs=(P("rep", "tp"), P("rep", "tp"), P("rep")),
        check_vma=False,
    )
```

profile of v0, /device:TPU:2, one launch (start us, length us, event | category | flops | bytes accessed | tf_op | source)
XLA Modules:
  0.0 1215.4 jit_solution(15158500317249230519)
XLA Ops:
  7.2 0.0 all-gather.5.cloned.1.call-start
  7.2 1.9 fusion.35
  9.1 0.0 all-gather.5.cloned.1.call-update
  9.1 0.0 all-gather.7.cloned.1.call-start
  9.1 0.7 all-gather.7.cloned.1.call-update
  9.8 0.0 all-reduce.2.cloned.1.call-start
  9.9 1.3 fusion.36
  11.9 0.7 broadcast_multiply_fusion.2
  12.5 0.0 copy-start.1
  12.5 0.0 copy-start.2
  12.6 0.0 copy-start
  12.6 119.6 %all-gather.5.cloned.1.call-done = bf16[1,512,2048]{2,1,0:T(8,128)(2,1)} async-done(((bf16[1,512,256]{2,1,0:T(8,128)(2,1)}), bf16[1,512,2048]{2,1,0:T(8,128)(2,1)}) %all-gather.5.cloned.1.call-update) | async-done | bytes 2097168 | tf_op jit(solution)/shard_map/all_gather | solution.py:39
  132.1 2.8 multiply_reduce_fusion.3
  134.9 38.3 %psum.35 = f32[512]{0:T(512)S(1)} all-reduce(f32[512]{0:T(512)S(1)} %get-tuple-element.12), channel_id=1, replica_groups=mesh['rep'=64,'tp'=8] {'tp'}, use_global_device_ids=true, to_apply=%region_1.0 | all-reduce | flops 512 | bytes 4096 | tf_op jit(solution)/shard_map/psum | solution.py:41
  173.3 0.0 copy-done.1
  173.3 0.0 copy-done.2
  173.3 0.2 multiply_reduce_fusion.2
  173.5 67.1 %psum.36 = f32[512]{0:T(512)S(1)} all-reduce(f32[512]{0:T(512)S(1)} %multiply_reduce_fusion.2), channel_id=1, replica_groups=mesh['rep'=64,'tp'=8] {'tp'}, use_global_device_ids=true, to_apply=%region_3.0 | all-reduce | flops 512 | bytes 4096 | tf_op jit(solution)/shard_map/psum | solution.py:45
  240.6 0.0 copy-done
  240.6 4.4 multiply_convert_fusion.1
  245.0 1.9 collective-permute-start
  246.9 4.5 collective-permute-start.1
  252.1 19.7 %collective-permute-done.1 = f32[1]{0:T(128)} collective-permute-done((f32[1]{0:T(128)}, f32[1]{0:T(128)}, u32[]{:S(2)}, u32[]{:S(2)}) %collective-permute-start.1) | collective-permute-done | bytes 36 | tf_op jit(solution)/shard_map/ppermute | solution.py:20
  273.0 0.0 all-gather.7.cloned.1.call-done
  273.1 0.0 collective-permute-done
  273.1 0.0 copy-start.3
  273.1 3.8 multiply_reduce_fusion.1
  276.9 0.0 copy-done.3
  276.9 33.5 %psum.37 = f32[512]{0:T(512)S(1)} all-reduce(f32[512]{0:T(512)S(1)} %get-tuple-element.16), channel_id=1, replica_groups=mesh['rep'=64,'tp'=8] {'tp'}, use_global_device_ids=true, to_apply=%region_5.0 | all-reduce | flops 512 | bytes 4096 | tf_op jit(solution)/shard_map/psum | solution.py:41
  310.4 0.2 multiply_reduce_fusion
  310.7 44.2 %psum.38 = f32[512]{0:T(512)S(1)} all-reduce(f32[512]{0:T(512)S(1)} %multiply_reduce_fusion), channel_id=1, replica_groups=mesh['rep'=64,'tp'=8] {'tp'}, use_global_device_ids=true, to_apply=%region_7.0 | all-reduce | flops 512 | bytes 4096 | tf_op jit(solution)/shard_map/psum | solution.py:45
  354.9 4.4 multiply_convert_fusion
  359.2 1.9 collective-permute-start.2
  361.2 13.7 %collective-permute-start.3 = (f32[1]{0:T(128)}, f32[1]{0:T(128)}, u32[]{:S(2)}, u32[]{:S(2)}) collective-permute-start(f32[1]{0:T(128)} %mul.153), channel_id=1, source_target_pairs={{0,16},{8,24},{16,32},{24,40},{32,48},{40,56},{48,64},{56,72},{64,... | collective-permute-start | bytes 20 | tf_op jit(solution)/shard_map/ppermute | solution.py:20
  375.6 10.5 collective-permute-done.3
  386.8 0.0 collective-permute-done.2
  386.8 2.4 add_divide_fusion
  389.2 0.0 all-reduce.2.cloned.1.call-update
  389.2 0.3 convert_element_type.49
  389.5 0.9 copy.10
  390.4 814.9 %all-reduce.2.cloned.1.call-done = f32[2048,288]{0,1:T(8,128)} async-done(((f32[2048,288]{0,1:T(8,128)}), f32[2048,288]{0,1:T(8,128)}) %all-reduce.2.cloned.1.call-update) | async-done | bytes 2359312 | tf_op jit(solution)/shard_map/psum | solution.py:61
  1205.2 1.1 multiply_subtract_fusion
  1206.3 0.7 copy.11
  1207.0 0.7 copy.12
  (4 shorter events, 0.0 us)
Async XLA Ops:
  7.2 125.0 %all-gather.5.cloned.1.call-start = ((), (), s32[]{:S(2)}) async-start(), calls=%async_computation.1 | async-start | bytes 2359296 | tf_op jit(solution)/shard_map/all_gather | solution.py:39
  9.1 264.0 %all-gather.7.cloned.1.call-start = ((), (), s32[]{:S(2)}) async-start(), calls=%async_computation.2 | async-start | bytes 2359296 | tf_op jit(solution)/shard_map/all_gather | solution.py:39
  9.8 1195.4 %all-reduce.2.cloned.1.call-start = ((), (), s32[]{:S(2)}) async-start(), calls=%async_computation | async-start | bytes 4718592 | tf_op jit(solution)/shard_map/psum | solution.py:61
  12.5 160.7 %copy-start.1 = (bf16[2,512,288]{1,2,0:T(8,128)(2,1)S(1)}, bf16[2,512,288]{1,2,0:T(8,128)(2,1)}, u32[]{:S(2)}) copy-start(bf16[2,512,288]{1,2,0:T(8,128)(2,1)} %param.9) | copy-start | bytes 1769476
  12.5 160.7 %copy-start.2 = (f32[288]{0:T(512)S(1)}, f32[288]{0:T(512)}, u32[]{:S(2)}) copy-start(f32[288]{0:T(512)} %param.10) | copy-start | bytes 3460
  12.6 228.0 %copy-start = (bf16[2048,288]{0,1:T(8,128)(2,1)S(1)}, bf16[2048,288]{0,1:T(8,128)(2,1)}, u32[]{:S(2)}) copy-start(bf16[2048,288]{0,1:T(8,128)(2,1)} %param.11) | copy-start | bytes 3538948
  245.0 28.1 %collective-permute-start = (bf16[2048,288]{0,1:T(8,128)(2,1)}, bf16[2048,288]{0,1:T(8,128)(2,1)S(1)}, u32[]{:S(2)}, u32[]{:S(2)}) collective-permute-start(bf16[2048,288]{0,1:T(8,128)(2,1)} %get-tuple-element.14), channel_id=1, source_target_pairs={{0,8},{8,16},{16,24},{24,32},{32,40},{40,48},{48,56},{56,64},{64,7... | collective-permute-start | bytes 3538952 | tf_op jit(solution)/shard_map/ppermute | solution.py:20
  246.9 24.9 %collective-permute-start.1 = (f32[1]{0:T(128)}, f32[1]{0:T(128)}, u32[]{:S(2)}, u32[]{:S(2)}) collective-permute-start(f32[1]{0:T(128)} %bitcast.8), channel_id=1, source_target_pairs={{0,8},{8,16},{16,24},{24,32},{32,40},{40,48},{48,56},{56,64},{64,7... | collective-permute-start | bytes 20 | tf_op jit(solution)/shard_map/ppermute | solution.py:20
  273.1 3.8 copy-start.3
  359.2 27.5 %collective-permute-start.2 = (bf16[2048,288]{0,1:T(8,128)(2,1)S(1)}, bf16[2048,288]{0,1:T(8,128)(2,1)S(1)}, u32[]{:S(2)}, u32[]{:S(2)}) collective-permute-start(bf16[2048,288]{0,1:T(8,128)(2,1)S(1)} %get-tuple-element.18), channel_id=1, source_target_pairs={{0,16},{8,24},{16,32},{24,40},{32,48},{40,56},{48,64},{56,72},{64,... | collective-permute-start | bytes 3538952 | tf_op jit(solution)/shard_map/ppermute | solution.py:20
  361.2 24.9 %collective-permute-start.3 = (f32[1]{0:T(128)}, f32[1]{0:T(128)}, u32[]{:S(2)}, u32[]{:S(2)}) collective-permute-start(f32[1]{0:T(128)} %mul.153), channel_id=1, source_target_pairs={{0,16},{8,24},{16,32},{24,40},{32,48},{40,56},{48,64},{56,72},{64,... | collective-permute-start | bytes 20 | tf_op jit(solution)/shard_map/ppermute | solution.py:20
Sparse Core Ops, SparseCore 0:
  11.1 121.0 all-gather.4
  135.2 116.7 all-gather.6
  389.3 815.8 all-reduce.1
where the time goes:
time: 1220 us
  waiting for transfers between devices  965 us (79%)
  blocking collectives  183 us (15%)
  starting transfers between devices  22.2 us (2%)
  between operations  18.9 us (2%)
  matrix products  15.4 us (1%)
    psum x1, waiting for transfers between devices, body(): summed = lax.psum(debiased, 'rep')  815 us
    all_gather x2, waiting for transfers between devices, body(): gathered = lax.all_gather(context_step, 'tp', axis=1, tiled=True)  120 us
    psum x2, blocking collectives, body(): projection = lax.psum(jnp.sum(normed_grad * normed, axis=1), 'tp') / D  111 us
    psum x2, blocking collectives, body(): total_sq = lax.psum(jnp.sum(output * output, axis=1), 'tp')  71.9 us
    ppermute x4, waiting for transfers between devices, passed_along(): return lax.ppermute(value, axis, pairs)  30.2 us
  transfers between devices with their start and end apart: 7, of which 4 were waited for; matrix products, arithmetic and copies ran while one was open for 1% of the time, Pallas kernels for 0%

commit v1 on v0

v1 whole, which is shorter than its diff:
```python
import jax
import jax.numpy as jnp
from jax import lax
from jax.sharding import Mesh, PartitionSpec as P

D = 2304
TOK = 512
LR = 0.005
BETA = 0.7
ALPHA = 1.0
EPS = 1e-06
SCALE = TOK ** (-0.5)

AXES = ("z_lo", "y", "core", "x", "z_hi")
SIZES = (8, 4, 2, 4, 2)
REP = AXES[:3]
TP = AXES[3:]
F32 = jnp.float32
BF16 = jnp.bfloat16


def shifted(value, axis, steps):
    count = lax.axis_size(axis)
    return lax.ppermute(value, axis, [(i, (i + steps) % count) for i in range(count)])


def to_all(value, axis):
    count = lax.axis_size(axis)
    return lax.all_to_all(jnp.broadcast_to(value[None], (count,) + value.shape), axis, 0, 0)


def contract_rows(left, right):
    return lax.dot_general(left, right, (((0,), (0,)), ((), ())), preferred_element_type=F32)


def merged(own, other, hi):
    low = jnp.where(hi == 0, own, other)
    high = jnp.where(hi == 0, other, own)
    both = jnp.stack([low, high], axis=1)
    return jnp.transpose(both, (2, 0, 1, 3)).reshape(TOK, 2048)


def forward(gathered, quotient, residual, targets, gain):
    output = residual.astype(F32) + jnp.dot(gathered, quotient, preferred_element_type=F32)
    scaled = gain * output
    sums = jnp.stack(
        [
            jnp.sum(output * output, axis=1),
            jnp.sum(scaled * scaled, axis=1),
            jnp.sum(scaled * targets.astype(F32), axis=1),
        ]
    )
    return output, sums


def backward(output, totals, targets, gain):
    root_sq = totals[0] / D + EPS
    root = jnp.sqrt(root_sq)
    projection = SCALE * (totals[1] / root_sq - totals[2] / root) / D
    normed = output / root[:, None]
    normed_grad = SCALE * gain * (gain * normed - targets.astype(F32))
    return ((normed_grad - normed * projection[:, None]) / root[:, None]).astype(BF16)


def body(context, residual, targets, gain, slow_weight, momentum, shares):
    hi = lax.axis_index("z_hi")
    core = lax.axis_index("core")
    anchor = slow_weight.astype(F32)

    own_share = shares[:, 0]
    before = shifted(own_share, REP, 1)
    after = shifted(own_share, REP, -1)

    other0 = shifted(context[0], "z_hi", 1)
    x_own0 = to_all(context[0], "x")
    other0, x_own0 = lax.optimization_barrier((other0, x_own0))
    other1 = shifted(context[1], "z_hi", 1)
    x_own1 = lax.all_gather(context[1], "x", axis=0)
    x_other0 = to_all(other0, "x")
    gathered0 = merged(x_own0, x_other0, hi)

    output0, sums0 = forward(gathered0, slow_weight, residual[0], targets[0], gain)
    totals0 = jnp.sum(to_all(sums0, TP), axis=0)
    grad0 = backward(output0, totals0, targets[0], gain)
    weight_grad0 = contract_rows(gathered0, grad0)

    incoming = shifted(((1.0 - own_share[0]) * weight_grad0).astype(BF16), REP, 1)
    other1, weight_grad0 = lax.optimization_barrier((other1, weight_grad0))
    x_other1 = to_all(other1, "x")
    window = jnp.stack([before, own_share, after])
    earlier = shifted(window, REP, 2)
    later = shifted(window, REP, -2)
    gathered1 = merged(x_own1, x_other1, hi)

    mass1 = own_share[0] + (1.0 - before[0])
    step0 = own_share[0] * weight_grad0 + incoming.astype(F32)
    quotient1 = (anchor - (LR / mass1) * step0).astype(BF16)
    output1, sums1 = forward(gathered1, quotient1, residual[1], targets[1], gain)
    totals1 = jnp.sum(to_all(sums1, TP), axis=0)
    grad1 = backward(output1, totals1, targets[1], gain)
    weight_grad1 = contract_rows(gathered1, grad1)

    near = jnp.concatenate([earlier[:2], window, later[1:]])
    first = {k: near[k + 3, 0] for k in range(-3, 4)}
    second = {k: near[k + 3, 1] for k in range(-3, 4)}
    mass_of = {k: first[k] + (1.0 - first[k - 1]) for k in range(-2, 4)}
    final_of = {
        k: second[k] * mass_of[k] + (1.0 - second[k - 2]) * mass_of[k - 2] for k in range(0, 4)
    }
    part_of = {k: second[k] / final_of[k] + (1.0 - second[k]) / final_of[k + 2] for k in (0, 1)}
    replicas = lax.axis_size(REP)
    coef1 = part_of[0] / replicas
    coef0 = (part_of[0] * first[0] + part_of[1] * (1.0 - first[0])) / replicas
    total = coef0 * weight_grad0 + coef1 * weight_grad1

    width = total.shape[1]
    total = total.reshape(8, 4, 2, 32, width)
    kept = jnp.where(core == 0, total[:, :, 0], total[:, :, 1])
    sent = jnp.where(core == 0, total[:, :, 1], total[:, :, 0]).astype(BF16)
    total = kept + shifted(sent, "core", 1).astype(F32)
    parts = jnp.transpose(total.astype(BF16), (1, 0, 2, 3))
    parts = lax.all_to_all(parts, "y", 0, 0)
    total = jnp.sum(parts.astype(F32), axis=0)
    parts = lax.all_to_all(total.astype(BF16), "z_lo", 0, 0)
    gradient = jnp.sum(parts.astype(F32), axis=0)

    anchor_rows = lax.dynamic_slice_in_dim(slow_weight, lax.axis_index(REP) * 32, 32, 0)
    new_momentum = BETA * momentum + gradient
    new_weight = anchor_rows.astype(F32) - ALPHA * LR * new_momentum
    return (new_weight, new_momentum, final_of[0][None])


def solution(mesh):
    fine = Mesh(mesh.devices.reshape(SIZES), AXES)
    return jax.shard_map(
        body,
        mesh=fine,
        in_specs=(
            P(None, REP, TP),
            P(None, REP, TP),
            P(None, REP, TP),
            P(TP),
            P(None, TP),
            P(REP, TP),
            P(None, REP),
        ),
        out_specs=(P(REP, TP), P(REP, TP), P(REP)),
        check_vma=False,
    )
```

time: 1220 us -> 232 us (0.19)
  the two profiles are of different devices: /device:TPU:2 before, /device:TPU:32 now
where the time goes in v1:
time: 232 us; the launch traced here: 231 us
  starting transfers between devices  81.9 us (35%)
  waiting for transfers between devices  67.6 us (29%)
  between operations  30.1 us (13%)
  local copies, waits for them, and re-layouts  18.2 us (8%)
  blocking collectives  17 us (7%)
  matrix products  12.8 us (6%)
  other arithmetic  2.87 us (1%)
    ppermute x8, starting transfers between devices, shifted(): lax.ppermute(value, axis, [(i, (i + steps) % count) for i in range(count)])  44.5 us
    ppermute x8, waiting for transfers between devices, shifted(): lax.ppermute(value, axis, [(i, (i + steps) % count) for i in range(count)])  33.8 us
    all_to_all x5, starting transfers between devices, to_all(): lax.all_to_all(jnp.broadcast_to(value[None], (count,) + value.shape), axi...  29.5 us
    all_to_all x5, waiting for transfers between devices, to_all(): lax.all_to_all(jnp.broadcast_to(value[None], (count,) + value.shape), axi...  22.4 us
    all_to_all x1, blocking collectives, body(): parts = lax.all_to_all(parts, 'y', 0, 0)  17 us
    all_to_all x1, waiting for transfers between devices, body(): parts = lax.all_to_all(total.astype(BF16), 'z_lo', 0, 0)  11.4 us
    dot_general x2, matrix products, contract_rows(): lax.dot_general(left, right, (((0,), (0,)), ((), ())), preferred_element_...  8.06 us
    all_to_all x1, starting transfers between devices, body(): parts = lax.all_to_all(total.astype(BF16), 'z_lo', 0, 0)  7.87 us
  transfers between devices with their start and end apart: 15, of which 7 were waited for; matrix products, arithmetic and copies ran while one was open for 8% of the time, Pallas kernels for 0%

profile of v1, /device:TPU:32, one launch (start us, length us, event | category | flops | bytes accessed | tf_op | source)
XLA Modules:
  0.0 230.6 jit_solution(18200063010337466206)
XLA Ops:
  7.2 1.8 fusion.38
  9.1 1.1 broadcast_in_dim.12
  10.2 4.3 %all-to-all-start = ((bf16[4,512,256]{1,2,0:T(8,128)(2,1)}), bf16[4,512,256]{1,2,0:T(8,128)(2,1)S(1)}, u32[]{:S(2)}, u32[]{:S(2)}) async-start(bf16[4,512,256]{1,2,0:T(8,128)(2,1)} %broadcast_in_dim.12), calls=%async_computation | async-start | bytes 2097152 | tf_op jit(solution)/shard_map/all_to_all | solution.py:29
  14.5 14.9 %collective-permute-start.5 = (bf16[512,256]{1,0:T(8,128)(2,1)S(1)}, bf16[512,256]{1,0:T(8,128)(2,1)S(1)}, u32[]{:S(2)}, u32[]{:S(2)}) collective-permute-start(bf16[512,256]{1,0:T(8,128)(2,1)S(1)} %get-tuple-element.25), channel_id=1, source_target_pairs={{0,1},{1,0},{2,3},{3,2},{4,5},{5,4},{6,7},{7,6},{8,9},{9,8},{10,11... | collective-permute-start | bytes 786440 | tf_op jit(solution)/shard_map/ppermute | solution.py:24
  29.4 23.1 %collective-permute-done.5 = bf16[512,256]{1,0:T(8,128)(2,1)S(1)} collective-permute-done((bf16[512,256]{1,0:T(8,128)(2,1)S(1)}, bf16[512,256]{1,0:T(8,128)(2,1)S(1)}, u32[]{:S(2)}, u32[]{:S(2)}) %collective-permute-start.5) | collective-permute-done | bytes 262176 | tf_op jit(solution)/shard_map/ppermute | solution.py:24
  52.7 1.1 broadcast_in_dim.13
  53.7 4.5 %all-to-all-start.1 = ((bf16[4,512,256]{1,2,0:T(8,128)(2,1)}), bf16[4,512,256]{1,2,0:T(8,128)(2,1)S(1)}, u32[]{:S(2)}, u32[]{:S(2)}) async-start(bf16[4,512,256]{1,2,0:T(8,128)(2,1)} %broadcast_in_dim.13), calls=%async_computation.1 | async-start | bytes 2097152 | tf_op jit(solution)/shard_map/all_to_all | solution.py:29
  58.2 12.2 %collective-permute-start.4 = (bf16[512,256]{1,0:T(8,128)(2,1)S(1)}, bf16[512,256]{1,0:T(8,128)(2,1)S(1)}, u32[]{:S(2)}, u32[]{:S(2)}) collective-permute-start(bf16[512,256]{1,0:T(8,128)(2,1)S(1)} %get-tuple-element.24), channel_id=1, source_target_pairs={{0,1},{1,0},{2,3},{3,2},{4,5},{5,4},{6,7},{7,6},{8,9},{9,8},{10,11... | collective-permute-start | bytes 786440 | tf_op jit(solution)/shard_map/ppermute | solution.py:24
  70.5 1.8 all-to-all-done.1
  72.7 1.0 copy-done.2
  73.9 0.2 copy-done.6
  74.1 1.7 multiply_reduce_fusion.2
  75.8 0.6 broadcast_in_dim.14
  76.5 12.2 %all-to-all-start.2 = ((f32[8,3,512]{2,1,0:T(4,128)}), f32[8,3,512]{2,1,0:T(4,128)S(1)}, u32[]{:S(2)}, u32[]{:S(2)}) async-start(f32[8,3,512]{2,1,0:T(4,128)} %broadcast_in_dim.14), calls=%async_computation.2 | async-start | bytes 131072 | tf_op jit(solution)/shard_map/all_to_all | solution.py:29
  88.7 15.1 %all-to-all-done.2 = f32[8,3,512]{2,1,0:T(4,128)S(1)} async-done(((f32[8,3,512]{2,1,0:T(4,128)}), f32[8,3,512]{2,1,0:T(4,128)S(1)}, u32[]{:S(2)}, u32[]{:S(2)}) %all-to-all-start.2) | async-done | bytes 49184 | tf_op jit(solution)/shard_map/all_to_all | solution.py:29
  103.8 3.8 %multiply_convert_fusion = (bf16[2048,288]{0,1:T(8,128)(2,1)}, f32[2048,288]{0,1:T(8,128)}) fusion(f32[]{:T(128)S(6)} %sub.97, bf16[512,2048]{0,1:T(8,128)(2,1)S(1)} %bitcast.93, f32[512,288]{0,1:T(8,128)} %get-tuple-element.43, f32[512]{0:T(512)S(1)} %bitcast.109, f32[512]{0:T(512)S(1)} %bitcast.108, f32[288]{0:T(512)S(1)} %copy-done.4, ...), kind=kOutput, calls=%fused_computation.2 | convolution fusion | flops 606486528 | bytes 6527236 | tf_op jit(solution)/shard_map/dot_general | solution.py:33
  107.8 1.0 broadcast_in_dim.15
  108.8 3.5 %all-to-all-start.3 = ((bf16[4,512,256]{1,2,0:T(8,128)(2,1)}), bf16[4,512,256]{1,2,0:T(8,128)(2,1)S(1)}, u32[]{:S(2)}, u32[]{:S(2)}) async-start(bf16[4,512,256]{1,2,0:T(8,128)(2,1)} %broadcast_in_dim.15), calls=%async_computation.3 | async-start | bytes 2097152 | tf_op jit(solution)/shard_map/all_to_all | solution.py:29
  112.3 1.9 collective-permute-start.6
  114.3 3.6 %collective-permute-start = (f32[2]{0:T(128)S(1)}, f32[2]{0:T(128)S(1)}, u32[]{:S(2)}, u32[]{:S(2)}) collective-permute-start(f32[2]{0:T(128)S(1)} %bitcast.95), channel_id=1, source_target_pairs={{0,8},{8,16},{16,24},{24,32},{32,40},{40,48},{48,56},{56,64},{64,7... | collective-permute-start | bytes 32 | tf_op jit(solution)/shard_map/ppermute | solution.py:24
  117.8 4.1 %collective-permute-start.1 = (f32[2]{0:T(128)S(1)}, f32[2]{0:T(128)S(1)}, u32[]{:S(2)}, u32[]{:S(2)}) collective-permute-start(f32[2]{0:T(128)S(1)} %bitcast.96), channel_id=1, source_target_pairs={{0,504},{8,0},{16,8},{24,16},{32,24},{40,32},{48,40},{56,48},{64,5... | collective-permute-start | bytes 32 | tf_op jit(solution)/shard_map/ppermute | solution.py:24
  121.9 0.6 fusion.43
  123.8 8.4 %collective-permute-done = f32[2]{0:T(128)S(1)} collective-permute-done((f32[2]{0:T(128)S(1)}, f32[2]{0:T(128)S(1)}, u32[]{:S(2)}, u32[]{:S(2)}) %collective-permute-start) | collective-permute-done | bytes 40 | tf_op jit(solution)/shard_map/ppermute | solution.py:24
  132.3 1.9 collective-permute-start.3
  134.2 3.9 %collective-permute-start.2 = (f32[3,2]{1,0:T(4,128)S(1)}, f32[3,2]{1,0:T(4,128)S(1)}, u32[]{:S(2)}, u32[]{:S(2)}) collective-permute-start(f32[3,2]{1,0:T(4,128)S(1)} %pad_maximum_fusion.3), channel_id=1, source_target_pairs={{0,16},{8,24},{16,32},{24,40},{32,48},{40,56},{48,64},{56,72},{64,... | collective-permute-start | bytes 80 | tf_op jit(solution)/shard_map/ppermute | solution.py:24
  138.2 0.6 fusion.42
  141.3 0.6 fusion.41
  144.5 1.5 copy.48
  146.4 0.2 copy.50
  146.6 1.0 copy-done.3
  147.8 0.8 copy-done.8
  148.6 3.1 %multiply_reduce_fusion = (f32[512]{0:T(512)S(1)}, f32[512]{0:T(512)S(1)}, f32[512]{0:T(512)S(1)}, f32[512,288]{0,1:T(8,128)}) fusion(f32[288]{0:T(512)S(1)} %copy-done.4, bf16[2,512,288]{1,2,0:T(8,128)(2,1)S(1)} %copy-done.7, bf16[512,2048]{0,1:T(8,128)(2,1)S(1)} %bitcast.90, bf16[2048,288]{0,1:T(8,128)(2,1)} %collective-permute-done.6, ...), kind=kOutput, calls=%fused_computation.31 | convolution fusion | flops 609581568 | bytes 8002696 | tf_op jit(solution)/shard_map/dot_general | solution.py:44
  151.6 0.6 broadcast_in_dim.16
  152.3 4.9 %all-to-all-start.4 = ((f32[8,3,512]{2,1,0:T(4,128)}), f32[8,3,512]{2,1,0:T(4,128)S(1)}, u32[]{:S(2)}, u32[]{:S(2)}) async-start(f32[8,3,512]{2,1,0:T(4,128)} %broadcast_in_dim.16), calls=%async_computation.4 | async-start | bytes 131072 | tf_op jit(solution)/shard_map/all_to_all | solution.py:29
  157.2 0.6 fusion.39
  159.8 0.7 fusion.40
  166.7 5.5 %all-to-all-done.4 = f32[8,3,512]{2,1,0:T(4,128)S(1)} async-done(((f32[8,3,512]{2,1,0:T(4,128)}), f32[8,3,512]{2,1,0:T(4,128)S(1)}, u32[]{:S(2)}, u32[]{:S(2)}) %all-to-all-start.4) | async-done | bytes 49184 | tf_op jit(solution)/shard_map/all_to_all | solution.py:29
  172.3 4.3 %multiply_add_fusion = f32[2048,288]{0,1:T(8,128)} fusion(f32[2048,288]{0,1:T(8,128)} %get-tuple-element.9, bf16[512,2048]{0,1:T(8,128)(2,1)S(1)} %bitcast.91, f32[]{:T(128)S(6)} %div.110, f32[]{:T(128)S(6)} %div.99, f32[512,288]{0,1:T(8,128)} %get-tuple-element.46, f32[512]{0:T(512)S(1)} %bitcast.107, f32[512]{0:T(512)S(1)} %bitcast.106, ...), kind=kOutput, calls=%fused_computation.3 | convolution fusion | flops 607076352 | bytes 7706888 | tf_op jit(solution)/shard_map/dot_general | solution.py:33
  176.6 2.2 copy.52
  179.0 1.9 collective-permute-start.7
  180.9 2.3 collective-permute-done.7
  183.2 0.4 fusion.4
  183.7 17.0 %all_to_all.35 = bf16[4,8,32,288]{3,2,1,0:T(8,128)(2,1)S(1)} all-to-all(bf16[4,8,32,288]{3,2,1,0:T(8,128)(2,1)S(1)} %copy.53), channel_id=1, replica_groups=mesh['z_lo'=8,'y'=4,'core'=2,'x'=4,'z_hi'=2] {'y'}, dimensions={0} | all-to-all | bytes 1179648 | tf_op jit(solution)/shard_map/all_to_all | solution.py:122
  200.7 0.9 reduce_sum.101
  201.6 7.9 %all-to-all-start.6 = ((bf16[8,32,288]{2,1,0:T(8,128)(2,1)}), bf16[8,32,288]{2,1,0:T(8,128)(2,1)S(1)}, u32[]{:S(2)}, u32[]{:S(2)}) async-start(bf16[8,32,288]{2,1,0:T(8,128)(2,1)} %reduce_sum.101), calls=%async_computation.6 | async-start | bytes 393216 | tf_op jit(solution)/shard_map/all_to_all | solution.py:124
  209.5 1.0 constant_dynamic-slice_fusion
  210.5 11.4 %all-to-all-done.6 = bf16[8,32,288]{2,1,0:T(8,128)(2,1)S(1)} async-done(((bf16[8,32,288]{2,1,0:T(8,128)(2,1)}), bf16[8,32,288]{2,1,0:T(8,128)(2,1)S(1)}, u32[]{:S(2)}, u32[]{:S(2)}) %all-to-all-start.6) | async-done | bytes 147488 | tf_op jit(solution)/shard_map/all_to_all | solution.py:124
  222.0 0.7 multiply_subtract_fusion
  (43 shorter events, 2.0 us)
Async XLA Ops:
  10.2 42.3 %all-to-all-start = ((bf16[4,512,256]{1,2,0:T(8,128)(2,1)}), bf16[4,512,256]{1,2,0:T(8,128)(2,1)S(1)}, u32[]{:S(2)}, u32[]{:S(2)}) async-start(bf16[4,512,256]{1,2,0:T(8,128)(2,1)} %broadcast_in_dim.12), calls=%async_computation | async-start | bytes 2097152 | tf_op jit(solution)/shard_map/all_to_all | solution.py:29
  14.5 56.0 %copy-start.1 = (f32[2,1]{0,1:T(1,128)S(1)}, f32[2,1]{0,1:T(1,128)}, u32[]{:S(2)}) copy-start(f32[2,1]{0,1:T(1,128)} %param.13) | copy-start | bytes 28
  14.5 38.0 %collective-permute-start.5 = (bf16[512,256]{1,0:T(8,128)(2,1)S(1)}, bf16[512,256]{1,0:T(8,128)(2,1)S(1)}, u32[]{:S(2)}, u32[]{:S(2)}) collective-permute-start(bf16[512,256]{1,0:T(8,128)(2,1)S(1)} %get-tuple-element.25), channel_id=1, source_target_pairs={{0,1},{1,0},{2,3},{3,2},{4,5},{5,4},{6,7},{7,6},{8,9},{9,8},{10,11... | collective-permute-start | bytes 786440 | tf_op jit(solution)/shard_map/ppermute | solution.py:24
  53.7 18.6 %all-to-all-start.1 = ((bf16[4,512,256]{1,2,0:T(8,128)(2,1)}), bf16[4,512,256]{1,2,0:T(8,128)(2,1)S(1)}, u32[]{:S(2)}, u32[]{:S(2)}) async-start(bf16[4,512,256]{1,2,0:T(8,128)(2,1)} %broadcast_in_dim.13), calls=%async_computation.1 | async-start | bytes 2097152 | tf_op jit(solution)/shard_map/all_to_all | solution.py:29
  58.2 86.2 %all-gather.2.cloned.1.call-start = ((), (), s32[]{:S(2)}) async-start(), calls=%async_computation.7 | async-start | bytes 1310720 | tf_op jit(solution)/shard_map/all_gather | solution.py:78
  58.2 49.4 %collective-permute-start.4 = (bf16[512,256]{1,0:T(8,128)(2,1)S(1)}, bf16[512,256]{1,0:T(8,128)(2,1)S(1)}, u32[]{:S(2)}, u32[]{:S(2)}) collective-permute-start(bf16[512,256]{1,0:T(8,128)(2,1)S(1)} %get-tuple-element.24), channel_id=1, source_target_pairs={{0,1},{1,0},{2,3},{3,2},{4,5},{5,4},{6,7},{7,6},{8,9},{9,8},{10,11... | collective-permute-start | bytes 786440 | tf_op jit(solution)/shard_map/ppermute | solution.py:24
  72.5 1.3 copy-start.2
  72.5 1.3 copy-start.4
  72.5 1.4 copy-start.5
  72.5 1.6 copy-start.6
  76.5 27.3 %all-to-all-start.2 = ((f32[8,3,512]{2,1,0:T(4,128)}), f32[8,3,512]{2,1,0:T(4,128)S(1)}, u32[]{:S(2)}, u32[]{:S(2)}) async-start(f32[8,3,512]{2,1,0:T(4,128)} %broadcast_in_dim.14), calls=%async_computation.2 | async-start | bytes 131072 | tf_op jit(solution)/shard_map/all_to_all | solution.py:29
  108.8 37.2 %all-to-all-start.3 = ((bf16[4,512,256]{1,2,0:T(8,128)(2,1)}), bf16[4,512,256]{1,2,0:T(8,128)(2,1)S(1)}, u32[]{:S(2)}, u32[]{:S(2)}) async-start(bf16[4,512,256]{1,2,0:T(8,128)(2,1)} %broadcast_in_dim.15), calls=%async_computation.3 | async-start | bytes 2097152 | tf_op jit(solution)/shard_map/all_to_all | solution.py:29
  112.3 34.3 %collective-permute-start.6 = (bf16[2048,288]{0,1:T(8,128)(2,1)}, bf16[2048,288]{0,1:T(8,128)(2,1)}, u32[]{:S(2)}, u32[]{:S(2)}) collective-permute-start(bf16[2048,288]{0,1:T(8,128)(2,1)} %get-tuple-element.44), channel_id=1, source_target_pairs={{0,8},{8,16},{16,24},{24,32},{32,40},{40,48},{48,56},{56,64},{64,7... | collective-permute-start | bytes 3538952 | tf_op jit(solution)/shard_map/ppermute | solution.py:24
  114.3 18.0 %collective-permute-start = (f32[2]{0:T(128)S(1)}, f32[2]{0:T(128)S(1)}, u32[]{:S(2)}, u32[]{:S(2)}) collective-permute-start(f32[2]{0:T(128)S(1)} %bitcast.95), channel_id=1, source_target_pairs={{0,8},{8,16},{16,24},{24,32},{32,40},{40,48},{48,56},{56,64},{64,7... | collective-permute-start | bytes 32 | tf_op jit(solution)/shard_map/ppermute | solution.py:24
  117.8 14.4 %collective-permute-start.1 = (f32[2]{0:T(128)S(1)}, f32[2]{0:T(128)S(1)}, u32[]{:S(2)}, u32[]{:S(2)}) collective-permute-start(f32[2]{0:T(128)S(1)} %bitcast.96), channel_id=1, source_target_pairs={{0,504},{8,0},{16,8},{24,16},{32,24},{40,32},{48,40},{56,48},{64,5... | collective-permute-start | bytes 32 | tf_op jit(solution)/shard_map/ppermute | solution.py:24
  132.3 24.9 %collective-permute-start.3 = (f32[3,2]{1,0:T(4,128)S(1)}, f32[3,2]{1,0:T(4,128)S(1)}, u32[]{:S(2)}, u32[]{:S(2)}) collective-permute-start(f32[3,2]{1,0:T(4,128)S(1)} %pad_maximum_fusion.3), channel_id=1, source_target_pairs={{0,496},{8,504},{16,0},{24,8},{32,16},{40,24},{48,32},{56,40},{64,... | collective-permute-start | bytes 80 | tf_op jit(solution)/shard_map/ppermute | solution.py:24
  134.2 25.5 %collective-permute-start.2 = (f32[3,2]{1,0:T(4,128)S(1)}, f32[3,2]{1,0:T(4,128)S(1)}, u32[]{:S(2)}, u32[]{:S(2)}) collective-permute-start(f32[3,2]{1,0:T(4,128)S(1)} %pad_maximum_fusion.3), channel_id=1, source_target_pairs={{0,16},{8,24},{16,32},{24,40},{32,48},{40,56},{48,64},{56,72},{64,... | collective-permute-start | bytes 80 | tf_op jit(solution)/shard_map/ppermute | solution.py:24
  146.3 1.3 copy-start.3
  146.4 1.4 copy-start.7
  146.4 2.2 copy-start.8
  152.3 20.0 %all-to-all-start.4 = ((f32[8,3,512]{2,1,0:T(4,128)}), f32[8,3,512]{2,1,0:T(4,128)S(1)}, u32[]{:S(2)}, u32[]{:S(2)}) async-start(f32[8,3,512]{2,1,0:T(4,128)} %broadcast_in_dim.16), calls=%async_computation.4 | async-start | bytes 131072 | tf_op jit(solution)/shard_map/all_to_all | solution.py:29
  179.0 4.2 %collective-permute-start.7 = (bf16[8,4,32,288]{3,2,1,0:T(8,128)(2,1)S(1)}, bf16[8,4,32,288]{3,2,1,0:T(8,128)(2,1)S(1)}, u32[]{:S(2)}, u32[]{:S(2)}) collective-permute-start(bf16[8,4,32,288]{3,2,1,0:T(8,128)(2,1)S(1)} %fusion.3), channel_id=1, source_target_pairs={{0,8},{8,0},{1,9},{9,1},{2,10},{10,2},{3,11},{11,3},{4,12},{12,4},... | collective-permute-start | bytes 1769480 | tf_op jit(solution)/shard_map/ppermute | solution.py:24
  183.7 38.3 %copy-start = (f32[32,288]{1,0:T(8,128)S(1)}, f32[32,288]{1,0:T(8,128)}, u32[]{:S(2)}) copy-start(f32[32,288]{1,0:T(8,128)} %param.12) | copy-start | bytes 110596
  201.6 20.3 %all-to-all-start.6 = ((bf16[8,32,288]{2,1,0:T(8,128)(2,1)}), bf16[8,32,288]{2,1,0:T(8,128)(2,1)S(1)}, u32[]{:S(2)}, u32[]{:S(2)}) async-start(bf16[8,32,288]{2,1,0:T(8,128)(2,1)} %reduce_sum.101), calls=%async_computation.6 | async-start | bytes 393216 | tf_op jit(solution)/shard_map/all_to_all | solution.py:124
Sparse Core Ops, SparseCore 0:
  70.6 26.6 all-gather.1

commit v2 on v1

v2 whole, which is shorter than its diff:
```python
import jax
import jax.numpy as jnp
from jax import lax
from jax.experimental import pallas as pl
from jax.experimental.pallas import tpu as pltpu
from jax.sharding import Mesh, PartitionSpec as P

D = 2304
TOK = 512
LR = 0.005
BETA = 0.7
ALPHA = 1.0
EPS = 1e-06
SCALE = TOK ** (-0.5)

AXES = ("z_lo", "y", "core", "x", "z_hi")
SIZES = (8, 4, 2, 4, 2)
REP = AXES[:3]
TP = AXES[3:]
F32 = jnp.float32
BF16 = jnp.bfloat16
CHUNK = 256
SMEM = pl.BlockSpec(memory_space=pltpu.SMEM)


def shifted(value, axis, steps):
    count = lax.axis_size(axis)
    return lax.ppermute(value, axis, [(i, (i + steps) % count) for i in range(count)])


def to_all(value, axis):
    count = lax.axis_size(axis)
    return lax.all_to_all(jnp.broadcast_to(value[None], (count,) + value.shape), axis, 0, 0)


def after(value, *others):
    return lax.optimization_barrier((value,) + others)[0]


def call(kernel, specs, out_specs, outs, flops, *args, scratch=(), steps=4):
    size = sum(a.size * a.dtype.itemsize for a in args) + sum(
        o.size * o.dtype.itemsize for o in outs
    )
    return pl.pallas_call(
        kernel,
        grid=(steps,),
        out_shape=outs,
        in_specs=specs,
        out_specs=out_specs,
        scratch_shapes=scratch,
        compiler_params=pltpu.CompilerParams(vmem_limit_bytes=24 * 2**20),
        cost_estimate=pl.CostEstimate(flops=flops, bytes_accessed=size, transcendentals=0),
    )(*args)


def whole(dims):
    return pl.BlockSpec(dims, lambda x: (0,) * len(dims))


def layer(step, dims):
    return pl.BlockSpec((1,) + dims, lambda x: (step, 0, 0))


FEATURES = pl.BlockSpec((1, 2, TOK, CHUNK), lambda x: (x, 0, 0, 0))


def dot(left, right, left_dim, right_dim):
    return lax.dot_general(
        left, right, (((left_dim,), (right_dim,)), ((), ())), preferred_element_type=F32
    )


def columns(hi, other):
    half = 1 - hi if other else hi
    return half, pl.ds(pl.multiple_of(half * CHUNK, CHUNK), CHUNK)


def token_sums(output, gain, targets, sums_ref):
    scaled = gain * output
    rows = [
        jnp.sum(output * output, axis=0, keepdims=True),
        jnp.sum(scaled * scaled, axis=0, keepdims=True),
        jnp.sum(scaled * targets, axis=0, keepdims=True),
        jnp.zeros((5, TOK), F32),
    ]
    block = jnp.concatenate(rows, axis=0)
    for peer in range(sums_ref.shape[0]):
        sums_ref[peer] = block


def first_forward(place_ref, both_ref, weight_ref, res_ref, tgt_ref, gain_ref, out_ref, sums_ref):
    x = pl.program_id(0)

    @pl.when(x == 0)
    def _():
        out_ref[...] = res_ref[0].astype(F32)

    acc = out_ref[...]
    for other in range(2):
        _, cols = columns(place_ref[0], other)
        acc += dot(weight_ref[:, cols], both_ref[0, other], 1, 1)
    out_ref[...] = acc

    @pl.when(x == 3)
    def _():
        token_sums(out_ref[...], gain_ref[...], tgt_ref[0].astype(F32), sums_ref)


def output_gradient(recv_ref, out_ref, tgt_ref, gain_ref):
    totals = recv_ref[0]
    for peer in range(1, recv_ref.shape[0]):
        totals += recv_ref[peer]
    root_sq = totals[0:1] / D + EPS
    root = jnp.sqrt(root_sq)
    projection = SCALE * (totals[1:2] / root_sq - totals[2:3] / root) / D
    gain = gain_ref[...]
    normed = out_ref[...] / root
    normed_grad = SCALE * gain * (gain * normed - tgt_ref[0].astype(F32))
    return (normed_grad - normed * projection) / root


def first_backward(recv_ref, out_ref, tgt_ref, gain_ref, share_ref, kept_ref, sent_ref):
    grad = output_gradient(recv_ref, out_ref, tgt_ref, gain_ref)
    share = share_ref[...]
    kept_ref[...] = (share * grad).astype(BF16)
    sent_ref[...] = ((1.0 - share) * grad).astype(BF16)


def second_forward(
    place_ref, both_ref, prev_ref, next_ref, kept_ref, recv_ref, weight_ref, res_ref, tgt_ref,
    gain_ref, mass_ref, out_ref, sums_ref,
):
    x = pl.program_id(0)

    @pl.when(x == 0)
    def _():
        out_ref[...] = res_ref[0].astype(F32)

    factor = LR / mass_ref[:, :CHUNK]
    acc = out_ref[...]
    for other in range(2):
        _, cols = columns(place_ref[0], other)
        move = dot(kept_ref[...], both_ref[0, other], 1, 0)
        move += dot(recv_ref[...], prev_ref[0, other], 1, 0)
        quotient = (weight_ref[:, cols].astype(F32) - factor * move).astype(BF16)
        acc += dot(quotient, next_ref[0, other], 1, 1)
    out_ref[...] = acc

    @pl.when(x == 3)
    def _():
        token_sums(out_ref[...], gain_ref[...], tgt_ref[0].astype(F32), sums_ref)


def first_rows(place_ref, both_ref, prev_ref, kept_ref, recv_ref, rows_ref):
    for other in range(2):
        half, _ = columns(place_ref[0], other)
        rows_ref[half] = dot(both_ref[0, other], kept_ref[...], 0, 1) + dot(
            prev_ref[0, other], recv_ref[...], 0, 1
        )


def second_backward(
    place_ref, recv_ref, out_ref, tgt_ref, gain_ref, coef_ref, next_ref, rows_ref,
    kept_ref, sent_ref, grad_ref, total_ref,
):
    hi, core = place_ref[0], place_ref[1]

    @pl.when(pl.program_id(0) == 0)
    def _():
        grad_ref[...] = output_gradient(recv_ref, out_ref, tgt_ref, gain_ref).astype(BF16)

    coef = coef_ref[:, :288]
    for other in range(2):
        half, _ = columns(hi, other)
        total_ref[...] = coef * (rows_ref[half] + dot(next_ref[0, other], grad_ref[...], 0, 1))
        for y in range(4):
            mine = pl.ds(pl.multiple_of((2 * y + core) * 32, 32), 32)
            away = pl.ds(pl.multiple_of((2 * y + 1 - core) * 32, 32), 32)
            kept_ref[y, half] = total_ref[mine, :]
            sent_ref[y, half] = total_ref[away, :].astype(BF16)


def shape(dims, dtype):
    return jax.ShapeDtypeStruct(dims, dtype)


def body(context, residual, targets, gain, slow_weight, momentum, shares):
    hi = lax.axis_index("z_hi").astype(jnp.int32)
    core = lax.axis_index("core").astype(jnp.int32)
    place = jnp.stack([hi, core])
    weight = slow_weight.T
    res = jnp.transpose(residual, (0, 2, 1))
    tgt = jnp.transpose(targets, (0, 2, 1))
    gain = gain[:, None]
    width = weight.shape[0]
    share0 = jnp.broadcast_to(shares[0:1], (1, TOK))
    share1 = jnp.broadcast_to(shares[1:2], (1, TOK))

    out, sums, pair = whole((width, TOK)), whole((8, 8, TOK)), whole((width, TOK))
    col, row = whole((width, 1)), whole((1, TOK))
    wts = pl.BlockSpec((width, 2 * CHUNK), lambda x: (0, x))
    rows_spec = pl.BlockSpec((2, CHUNK, width), lambda x: (x, 0, 0))
    cut = pl.BlockSpec((4, 2, 32, width), lambda x: (0, x, 0, 0))
    flops = 2 * TOK * 2048 * width

    other0 = shifted(context[0], "z_hi", 1)
    context1, share0 = lax.optimization_barrier((context[1], share0, other0))[:2]
    other1 = shifted(context1, "z_hi", 1)
    both0 = to_all(jnp.stack([context[0], other0]), "x")
    mass1 = share0 + (1.0 - shifted(share0, REP, 1))

    output0, sums0 = call(
        first_forward, [SMEM, FEATURES, wts, layer(0, (width, TOK)), layer(0, (width, TOK)), col],
        [out, sums], [shape((width, TOK), F32), shape((8, 8, TOK), F32)], flops,
        place, both0, weight, res, tgt, gain,
    )
    totals0 = lax.all_to_all(sums0, TP, 0, 0)
    both0, other1, share1 = lax.optimization_barrier((both0, other1, share1, sums0))[:3]
    both1 = to_all(jnp.stack([context1, other1]), "x")
    prev = shifted(both0, REP, 1)
    mass_in = shifted((1.0 - share1) * mass1, REP, 2)
    kept0, sent0 = call(
        first_backward, [sums, out, layer(0, (width, TOK)), col, row], [pair] * 2,
        [shape((width, TOK), BF16)] * 2, 20 * width * TOK,
        totals0, output0, tgt, gain, share0, steps=1,
    )
    recv0 = shifted(sent0, REP, 1)
    mass2 = share1 * mass1 + mass_in
    mass_later = shifted(after(mass2, sent0), REP, -2)

    output1, sums1 = call(
        second_forward,
        [SMEM, FEATURES, FEATURES, FEATURES, pair, pair, wts]
        + [layer(1, (width, TOK)), layer(1, (width, TOK)), col, row],
        [out, sums], [shape((width, TOK), F32), shape((8, 8, TOK), F32)], 3 * flops,
        place, both0, prev, both1, kept0, recv0, weight, res, tgt, gain, mass1,
    )
    totals1 = lax.all_to_all(sums1, TP, 0, 0)
    late = lax.optimization_barrier((both0, prev, kept0, recv0, sums1))[:4]
    (rows,) = call(
        first_rows, [SMEM, FEATURES, FEATURES, pair, pair], [rows_spec],
        [shape((8, CHUNK, width), F32)], 2 * flops, place, *late,
    )
    coef = (share1 / mass2 + (1.0 - share1) / mass_later) / lax.axis_size(REP)
    kept, sent = call(
        second_backward, [SMEM, sums, out, layer(1, (width, TOK)), col, row, FEATURES, rows_spec],
        [cut] * 2, [shape((4, 8, 32, width), F32), shape((4, 8, 32, width), BF16)], flops,
        place, totals1, output1, tgt, gain, coef, both1, rows,
        scratch=[pltpu.VMEM((width, TOK), BF16), pltpu.VMEM((CHUNK, width), F32)],
    )

    total = (kept + shifted(sent, "core", 1).astype(F32)).astype(BF16)
    parts = lax.all_to_all(total, "y", 0, 0)
    total = jnp.sum(parts.astype(F32), axis=0).astype(BF16)
    parts = lax.all_to_all(total, "z_lo", 0, 0)
    gradient = jnp.sum(parts.astype(F32), axis=0)

    anchor_rows = lax.dynamic_slice_in_dim(slow_weight, lax.axis_index(REP) * 32, 32, 0)
    new_momentum = BETA * momentum + gradient
    new_weight = anchor_rows.astype(F32) - ALPHA * LR * new_momentum
    return (new_weight, new_momentum, mass2[0, :1])


def solution(mesh):
    fine = Mesh(mesh.devices.reshape(SIZES), AXES)
    return jax.shard_map(
        body,
        mesh=fine,
        in_specs=(
            P(None, REP, TP),
            P(None, REP, TP),
            P(None, REP, TP),
            P(TP),
            P(None, TP),
            P(REP, TP),
            P(None, REP),
        ),
        out_specs=(P(REP, TP), P(REP, TP), P(REP)),
        check_vma=False,
    )
```

time: 232 us -> 239 us (1.030)
  the two profiles are of different devices: /device:TPU:32 before, /device:TPU:2 now
where the time goes in v2:
time: 239 us; the launch traced here: 238 us
  starting transfers between devices  97.2 us (41%)
  waiting for transfers between devices  70.5 us (29%)
  local copies, waits for them, and re-layouts  29.2 us (12%)
  blocking collectives  16.4 us (7%)
  Pallas kernels  16.2 us (7%)
  other arithmetic  7.05 us (3%)
    ppermute x8, starting transfers between devices, shifted(): lax.ppermute(value, axis, [(i, (i + steps) % count) for i in range(count)])  51.9 us
    ppermute x8, waiting for transfers between devices, shifted(): lax.ppermute(value, axis, [(i, (i + steps) % count) for i in range(count)])  38.5 us
    unnamed x59, local copies, waits for them, and re-layouts  18.2 us
    all_to_all x1, blocking collectives, body(): parts = lax.all_to_all(total, 'y', 0, 0)  16.4 us
    pallas_call x5, Pallas kernels, call(): pl.pallas_call(kernel, grid=(steps,), out_shape=outs, in_specs=specs, out...  16.2 us
    all_to_all x1, starting transfers between devices, body(): parts = lax.all_to_all(total, 'z_lo', 0, 0)  15.7 us
    all_to_all x1, starting transfers between devices, body(): totals0 = lax.all_to_all(sums0, TP, 0, 0)  13.6 us
    all_to_all x1, waiting for transfers between devices, body(): totals0 = lax.all_to_all(sums0, TP, 0, 0)  11.9 us
  transfers between devices with their start and end apart: 13, of which 7 were waited for; matrix products, arithmetic and copies ran while one was open for 5% of the time, Pallas kernels for 5%

profile of v2, /device:TPU:2, one launch (start us, length us, event | category | flops | bytes accessed | tf_op | source)
XLA Modules:
  0.0 237.6 jit_solution(15790389919698280222)
XLA Ops:
  0.6 1.8 slice_bitcast_fusion
  2.4 15.7 %collective-permute-start = (bf16[512,256]{1,0:T(8,128)(2,1)S(1)}, bf16[512,256]{1,0:T(8,128)(2,1)S(1)}, u32[]{:S(2)}, u32[]{:S(2)}) collective-permute-start(bf16[512,256]{1,0:T(8,128)(2,1)S(1)} %get-tuple-element.44), channel_id=1, source_target_pairs={{0,1},{1,0},{2,3},{3,2},{4,5},{5,4},{6,7},{7,6},{8,9},{9,8},{10,11... | collective-permute-start | bytes 786440 | tf_op jit(solution)/shard_map/ppermute | solution.py:28
  18.1 6.6 %collective-permute-done = bf16[512,256]{1,0:T(8,128)(2,1)S(1)} collective-permute-done((bf16[512,256]{1,0:T(8,128)(2,1)S(1)}, bf16[512,256]{1,0:T(8,128)(2,1)S(1)}, u32[]{:S(2)}, u32[]{:S(2)}) %collective-permute-start) | collective-permute-done | bytes 262176 | tf_op jit(solution)/shard_map/ppermute | solution.py:28
  24.8 1.5 broadcast_in_dim.14
  26.2 5.0 %all-to-all-start = ((bf16[4,2,512,256]{3,2,1,0:T(8,128)(2,1)}), bf16[4,2,512,256]{3,2,1,0:T(8,128)(2,1)S(1)}, u32[]{:S(2)}, u32[]{:S(2)}) async-start(bf16[4,2,512,256]{3,2,1,0:T(8,128)(2,1)} %broadcast_in_dim.14), calls=%async_computation | async-start | bytes 4194304 | tf_op jit(solution)/shard_map/all_to_all | solution.py:33
  31.9 1.2 broadcast_in_dim.31.share_ref
  33.1 12.3 %collective-permute-start.1 = (bf16[512,256]{1,0:T(8,128)(2,1)}, bf16[512,256]{1,0:T(8,128)(2,1)}, u32[]{:S(2)}, u32[]{:S(2)}) collective-permute-start(bf16[512,256]{1,0:T(8,128)(2,1)} %get-tuple-element.21), channel_id=1, source_target_pairs={{0,1},{1,0},{2,3},{3,2},{4,5},{5,4},{6,7},{7,6},{8,9},{9,8},{10,11... | collective-permute-start | bytes 786440 | tf_op jit(solution)/shard_map/ppermute | solution.py:28
  45.6 9.6 %all-to-all-done.both_ref = bf16[4,2,512,256]{3,2,1,0:T(8,128)(2,1)S(1)} async-done(((bf16[4,2,512,256]{3,2,1,0:T(8,128)(2,1)}), bf16[4,2,512,256]{3,2,1,0:T(8,128)(2,1)S(1)}, u32[]{:S(2)}, u32[]{:S(2)}) %all-to-all-start) | async-done | bytes 2097184 | tf_op jit(solution)/shard_map/all_to_all | solution.py:33
  55.2 1.3 copy-done.3
  56.5 2.3 shard_map.94
  58.9 0.8 copy-done.14
  59.7 1.2 broadcast_in_dim.33
  60.9 1.9 collective-permute-start.2
  62.8 13.6 %all-to-all-start.2 = ((f32[8,8,512]{2,1,0:T(8,128)}), f32[8,8,512]{2,1,0:T(8,128)S(1)}, u32[]{:S(2)}, u32[]{:S(2)}) async-start(f32[8,8,512]{2,1,0:T(8,128)} %copy-done.17), calls=%async_computation.2 | async-start | bytes 262144 | tf_op jit(solution)/shard_map/all_to_all | solution.py:217
  76.4 1.9 pad_maximum_fusion.1
  78.3 11.9 %all-to-all-done.2.recv_ref = f32[8,8,512]{2,1,0:T(8,128)S(1)} async-done(((f32[8,8,512]{2,1,0:T(8,128)}), f32[8,8,512]{2,1,0:T(8,128)S(1)}, u32[]{:S(2)}, u32[]{:S(2)}) %all-to-all-start.2) | async-done | bytes 131104 | tf_op jit(solution)/shard_map/all_to_all | solution.py:217
  90.2 2.5 %broadcast_in_dim.35 = bf16[4,2,512,256]{3,2,1,0:T(8,128)(2,1)} broadcast(bf16[2,512,256]{2,1,0:T(8,128)(2,1)} %pad_maximum_fusion.1), dimensions={1,2,3} | broadcast | bytes 2621440 | tf_op jit(solution)/shard_map/broadcast_in_dim | solution.py:33
  92.7 6.3 %all-to-all-start.1 = ((bf16[4,2,512,256]{3,2,1,0:T(8,128)(2,1)}), bf16[4,2,512,256]{3,2,1,0:T(8,128)(2,1)}, u32[]{:S(2)}, u32[]{:S(2)}) async-start(bf16[4,2,512,256]{3,2,1,0:T(8,128)(2,1)} %broadcast_in_dim.35), calls=%async_computation.1 | async-start | bytes 4194304 | tf_op jit(solution)/shard_map/all_to_all | solution.py:33
  98.9 1.1 copy-done.15
  101.0 0.7 copy-done.6
  101.7 1.9 collective-permute-start.3
  103.6 3.6 %collective-permute-start.4 = (f32[1,512]{1,0:T(1,128)S(1)}, f32[1,512]{1,0:T(1,128)S(1)}, u32[]{:S(2)}, u32[]{:S(2)}) collective-permute-start(f32[1,512]{1,0:T(1,128)S(1)} %copy-done.18), channel_id=1, source_target_pairs={{0,8},{8,16},{16,24},{24,32},{32,40},{40,48},{48,56},{56,64},{64,7... | collective-permute-start | bytes 6152 | tf_op jit(solution)/shard_map/ppermute | solution.py:28
  107.2 28.4 %collective-permute-done.4 = f32[1,512]{1,0:T(1,128)S(1)} collective-permute-done((f32[1,512]{1,0:T(1,128)S(1)}, f32[1,512]{1,0:T(1,128)S(1)}, u32[]{:S(2)}, u32[]{:S(2)}) %collective-permute-start.4) | collective-permute-done | bytes 2080 | tf_op jit(solution)/shard_map/ppermute | solution.py:28
  135.6 1.3 subtract_multiply_fusion
  136.9 1.9 collective-permute-start.5
  139.5 1.3 copy-done.4
  140.8 1.0 copy-done.7
  141.8 1.0 copy-done.10
  143.4 4.9 %shard_map.96 = (f32[288,512]{1,0:T(8,128)S(1)}, f32[8,8,512]{2,1,0:T(8,128)S(1)}) custom-call(s32[2]{0:T(128)S(1)} %copy-done.22, bf16[4,2,512,256]{3,2,1,0:T(8,128)(2,1)S(1)} %all-to-all-done.both_ref, bf16[4,2,512,256]{3,2,1,0:T(8,128)(2,1)} %collective-permute-done.2.prev_ref, bf16[4,2,512,256]{3,2,1,0:T(8,128)(2,1)} %all-to-all-done.1.next_ref, ...), custom_call_target="tpu_custom_call" | custom-call | flops 1811939328 | bytes 9964680 | tf_op jit(solution)/shard_map/pallas_call | solution.py:44
  148.3 0.8 copy-done.12
  149.8 4.8 %all-to-all-start.3 = ((f32[8,8,512]{2,1,0:T(8,128)}), f32[8,8,512]{2,1,0:T(8,128)S(1)}, u32[]{:S(2)}, u32[]{:S(2)}) async-start(f32[8,8,512]{2,1,0:T(8,128)} %copy-done.16), calls=%async_computation.3 | async-start | bytes 262144 | tf_op jit(solution)/shard_map/all_to_all | solution.py:238
  155.3 12.6 %collective-permute-start.6 = (f32[1,512]{1,0:T(1,128)S(1)}, f32[1,512]{1,0:T(1,128)S(1)}, u32[]{:S(2)}, u32[]{:S(2)}) collective-permute-start(f32[1,512]{1,0:T(1,128)S(1)} %multiply_add_fusion.1), channel_id=1, source_target_pairs={{0,496},{8,504},{16,0},{24,8},{32,16},{40,24},{48,32},{56,40},{64,... | collective-permute-start | bytes 6152 | tf_op jit(solution)/shard_map/ppermute | solution.py:28
  167.9 1.3 collective-permute-done.6
  169.2 1.3 add_multiply_fusion.coef_ref
  170.5 1.0 copy-done.8
  171.5 1.0 copy-done.11
  173.1 4.5 %shard_map.97.rows_ref = f32[8,256,288]{2,1,0:T(8,128)S(1)} custom-call(s32[2]{0:T(128)S(1)} %copy-done.23, bf16[4,2,512,256]{3,2,1,0:T(8,128)(2,1)S(1)} %all-to-all-done.both_ref, bf16[4,2,512,256]{3,2,1,0:T(8,128)(2,1)} %collective-permute-done.2.prev_ref, bf16[288,512]{1,0:T(8,128)(2,1)S(1)} %copy-done.8, bf16[288,512]{1,0:T(8,128)(2,1)S(1)} %copy-done.11), custom_call_target="tpu_custom_call" | custom-call | flops 1207959552 | bytes 7143432 | tf_op jit(solution)/shard_map/pallas_call | solution.py:44
  177.6 1.6 copy-done
  179.2 1.9 copy-done.1
  182.5 4.2 %shard_map.98 = (f32[4,8,32,288]{3,2,1,0:T(8,128)S(1)}, bf16[4,8,32,288]{3,2,1,0:T(8,128)(2,1)S(1)}) custom-call(s32[2]{0:T(128)S(1)} %copy-done.24, f32[8,8,512]{2,1,0:T(8,128)S(1)} %all-to-all-done.3.recv_ref, f32[288,512]{1,0:T(8,128)S(1)} %copy-done.13, bf16[2,288,512]{2,1,0:T(8,128)(2,1)S(1)} %bitcast.18, f32[288,1]{1,0:T(8,128)S(1)} %broadcast_in_dim.36.gain_ref, ...), custom_call_target="tpu_custom_call" | custom-call | flops 603979776 | bytes 7539848 | tf_op jit(solution)/shard_map/pallas_call | solution.py:44
  186.6 1.9 collective-permute-start.7
  188.6 2.3 collective-permute-done.7
  191.1 16.4 %all_to_all.30 = bf16[4,8,32,288]{3,2,1,0:T(8,128)(2,1)S(1)} all-to-all(bf16[4,8,32,288]{3,2,1,0:T(8,128)(2,1)S(1)} %add_convert_fusion), channel_id=1, replica_groups=mesh['z_lo'=8,'y'=4,'core'=2,'x'=4,'z_hi'=2] {'y'}, dimensions={0} | all-to-all | bytes 1179648 | tf_op jit(solution)/shard_map/all_to_all | solution.py:253
  207.5 0.9 reduce_sum.21
  208.4 15.7 %all-to-all-start.5 = ((bf16[8,32,288]{2,1,0:T(8,128)(2,1)}), bf16[8,32,288]{2,1,0:T(8,128)(2,1)S(1)}, u32[]{:S(2)}, u32[]{:S(2)}) async-start(bf16[8,32,288]{2,1,0:T(8,128)(2,1)} %reduce_sum.21), calls=%async_computation.5 | async-start | bytes 393216 | tf_op jit(solution)/shard_map/all_to_all | solution.py:255
  224.1 1.0 constant_dynamic-slice_fusion
  225.2 1.2 slice.21
  226.4 10.5 %all-to-all-done.5 = bf16[8,32,288]{2,1,0:T(8,128)(2,1)S(1)} async-done(((bf16[8,32,288]{2,1,0:T(8,128)(2,1)}), bf16[8,32,288]{2,1,0:T(8,128)(2,1)S(1)}, u32[]{:S(2)}, u32[]{:S(2)}) %all-to-all-start.5) | async-done | bytes 147488 | tf_op jit(solution)/shard_map/all_to_all | solution.py:255
  (62 shorter events, 7.7 us)
Async XLA Ops:
  2.4 22.3 %collective-permute-start = (bf16[512,256]{1,0:T(8,128)(2,1)S(1)}, bf16[512,256]{1,0:T(8,128)(2,1)S(1)}, u32[]{:S(2)}, u32[]{:S(2)}) collective-permute-start(bf16[512,256]{1,0:T(8,128)(2,1)S(1)} %get-tuple-element.44), channel_id=1, source_target_pairs={{0,1},{1,0},{2,3},{3,2},{4,5},{5,4},{6,7},{7,6},{8,9},{9,8},{10,11... | collective-permute-start | bytes 786440 | tf_op jit(solution)/shard_map/ppermute | solution.py:28
  26.2 5.0 %copy-start.28 = (f32[2,1]{0,1:T(1,128)S(1)}, f32[2,1]{0,1:T(1,128)}, u32[]{:S(2)}) copy-start(f32[2,1]{0,1:T(1,128)} %param.13) | copy-start | bytes 28
  26.2 19.2 %copy-start.27 = (f32[288]{0:T(512)S(1)}, f32[288]{0:T(512)}, u32[]{:S(2)}) copy-start(f32[288]{0:T(512)} %param.10) | copy-start | bytes 3460
  26.2 29.0 %copy-start.2 = (bf16[2,512,288]{1,2,0:T(8,128)(2,1)S(1)}, bf16[2,512,288]{1,2,0:T(8,128)(2,1)}, u32[]{:S(2)}) copy-start(bf16[2,512,288]{1,2,0:T(8,128)(2,1)} %param.9) | copy-start | bytes 1769476
  26.2 29.0 %copy-start.5 = (bf16[2,512,288]{1,2,0:T(8,128)(2,1)S(1)}, bf16[2,512,288]{1,2,0:T(8,128)(2,1)}, u32[]{:S(2)}) copy-start(bf16[2,512,288]{1,2,0:T(8,128)(2,1)} %param.8) | copy-start | bytes 1769476
  26.2 29.0 %all-to-all-start = ((bf16[4,2,512,256]{3,2,1,0:T(8,128)(2,1)}), bf16[4,2,512,256]{3,2,1,0:T(8,128)(2,1)S(1)}, u32[]{:S(2)}, u32[]{:S(2)}) async-start(bf16[4,2,512,256]{3,2,1,0:T(8,128)(2,1)} %broadcast_in_dim.14), calls=%async_computation | async-start | bytes 4194304 | tf_op jit(solution)/shard_map/all_to_all | solution.py:33
  33.1 26.6 %collective-permute-start.1 = (bf16[512,256]{1,0:T(8,128)(2,1)}, bf16[512,256]{1,0:T(8,128)(2,1)}, u32[]{:S(2)}, u32[]{:S(2)}) collective-permute-start(bf16[512,256]{1,0:T(8,128)(2,1)} %get-tuple-element.21), channel_id=1, source_target_pairs={{0,1},{1,0},{2,3},{3,2},{4,5},{5,4},{6,7},{7,6},{8,9},{9,8},{10,11... | collective-permute-start | bytes 786440 | tf_op jit(solution)/shard_map/ppermute | solution.py:28
  45.6 13.2 %copy-start.21 = (s32[2]{0:T(128)}, s32[2]{0:T(128)S(1)}, u32[]{:S(2)}) copy-start(s32[2]{0:T(128)S(1)} %pad_add_fusion.place_ref) | copy-start | bytes 28
  55.2 1.3 copy-start.3
  58.9 0.8 copy-start.14
  59.7 1.2 copy-start.17
  60.9 78.6 %collective-permute-start.2 = (bf16[4,2,512,256]{3,2,1,0:T(8,128)(2,1)S(1)}, bf16[4,2,512,256]{3,2,1,0:T(8,128)(2,1)}, u32[]{:S(2)}, u32[]{:S(2)}) collective-permute-start(bf16[4,2,512,256]{3,2,1,0:T(8,128)(2,1)S(1)} %all-to-all-done.both_ref), channel_id=1, source_target_pairs={{0,8},{8,16},{16,24},{24,32},{32,40},{40,48},{48,56},{56,64},{64,7... | collective-permute-start | bytes 6291464 | tf_op jit(solution)/shard_map/ppermute | solution.py:28
  62.8 27.3 %all-to-all-start.2 = ((f32[8,8,512]{2,1,0:T(8,128)}), f32[8,8,512]{2,1,0:T(8,128)S(1)}, u32[]{:S(2)}, u32[]{:S(2)}) async-start(f32[8,8,512]{2,1,0:T(8,128)} %copy-done.17), calls=%async_computation.2 | async-start | bytes 262144 | tf_op jit(solution)/shard_map/all_to_all | solution.py:217
  92.7 46.9 %all-to-all-start.1 = ((bf16[4,2,512,256]{3,2,1,0:T(8,128)(2,1)}), bf16[4,2,512,256]{3,2,1,0:T(8,128)(2,1)}, u32[]{:S(2)}, u32[]{:S(2)}) async-start(bf16[4,2,512,256]{3,2,1,0:T(8,128)(2,1)} %broadcast_in_dim.35), calls=%async_computation.1 | async-start | bytes 4194304 | tf_op jit(solution)/shard_map/all_to_all | solution.py:33
  98.9 1.1 copy-start.15
  100.0 0.7 copy-start.18
  101.0 0.7 copy-start.6
  101.7 37.1 %collective-permute-start.3 = (bf16[288,512]{1,0:T(8,128)(2,1)S(1)}, bf16[288,512]{1,0:T(8,128)(2,1)S(1)}, u32[]{:S(2)}, u32[]{:S(2)}) collective-permute-start(bf16[288,512]{1,0:T(8,128)(2,1)S(1)} %get-tuple-element.28), channel_id=1, source_target_pairs={{0,8},{8,16},{16,24},{24,32},{32,40},{40,48},{48,56},{56,64},{64,7... | collective-permute-start | bytes 884744 | tf_op jit(solution)/shard_map/ppermute | solution.py:28
  103.6 32.0 %collective-permute-start.4 = (f32[1,512]{1,0:T(1,128)S(1)}, f32[1,512]{1,0:T(1,128)S(1)}, u32[]{:S(2)}, u32[]{:S(2)}) collective-permute-start(f32[1,512]{1,0:T(1,128)S(1)} %copy-done.18), channel_id=1, source_target_pairs={{0,8},{8,16},{16,24},{24,32},{32,40},{40,48},{48,56},{56,64},{64,7... | collective-permute-start | bytes 6152 | tf_op jit(solution)/shard_map/ppermute | solution.py:28
  136.9 12.9 %copy-start.19 = (f32[1,512]{1,0:T(1,128)}, f32[1,512]{1,0:T(1,128)S(1)}, u32[]{:S(2)}) copy-start(f32[1,512]{1,0:T(1,128)S(1)} %get-tuple-element.42.mass_ref) | copy-start | bytes 6148
  136.9 17.7 %collective-permute-start.5 = (f32[1,512]{1,0:T(1,128)}, f32[1,512]{1,0:T(1,128)}, u32[]{:S(2)}, u32[]{:S(2)}) collective-permute-start(f32[1,512]{1,0:T(1,128)} %get-tuple-element.41), channel_id=1, source_target_pairs={{0,16},{8,24},{16,32},{24,40},{32,48},{40,56},{48,64},{56,72},{64,... | collective-permute-start | bytes 6152 | tf_op jit(solution)/shard_map/ppermute | solution.py:28
  138.8 0.7 copy-start.9
  139.5 1.3 copy-start.4
  140.8 1.0 copy-start.7
  141.8 1.0 copy-start.10
  142.7 0.7 copy-start.22
  148.3 0.8 copy-start.12
  149.2 0.6 copy-start.16
  149.8 29.4 %all-to-all-start.3 = ((f32[8,8,512]{2,1,0:T(8,128)}), f32[8,8,512]{2,1,0:T(8,128)S(1)}, u32[]{:S(2)}, u32[]{:S(2)}) async-start(f32[8,8,512]{2,1,0:T(8,128)} %copy-done.16), calls=%async_computation.3 | async-start | bytes 262144 | tf_op jit(solution)/shard_map/all_to_all | solution.py:238
  155.3 13.9 %copy-start.26 = (f32[1,512]{1,0:T(1,128)}, f32[1,512]{1,0:T(1,128)S(1)}, u32[]{:S(2)}) copy-start(f32[1,512]{1,0:T(1,128)S(1)} %multiply_add_fusion.1) | copy-start | bytes 6148
  155.3 13.9 %collective-permute-start.6 = (f32[1,512]{1,0:T(1,128)S(1)}, f32[1,512]{1,0:T(1,128)S(1)}, u32[]{:S(2)}, u32[]{:S(2)}) collective-permute-start(f32[1,512]{1,0:T(1,128)S(1)} %multiply_add_fusion.1), channel_id=1, source_target_pairs={{0,496},{8,504},{16,0},{24,8},{32,16},{40,24},{48,32},{56,40},{64,... | collective-permute-start | bytes 6152 | tf_op jit(solution)/shard_map/ppermute | solution.py:28
  170.5 1.0 copy-start.8
  171.5 1.0 copy-start.11
  172.4 0.7 copy-start.23
  173.1 6.1 %copy-start.13 = (f32[288,512]{1,0:T(8,128)S(1)}, f32[288,512]{1,0:T(8,128)}, u32[]{:S(2)}) copy-start(f32[288,512]{1,0:T(8,128)} %copy-done.12) | copy-start | bytes 1769476
  177.6 1.6 copy-start
  179.2 1.9 copy-start.1
  181.1 0.7 copy-start.20
  181.8 0.7 copy-start.24
  186.6 4.2 %collective-permute-start.7 = (bf16[4,8,32,288]{3,2,1,0:T(8,128)(2,1)S(1)}, bf16[4,8,32,288]{3,2,1,0:T(8,128)(2,1)S(1)}, u32[]{:S(2)}, u32[]{:S(2)}) collective-permute-start(bf16[4,8,32,288]{3,2,1,0:T(8,128)(2,1)S(1)} %get-tuple-element.38), channel_id=1, source_target_pairs={{0,8},{8,0},{1,9},{9,1},{2,10},{10,2},{3,11},{11,3},{4,12},{12,4},... | collective-permute-start | bytes 1769480 | tf_op jit(solution)/shard_map/ppermute | solution.py:28
  191.1 45.8 %copy-start.25 = (f32[32,288]{1,0:T(8,128)S(1)}, f32[32,288]{1,0:T(8,128)}, u32[]{:S(2)}) copy-start(f32[32,288]{1,0:T(8,128)} %param.12) | copy-start | bytes 110596
  208.4 28.5 %all-to-all-start.5 = ((bf16[8,32,288]{2,1,0:T(8,128)(2,1)}), bf16[8,32,288]{2,1,0:T(8,128)(2,1)S(1)}, u32[]{:S(2)}, u32[]{:S(2)}) async-start(bf16[8,32,288]{2,1,0:T(8,128)(2,1)} %reduce_sum.21), calls=%async_computation.5 | async-start | bytes 393216 | tf_op jit(solution)/shard_map/all_to_all | solution.py:255

commit v3 on v1

--- a/solution.py
+++ b/solution.py
@@ -24,6 +24,10 @@
     return lax.ppermute(value, axis, [(i, (i + steps) % count) for i in range(count)])
 
 
+def after(value, *others):
+    return lax.optimization_barrier((value,) + others)[0]
+
+
 def to_all(value, axis):
     count = lax.axis_size(axis)
     return lax.all_to_all(jnp.broadcast_to(value[None], (count,) + value.shape), axis, 0, 0)
@@ -33,11 +37,26 @@
     return lax.dot_general(left, right, (((0,), (0,)), ((), ())), preferred_element_type=F32)
 
 
-def merged(own, other, hi):
-    low = jnp.where(hi == 0, own, other)
-    high = jnp.where(hi == 0, other, own)
+def ordered(both, hi):
+    low = jnp.where(hi == 0, both[:, 0], both[:, 1])
+    high = jnp.where(hi == 0, both[:, 1], both[:, 0])
     both = jnp.stack([low, high], axis=1)
     return jnp.transpose(both, (2, 0, 1, 3)).reshape(TOK, 2048)
+
+
+def from_others(value, x):
+    blocks = jnp.stack([value] + [shifted(value, "x", k) for k in (1, 2, 3)])
+    twice = jnp.concatenate([blocks[::-1], blocks[::-1]])
+    return lax.dynamic_slice_in_dim(twice, 3 - x, 4, 0)
+
+
+def coefficients(shares):
+    first, second = shares
+    mass1 = first + (1.0 - jnp.roll(first, 1))
+    mass2 = second * mass1 + jnp.roll((1.0 - second) * mass1, 2)
+    part = (second / mass2 + (1.0 - second) / jnp.roll(mass2, -2)) / first.shape[0]
+    early = part * first + jnp.roll(part, -1) * (1.0 - first)
+    return jnp.stack([mass1, mass2, part, early])
 
 
 def forward(gathered, quotient, residual, targets, gain):
@@ -67,51 +86,36 @@
     core = lax.axis_index("core")
     anchor = slow_weight.astype(F32)
 
-    own_share = shares[:, 0]
-    before = shifted(own_share, REP, 1)
-    after = shifted(own_share, REP, -1)
-
     other0 = shifted(context[0], "z_hi", 1)
-    x_own0 = to_all(context[0], "x")
-    other0, x_own0 = lax.optimization_barrier((other0, x_own0))
-    other1 = shifted(context[1], "z_hi", 1)
-    x_own1 = lax.all_gather(context[1], "x", axis=0)
-    x_other0 = to_all(other0, "x")
-    gathered0 = merged(x_own0, x_other0, hi)
+    row = jnp.repeat(shares[:, 0], 64)[None]
+    all_shares = to_all(row, REP)[:, 0]
+    other0, all_shares = lax.optimization_barrier((other0, all_shares))
+    context1 = after(context[1], other0)
+    other1 = shifted(context1, "z_hi", 1)
+    both0 = to_all(jnp.stack([context[0], other0]), "x")
+    replica = lax.axis_index(REP)
+    table = coefficients((all_shares[:, 0], all_shares[:, 64]))
+    mine = lax.dynamic_slice_in_dim(table, replica, 1, 1)
+    mine = after(mine, other1)
+    share0 = shares[0, 0]
+    gathered0 = ordered(both0, hi)
 
     output0, sums0 = forward(gathered0, slow_weight, residual[0], targets[0], gain)
     totals0 = jnp.sum(to_all(sums0, TP), axis=0)
+    pair1 = jnp.stack([context1, other1])
+    both1 = from_others(after(pair1, sums0), lax.axis_index("x"))
+    gathered1 = ordered(both1, hi)
     grad0 = backward(output0, totals0, targets[0], gain)
     weight_grad0 = contract_rows(gathered0, grad0)
 
-    incoming = shifted(((1.0 - own_share[0]) * weight_grad0).astype(BF16), REP, 1)
-    other1, weight_grad0 = lax.optimization_barrier((other1, weight_grad0))
-    x_other1 = to_all(other1, "x")
-    window = jnp.stack([before, own_share, after])
-    earlier = shifted(window, REP, 2)
-    later = shifted(window, REP, -2)
-    gathered1 = merged(x_own1, x_other1, hi)
-
-    mass1 = own_share[0] + (1.0 - before[0])
-    step0 = own_share[0] * weight_grad0 + incoming.astype(F32)
-    quotient1 = (anchor - (LR / mass1) * step0).astype(BF16)
+    incoming = shifted(((1.0 - share0) * weight_grad0).astype(BF16), REP, 1)
+    step0 = share0 * weight_grad0 + incoming.astype(F32)
+    quotient1 = (anchor - (LR / mine[0, 0]) * step0).astype(BF16)
     output1, sums1 = forward(gathered1, quotient1, residual[1], targets[1], gain)
     totals1 = jnp.sum(to_all(sums1, TP), axis=0)
     grad1 = backward(output1, totals1, targets[1], gain)
     weight_grad1 = contract_rows(gathered1, grad1)
-
-    near = jnp.concatenate([earlier[:2], window, later[1:]])
-    first = {k: near[k + 3, 0] for k in range(-3, 4)}
-    second = {k: near[k + 3, 1] for k in range(-3, 4)}
-    mass_of = {k: first[k] + (1.0 - first[k - 1]) for k in range(-2, 4)}
-    final_of = {
-        k: second[k] * mass_of[k] + (1.0 - second[k - 2]) * mass_of[k - 2] for k in range(0, 4)
-    }
-    part_of = {k: second[k] / final_of[k] + (1.0 - second[k]) / final_of[k + 2] for k in (0, 1)}
-    replicas = lax.axis_size(REP)
-    coef1 = part_of[0] / replicas
-    coef0 = (part_of[0] * first[0] + part_of[1] * (1.0 - first[0])) / replicas
-    total = coef0 * weight_grad0 + coef1 * weight_grad1
+    total = mine[3, 0] * weight_grad0 + mine[2, 0] * weight_grad1
 
     width = total.shape[1]
     total = total.reshape(8, 4, 2, 32, width)
@@ -127,7 +131,7 @@
     anchor_rows = lax.dynamic_slice_in_dim(slow_weight, lax.axis_index(REP) * 32, 32, 0)
     new_momentum = BETA * momentum + gradient
     new_weight = anchor_rows.astype(F32) - ALPHA * LR * new_momentum
-    return (new_weight, new_momentum, final_of[0][None])
+    return (new_weight, new_momentum, mine[1])
 
 
 def solution(mesh):

time: 232 us -> 207 us (0.89)
  between operations: 30.1 us -> 2.32 us
  waiting for transfers between devices: 67.6 us -> 74.1 us
  other arithmetic: 2.87 us -> 9.08 us
  starting transfers between devices: 81.9 us -> 77.1 us
  local copies, waits for them, and re-layouts: 18.2 us -> 13.7 us
    all_to_all x5 -> x4, waiting for transfers between devices: 22.4 us -> 49.4 us  [to_all(): lax.all_to_all(jnp.broadcast_to(value[None], (count,) + value.shape), axi...]
    ppermute x8 -> x7, waiting for transfers between devices: 33.8 us -> 12.4 us  [shifted(): lax.ppermute(value, axis, [(i, (i + steps) % count) for i in range(count)])]
    ppermute x8 -> x7, starting transfers between devices: 44.5 us -> 38.8 us  [shifted(): lax.ppermute(value, axis, [(i, (i + steps) % count) for i in range(count)])]
    all_to_all x5 -> x4, starting transfers between devices: 29.5 us -> 32.3 us  [to_all(): lax.all_to_all(jnp.broadcast_to(value[None], (count,) + value.shape), axi...]
    slice x6 -> x5, local copies, waits for them, and re-layouts: 4.86 us -> 2.48 us  [the longest x1 1.08 us: body(): other0 = shifted(context[0], 'z_hi', 1)]
    concatenate x0 -> x1, other arithmetic: none -> 2.33 us  [from_others(): twice = jnp.concatenate([blocks[::-1], blocks[::-1]])]
  transfers between devices with their start and end apart: 15 -> 12, of which waited for: 7 -> 9; matrix products, arithmetic and copies ran while one was open for 8% -> 9% of each run, Pallas kernels for 0% -> 0%
where the time goes in v3:
time: 207 us; the launch traced here: 206 us
  starting transfers between devices  77.1 us (37%)
  waiting for transfers between devices  74.1 us (36%)
  blocking collectives  17 us (8%)
  local copies, waits for them, and re-layouts  13.7 us (7%)
  matrix products  13.1 us (6%)
  other arithmetic  9.08 us (4%)
  between operations  2.32 us (1%)
    all_to_all x4, waiting for transfers between devices, to_all(): lax.all_to_all(jnp.broadcast_to(value[None], (count,) + value.shape), axi...  49.4 us
    ppermute x7, starting transfers between devices, shifted(): lax.ppermute(value, axis, [(i, (i + steps) % count) for i in range(count)])  38.8 us
    all_to_all x4, starting transfers between devices, to_all(): lax.all_to_all(jnp.broadcast_to(value[None], (count,) + value.shape), axi...  32.3 us
    all_to_all x1, blocking collectives, body(): parts = lax.all_to_all(parts, 'y', 0, 0)  17 us
    ppermute x7, waiting for transfers between devices, shifted(): lax.ppermute(value, axis, [(i, (i + steps) % count) for i in range(count)])  12.4 us
    all_to_all x1, waiting for transfers between devices, body(): parts = lax.all_to_all(total.astype(BF16), 'z_lo', 0, 0)  12.3 us
    dot_general x2, matrix products, contract_rows(): lax.dot_general(left, right, (((0,), (0,)), ((), ())), preferred_element_...  9.12 us
    all_to_all x1, starting transfers between devices, body(): parts = lax.all_to_all(total.astype(BF16), 'z_lo', 0, 0)  5.97 us
  transfers between devices with their start and end apart: 12, of which 9 were waited for; matrix products, arithmetic and copies ran while one was open for 9% of the time, Pallas kernels for 0%

profile of v3, /device:TPU:32, one launch (start us, length us, event | category | flops | bytes accessed | tf_op | source)
XLA Modules:
  0.0 206.4 jit_solution(5734700999068154803)
XLA Ops:
  0.6 1.1 fusion.48
  1.7 14.8 %collective-permute-start = (bf16[512,256]{1,0:T(8,128)(2,1)S(1)}, bf16[512,256]{1,0:T(8,128)(2,1)S(1)}, u32[]{:S(2)}, u32[]{:S(2)}) collective-permute-start(bf16[512,256]{1,0:T(8,128)(2,1)S(1)} %get-tuple-element.34), channel_id=1, source_target_pairs={{0,1},{1,0},{2,3},{3,2},{4,5},{5,4},{6,7},{7,6},{8,9},{9,8},{10,11... | collective-permute-start | bytes 786440 | tf_op jit(solution)/shard_map/ppermute | solution.py:24
  16.5 0.7 broadcast_in_dim.12
  17.4 0.6 broadcast_in_dim.14
  18.0 9.2 %all-to-all-start = ((f32[64,1,128]{2,1,0:T(1,128)}), f32[64,1,128]{2,1,0:T(1,128)S(1)}, u32[]{:S(2)}, u32[]{:S(2)}) async-start(f32[64,1,128]{2,1,0:T(1,128)} %broadcast_in_dim.14), calls=%async_computation | async-start | bytes 65536 | tf_op jit(solution)/shard_map/all_to_all | solution.py:33
  28.0 0.7 broadcast_multiply_fusion
  28.7 15.1 %all-to-all-done = f32[64,1,128]{2,1,0:T(1,128)S(1)} async-done(((f32[64,1,128]{2,1,0:T(1,128)}), f32[64,1,128]{2,1,0:T(1,128)S(1)}, u32[]{:S(2)}, u32[]{:S(2)}) %all-to-all-start) | async-done | bytes 32800 | tf_op jit(solution)/shard_map/all_to_all | solution.py:33
  43.9 0.2 copy.31
  44.1 1.5 broadcast_in_dim.15
  45.6 4.3 %all-to-all-start.1 = ((bf16[4,2,512,256]{2,3,1,0:T(8,128)(2,1)}), bf16[4,2,512,256]{2,3,1,0:T(8,128)(2,1)S(1)}, u32[]{:S(2)}, u32[]{:S(2)}) async-start(bf16[4,2,512,256]{2,3,1,0:T(8,128)(2,1)} %broadcast_in_dim.15), calls=%async_computation.1 | async-start | bytes 4194304 | tf_op jit(solution)/shard_map/all_to_all | solution.py:33
  50.2 0.5 slice.126
  50.7 8.3 %collective-permute-start.1 = (bf16[512,256]{0,1:T(8,128)(2,1)S(1)}, bf16[512,256]{0,1:T(8,128)(2,1)S(1)}, u32[]{:S(2)}, u32[]{:S(2)}) collective-permute-start(bf16[512,256]{0,1:T(8,128)(2,1)S(1)} %bitcast.118), channel_id=1, source_target_pairs={{0,1},{1,0},{2,3},{3,2},{4,5},{5,4},{6,7},{7,6},{8,9},{9,8},{10,11... | collective-permute-start | bytes 786440 | tf_op jit(solution)/shard_map/ppermute | solution.py:24
  59.0 0.7 subtract_multiply_fusion
  60.1 16.0 %all-to-all-done.1 = bf16[4,2,512,256]{2,3,1,0:T(8,128)(2,1)S(1)} async-done(((bf16[4,2,512,256]{2,3,1,0:T(8,128)(2,1)}), bf16[4,2,512,256]{2,3,1,0:T(8,128)(2,1)S(1)}, u32[]{:S(2)}, u32[]{:S(2)}) %all-to-all-start.1) | async-done | bytes 2097184 | tf_op jit(solution)/shard_map/all_to_all | solution.py:33
  76.4 1.0 copy-done.1
  77.6 0.2 copy-done.6
  77.8 1.7 multiply_reduce_fusion.2
  79.5 0.6 broadcast_in_dim.16
  80.2 7.7 %all-to-all-start.2 = ((f32[8,3,512]{2,1,0:T(4,128)}), f32[8,3,512]{2,1,0:T(4,128)S(1)}, u32[]{:S(2)}, u32[]{:S(2)}) async-start(f32[8,3,512]{2,1,0:T(4,128)} %broadcast_in_dim.16), calls=%async_computation.2 | async-start | bytes 131072 | tf_op jit(solution)/shard_map/all_to_all | solution.py:33
  88.0 3.9 %collective-permute-start.2 = (bf16[2,512,256]{1,2,0:T(8,128)(2,1)S(1)}, bf16[2,512,256]{1,2,0:T(8,128)(2,1)S(1)}, u32[]{:S(2)}, u32[]{:S(2)}) collective-permute-start(bf16[2,512,256]{1,2,0:T(8,128)(2,1)S(1)} %pad_maximum_fusion.4), channel_id=1, source_target_pairs={{0,2},{2,4},{4,6},{6,0},{1,3},{3,5},{5,7},{7,1},{8,10},{10,12},{12... | collective-permute-start | bytes 1572872 | tf_op jit(solution)/shard_map/ppermute | solution.py:24
  91.9 4.6 %collective-permute-start.3 = (bf16[2,512,256]{1,2,0:T(8,128)(2,1)S(1)}, bf16[2,512,256]{1,2,0:T(8,128)(2,1)}, u32[]{:S(2)}, u32[]{:S(2)}) collective-permute-start(bf16[2,512,256]{1,2,0:T(8,128)(2,1)S(1)} %pad_maximum_fusion.4), channel_id=1, source_target_pairs={{0,4},{2,6},{4,0},{6,2},{1,5},{3,7},{5,1},{7,3},{8,12},{10,14},{12... | collective-permute-start | bytes 1572872 | tf_op jit(solution)/shard_map/ppermute | solution.py:24
  96.5 3.4 %collective-permute-start.4 = (bf16[2,512,256]{1,2,0:T(8,128)(2,1)S(1)}, bf16[2,512,256]{1,2,0:T(8,128)(2,1)}, u32[]{:S(2)}, u32[]{:S(2)}) collective-permute-start(bf16[2,512,256]{1,2,0:T(8,128)(2,1)S(1)} %pad_maximum_fusion.4), channel_id=1, source_target_pairs={{0,6},{2,0},{4,2},{6,4},{1,7},{3,1},{5,3},{7,5},{8,14},{10,8},{12,... | collective-permute-start | bytes 1572872 | tf_op jit(solution)/shard_map/ppermute | solution.py:24
  99.9 3.2 %all-to-all-done.2 = f32[8,3,512]{2,1,0:T(4,128)S(1)} async-done(((f32[8,3,512]{2,1,0:T(4,128)}), f32[8,3,512]{2,1,0:T(4,128)S(1)}, u32[]{:S(2)}, u32[]{:S(2)}) %all-to-all-start.2) | async-done | bytes 49184 | tf_op jit(solution)/shard_map/all_to_all | solution.py:33
  103.2 3.8 %multiply_convert_fusion = (bf16[2048,288]{0,1:T(8,128)(2,1)}, f32[2048,288]{0,1:T(8,128)}) fusion(f32[]{:T(128)S(6)} %sub.98, bf16[512,2048]{0,1:T(8,128)(2,1)S(1)} %bitcast.114, f32[512,288]{0,1:T(8,128)} %get-tuple-element.52, f32[512]{0:T(512)S(1)} %bitcast.130, f32[512]{0:T(512)S(1)} %bitcast.129, f32[288]{0:T(512)S(1)} %copy-done.3, ...), kind=kOutput, calls=%fused_computation.5 | convolution fusion | flops 606486528 | bytes 6527236 | tf_op jit(solution)/shard_map/dot_general | solution.py:37
  107.0 1.9 collective-permute-start.5
  108.9 0.8 fusion.40
  109.8 0.6 fusion.49
  111.0 4.4 %collective-permute-done.3 = bf16[2,512,256]{1,2,0:T(8,128)(2,1)} collective-permute-done((bf16[2,512,256]{1,2,0:T(8,128)(2,1)S(1)}, bf16[2,512,256]{1,2,0:T(8,128)(2,1)}, u32[]{:S(2)}, u32[]{:S(2)}) %collective-permute-start.3) | collective-permute-done | bytes 524320 | tf_op jit(solution)/shard_map/ppermute | solution.py:24
  115.5 1.2 collective-permute-done.4
  116.7 1.5 pad_maximum_fusion.1
  118.1 1.5 rev.4
  119.7 2.3 %fusion.1 = bf16[4,2,512,256]{2,3,1,0:T(8,128)(2,1)S(1)} fusion(s32[]{:T(128)S(6)} %select_n.55, bf16[4,2,512,256]{2,3,1,0:T(8,128)(2,1)} %rev.4), kind=kLoop, calls=%fused_computation.6 | loop fusion | flops 1048576 | bytes 4194308 | tf_op jit(solution)/shard_map/concatenate | solution.py:49
  122.4 4.5 %collective-permute-done.5 = bf16[2048,288]{0,1:T(8,128)(2,1)} collective-permute-done((bf16[2048,288]{0,1:T(8,128)(2,1)}, bf16[2048,288]{0,1:T(8,128)(2,1)}, u32[]{:S(2)}, u32[]{:S(2)}) %collective-permute-start.5) | collective-permute-done | bytes 1179680 | tf_op jit(solution)/shard_map/ppermute | solution.py:24
  126.9 2.3 %multiply_reduce_fusion = (f32[512]{0:T(512)S(1)}, f32[512]{0:T(512)S(1)}, f32[512]{0:T(512)S(1)}, f32[512,288]{0,1:T(8,128)S(1)}) fusion(f32[288]{0:T(512)S(1)} %copy-done.3, bf16[2,512,288]{1,2,0:T(8,128)(2,1)S(1)} %copy-done.7, bf16[512,2048]{0,1:T(8,128)(2,1)S(1)} %bitcast.115, bf16[2048,288]{0,1:T(8,128)(2,1)} %collective-permute-done.5, ...), kind=kOutput, calls=%fused_computation.35 | convolution fusion | flops 609581568 | bytes 8002696 | tf_op jit(solution)/shard_map/dot_general | solution.py:63
  129.2 0.6 broadcast_in_dim.17
  129.9 11.1 %all-to-all-start.3 = ((f32[8,3,512]{2,1,0:T(4,128)}), f32[8,3,512]{2,1,0:T(4,128)S(1)}, u32[]{:S(2)}, u32[]{:S(2)}) async-start(f32[8,3,512]{2,1,0:T(4,128)} %broadcast_in_dim.17), calls=%async_computation.3 | async-start | bytes 131072 | tf_op jit(solution)/shard_map/all_to_all | solution.py:33
  141.0 15.1 %all-to-all-done.3 = f32[8,3,512]{2,1,0:T(4,128)S(1)} async-done(((f32[8,3,512]{2,1,0:T(4,128)}), f32[8,3,512]{2,1,0:T(4,128)S(1)}, u32[]{:S(2)}, u32[]{:S(2)}) %all-to-all-start.3) | async-done | bytes 49184 | tf_op jit(solution)/shard_map/all_to_all | solution.py:33
  156.1 5.3 %fusion = f32[2048,288]{0,1:T(8,128)} fusion(bf16[512,2048]{0,1:T(8,128)(2,1)S(1)} %bitcast.116, f32[2048,288]{0,1:T(8,128)} %get-tuple-element.54, f32[]{:T(128)} %bitcast.23, f32[]{:T(128)} %bitcast.11, f32[512,288]{0,1:T(8,128)S(1)} %get-tuple-element.55, f32[512]{0:T(512)S(1)} %bitcast.128, f32[512]{0:T(512)S(1)} %bitcast.127, f32[288]{0:T(512)S(1)} %copy-done.3, ...), kind=kOutput, calls=%fused_computation.3 | convolution fusion | flops 607076352 | bytes 7708680 | tf_op jit(solution)/shard_map/dot_general | solution.py:37
  161.4 2.2 %copy.34 = f32[2048,288]{1,0:T(8,128)S(1)} copy(f32[2048,288]{0,1:T(8,128)} %fusion) | data formatting | bytes 4718592 | tf_op jit(solution)/shard_map/add | solution.py:118
  163.8 1.9 collective-permute-start.6
  165.7 2.3 %collective-permute-done.6 = bf16[8,4,32,288]{3,2,1,0:T(8,128)(2,1)S(1)} collective-permute-done((bf16[8,4,32,288]{3,2,1,0:T(8,128)(2,1)S(1)}, bf16[8,4,32,288]{3,2,1,0:T(8,128)(2,1)S(1)}, u32[]{:S(2)}, u32[]{:S(2)}) %collective-permute-start.6) | collective-permute-done | bytes 589856 | tf_op jit(solution)/shard_map/ppermute | solution.py:24
  168.0 0.4 fusion.6
  168.5 17.0 %all_to_all.30 = bf16[4,8,32,288]{3,2,1,0:T(8,128)(2,1)S(1)} all-to-all(bf16[4,8,32,288]{3,2,1,0:T(8,128)(2,1)S(1)} %copy.35), channel_id=1, replica_groups=mesh['z_lo'=8,'y'=4,'core'=2,'x'=4,'z_hi'=2] {'y'}, dimensions={0} | all-to-all | bytes 1179648 | tf_op jit(solution)/shard_map/all_to_all | solution.py:126
  185.5 0.8 reduce_sum.101
  186.3 6.0 %all-to-all-start.5 = ((bf16[8,32,288]{2,1,0:T(8,128)(2,1)}), bf16[8,32,288]{2,1,0:T(8,128)(2,1)S(1)}, u32[]{:S(2)}, u32[]{:S(2)}) async-start(bf16[8,32,288]{2,1,0:T(8,128)(2,1)} %reduce_sum.101), calls=%async_computation.5 | async-start | bytes 393216 | tf_op jit(solution)/shard_map/all_to_all | solution.py:128
  192.3 1.0 constant_dynamic-slice_fusion.1
  193.4 12.3 %all-to-all-done.5 = bf16[8,32,288]{2,1,0:T(8,128)(2,1)S(1)} async-done(((bf16[8,32,288]{2,1,0:T(8,128)(2,1)}), bf16[8,32,288]{2,1,0:T(8,128)(2,1)S(1)}, u32[]{:S(2)}, u32[]{:S(2)}) %all-to-all-start.5) | async-done | bytes 147488 | tf_op jit(solution)/shard_map/all_to_all | solution.py:128
  205.7 0.7 multiply_subtract_fusion
  (50 shorter events, 2.5 us)
Async XLA Ops:
  1.7 42.1 %collective-permute-start = (bf16[512,256]{1,0:T(8,128)(2,1)S(1)}, bf16[512,256]{1,0:T(8,128)(2,1)S(1)}, u32[]{:S(2)}, u32[]{:S(2)}) collective-permute-start(bf16[512,256]{1,0:T(8,128)(2,1)S(1)} %get-tuple-element.34), channel_id=1, source_target_pairs={{0,1},{1,0},{2,3},{3,2},{4,5},{5,4},{6,7},{7,6},{8,9},{9,8},{10,11... | collective-permute-start | bytes 786440 | tf_op jit(solution)/shard_map/ppermute | solution.py:24
  18.0 25.8 %all-to-all-start = ((f32[64,1,128]{2,1,0:T(1,128)}), f32[64,1,128]{2,1,0:T(1,128)S(1)}, u32[]{:S(2)}, u32[]{:S(2)}) async-start(f32[64,1,128]{2,1,0:T(1,128)} %broadcast_in_dim.14), calls=%async_computation | async-start | bytes 65536 | tf_op jit(solution)/shard_map/all_to_all | solution.py:33
  45.6 30.4 %all-to-all-start.1 = ((bf16[4,2,512,256]{2,3,1,0:T(8,128)(2,1)}), bf16[4,2,512,256]{2,3,1,0:T(8,128)(2,1)S(1)}, u32[]{:S(2)}, u32[]{:S(2)}) async-start(bf16[4,2,512,256]{2,3,1,0:T(8,128)(2,1)} %broadcast_in_dim.15), calls=%async_computation.1 | async-start | bytes 4194304 | tf_op jit(solution)/shard_map/all_to_all | solution.py:33
  50.7 37.2 %collective-permute-start.1 = (bf16[512,256]{0,1:T(8,128)(2,1)S(1)}, bf16[512,256]{0,1:T(8,128)(2,1)S(1)}, u32[]{:S(2)}, u32[]{:S(2)}) collective-permute-start(bf16[512,256]{0,1:T(8,128)(2,1)S(1)} %bitcast.118), channel_id=1, source_target_pairs={{0,1},{1,0},{2,3},{3,2},{4,5},{5,4},{6,7},{7,6},{8,9},{9,8},{10,11... | collective-permute-start | bytes 786440 | tf_op jit(solution)/shard_map/ppermute | solution.py:24
  76.2 1.3 copy-start.1
  76.2 1.3 copy-start.3
  76.2 1.4 copy-start.4
  76.2 1.6 copy-start.6
  80.2 23.0 %all-to-all-start.2 = ((f32[8,3,512]{2,1,0:T(4,128)}), f32[8,3,512]{2,1,0:T(4,128)S(1)}, u32[]{:S(2)}, u32[]{:S(2)}) async-start(f32[8,3,512]{2,1,0:T(4,128)} %broadcast_in_dim.16), calls=%async_computation.2 | async-start | bytes 131072 | tf_op jit(solution)/shard_map/all_to_all | solution.py:33
  88.0 23.1 %collective-permute-start.2 = (bf16[2,512,256]{1,2,0:T(8,128)(2,1)S(1)}, bf16[2,512,256]{1,2,0:T(8,128)(2,1)S(1)}, u32[]{:S(2)}, u32[]{:S(2)}) collective-permute-start(bf16[2,512,256]{1,2,0:T(8,128)(2,1)S(1)} %pad_maximum_fusion.4), channel_id=1, source_target_pairs={{0,2},{2,4},{4,6},{6,0},{1,3},{3,5},{5,7},{7,1},{8,10},{10,12},{12... | collective-permute-start | bytes 1572872 | tf_op jit(solution)/shard_map/ppermute | solution.py:24
  91.9 23.6 %collective-permute-start.3 = (bf16[2,512,256]{1,2,0:T(8,128)(2,1)S(1)}, bf16[2,512,256]{1,2,0:T(8,128)(2,1)}, u32[]{:S(2)}, u32[]{:S(2)}) collective-permute-start(bf16[2,512,256]{1,2,0:T(8,128)(2,1)S(1)} %pad_maximum_fusion.4), channel_id=1, source_target_pairs={{0,4},{2,6},{4,0},{6,2},{1,5},{3,7},{5,1},{7,3},{8,12},{10,14},{12... | collective-permute-start | bytes 1572872 | tf_op jit(solution)/shard_map/ppermute | solution.py:24
  96.5 20.2 %collective-permute-start.4 = (bf16[2,512,256]{1,2,0:T(8,128)(2,1)S(1)}, bf16[2,512,256]{1,2,0:T(8,128)(2,1)}, u32[]{:S(2)}, u32[]{:S(2)}) collective-permute-start(bf16[2,512,256]{1,2,0:T(8,128)(2,1)S(1)} %pad_maximum_fusion.4), channel_id=1, source_target_pairs={{0,6},{2,0},{4,2},{6,4},{1,7},{3,1},{5,3},{7,5},{8,14},{10,8},{12,... | collective-permute-start | bytes 1572872 | tf_op jit(solution)/shard_map/ppermute | solution.py:24
  107.0 19.9 %collective-permute-start.5 = (bf16[2048,288]{0,1:T(8,128)(2,1)}, bf16[2048,288]{0,1:T(8,128)(2,1)}, u32[]{:S(2)}, u32[]{:S(2)}) collective-permute-start(bf16[2048,288]{0,1:T(8,128)(2,1)} %get-tuple-element.53), channel_id=1, source_target_pairs={{0,8},{8,16},{16,24},{24,32},{32,40},{40,48},{48,56},{56,64},{64,7... | collective-permute-start | bytes 3538952 | tf_op jit(solution)/shard_map/ppermute | solution.py:24
  122.0 4.9 %copy-start.9 = (f32[2048,288]{0,1:T(8,128)S(1)}, f32[2048,288]{0,1:T(8,128)}, u32[]{:S(2)}) copy-start(f32[2048,288]{0,1:T(8,128)} %get-tuple-element.54) | copy-start | bytes 7077892
  122.2 4.8 %copy-start.2 = (bf16[2048,288]{0,1:T(8,128)(2,1)S(1)}, bf16[2048,288]{0,1:T(8,128)(2,1)}, u32[]{:S(2)}) copy-start(bf16[2048,288]{0,1:T(8,128)(2,1)} %param.11) | copy-start | bytes 3538948
  122.2 4.7 %copy-start.5 = (bf16[2,512,288]{1,2,0:T(8,128)(2,1)S(1)}, bf16[2,512,288]{1,2,0:T(8,128)(2,1)}, u32[]{:S(2)}) copy-start(bf16[2,512,288]{1,2,0:T(8,128)(2,1)} %param.8) | copy-start | bytes 1769476
  122.2 4.7 %copy-start.7 = (bf16[2,512,288]{1,2,0:T(8,128)(2,1)S(1)}, bf16[2,512,288]{1,2,0:T(8,128)(2,1)}, u32[]{:S(2)}) copy-start(bf16[2,512,288]{1,2,0:T(8,128)(2,1)} %param.9) | copy-start | bytes 1769476
  122.2 4.7 %copy-start.8 = (f32[2,1]{0,1:T(1,128)S(1)}, f32[2,1]{0,1:T(1,128)}, u32[]{:S(2)}) copy-start(f32[2,1]{0,1:T(1,128)} %param.13) | copy-start | bytes 28
  129.9 26.2 %all-to-all-start.3 = ((f32[8,3,512]{2,1,0:T(4,128)}), f32[8,3,512]{2,1,0:T(4,128)S(1)}, u32[]{:S(2)}, u32[]{:S(2)}) async-start(f32[8,3,512]{2,1,0:T(4,128)} %broadcast_in_dim.17), calls=%async_computation.3 | async-start | bytes 131072 | tf_op jit(solution)/shard_map/all_to_all | solution.py:33
  163.8 4.2 %collective-permute-start.6 = (bf16[8,4,32,288]{3,2,1,0:T(8,128)(2,1)S(1)}, bf16[8,4,32,288]{3,2,1,0:T(8,128)(2,1)S(1)}, u32[]{:S(2)}, u32[]{:S(2)}) collective-permute-start(bf16[8,4,32,288]{3,2,1,0:T(8,128)(2,1)S(1)} %fusion.5), channel_id=1, source_target_pairs={{0,8},{8,0},{1,9},{9,1},{2,10},{10,2},{3,11},{11,3},{4,12},{12,4},... | collective-permute-start | bytes 1769480 | tf_op jit(solution)/shard_map/ppermute | solution.py:24
  168.5 37.2 %copy-start = (f32[32,288]{1,0:T(8,128)S(1)}, f32[32,288]{1,0:T(8,128)}, u32[]{:S(2)}) copy-start(f32[32,288]{1,0:T(8,128)} %param.12) | copy-start | bytes 110596
  186.3 19.4 %all-to-all-start.5 = ((bf16[8,32,288]{2,1,0:T(8,128)(2,1)}), bf16[8,32,288]{2,1,0:T(8,128)(2,1)S(1)}, u32[]{:S(2)}, u32[]{:S(2)}) async-start(bf16[8,32,288]{2,1,0:T(8,128)(2,1)} %reduce_sum.101), calls=%async_computation.5 | async-start | bytes 393216 | tf_op jit(solution)/shard_map/all_to_all | solution.py:128

commit v4 on v3

--- a/solution.py
+++ b/solution.py
@@ -50,13 +50,11 @@
     return lax.dynamic_slice_in_dim(twice, 3 - x, 4, 0)
 
 
-def coefficients(shares):
-    first, second = shares
-    mass1 = first + (1.0 - jnp.roll(first, 1))
-    mass2 = second * mass1 + jnp.roll((1.0 - second) * mass1, 2)
-    part = (second / mass2 + (1.0 - second) / jnp.roll(mass2, -2)) / first.shape[0]
-    early = part * first + jnp.roll(part, -1) * (1.0 - first)
-    return jnp.stack([mass1, mass2, part, early])
+def merged(own, other, hi):
+    low = jnp.where(hi == 0, own, other)
+    high = jnp.where(hi == 0, other, own)
+    both = jnp.stack([low, high], axis=1)
+    return jnp.transpose(both, (2, 0, 1, 3)).reshape(TOK, 2048)
 
 
 def forward(gathered, quotient, residual, targets, gain):
@@ -82,40 +80,41 @@
 
 
 def body(context, residual, targets, gain, slow_weight, momentum, shares):
-    hi = lax.axis_index("z_hi")
-    core = lax.axis_index("core")
+    x, hi, core = lax.axis_index("x"), lax.axis_index("z_hi"), lax.axis_index("core")
     anchor = slow_weight.astype(F32)
 
     other0 = shifted(context[0], "z_hi", 1)
-    row = jnp.repeat(shares[:, 0], 64)[None]
-    all_shares = to_all(row, REP)[:, 0]
-    other0, all_shares = lax.optimization_barrier((other0, all_shares))
+    before0 = shifted(shares[0], REP, 1)
+    own0 = from_others(context[0], x)
+    mass1 = shares[0] + (1.0 - before0)
+    other0, own0, mass1 = lax.optimization_barrier((other0, own0, mass1))
+    wide0 = to_all(other0, "x")
     context1 = after(context[1], other0)
     other1 = shifted(context1, "z_hi", 1)
-    both0 = to_all(jnp.stack([context[0], other0]), "x")
-    replica = lax.axis_index(REP)
-    table = coefficients((all_shares[:, 0], all_shares[:, 64]))
-    mine = lax.dynamic_slice_in_dim(table, replica, 1, 1)
-    mine = after(mine, other1)
+    mass_in = shifted((1.0 - shares[1]) * mass1, REP, 2)
+    own0, wide0, mass_in = lax.optimization_barrier((own0, wide0, mass_in))
+    gathered0 = merged(own0, wide0, hi)
+    mass2 = shares[1] * mass1 + mass_in
     share0 = shares[0, 0]
-    gathered0 = ordered(both0, hi)
 
     output0, sums0 = forward(gathered0, slow_weight, residual[0], targets[0], gain)
     totals0 = jnp.sum(to_all(sums0, TP), axis=0)
     pair1 = jnp.stack([context1, other1])
-    both1 = from_others(after(pair1, sums0), lax.axis_index("x"))
+    both1 = from_others(after(pair1, sums0), x)
     gathered1 = ordered(both1, hi)
     grad0 = backward(output0, totals0, targets[0], gain)
     weight_grad0 = contract_rows(gathered0, grad0)
 
     incoming = shifted(((1.0 - share0) * weight_grad0).astype(BF16), REP, 1)
+    mass_later = shifted(after(mass2, weight_grad0), REP, -2)
     step0 = share0 * weight_grad0 + incoming.astype(F32)
-    quotient1 = (anchor - (LR / mine[0, 0]) * step0).astype(BF16)
+    quotient1 = (anchor - (LR / mass1[0]) * step0).astype(BF16)
     output1, sums1 = forward(gathered1, quotient1, residual[1], targets[1], gain)
     totals1 = jnp.sum(to_all(sums1, TP), axis=0)
     grad1 = backward(output1, totals1, targets[1], gain)
     weight_grad1 = contract_rows(gathered1, grad1)
-    total = mine[3, 0] * weight_grad0 + mine[2, 0] * weight_grad1
+    part = (shares[1] / mass2 + (1.0 - shares[1]) / mass_later) / lax.axis_size(REP)
+    total = part[0] * (step0 + weight_grad1)
 
     width = total.shape[1]
     total = total.reshape(8, 4, 2, 32, width)
@@ -131,7 +130,7 @@
     anchor_rows = lax.dynamic_slice_in_dim(slow_weight, lax.axis_index(REP) * 32, 32, 0)
     new_momentum = BETA * momentum + gradient
     new_weight = anchor_rows.astype(F32) - ALPHA * LR * new_momentum
-    return (new_weight, new_momentum, mine[1])
+    return (new_weight, new_momentum, mass2)
 
 
 def solution(mesh):

time: 207 us -> 209 us (level)
  waiting for transfers between devices: 74.1 us -> 54.2 us
  starting transfers between devices: 77.1 us -> 93.9 us
  between operations: 2.32 us -> 7.41 us
  blocking collectives: 17 us -> 19.4 us
  local copies, waits for them, and re-layouts: 13.7 us -> 11.5 us
    all_to_all x4 -> x3, waiting for transfers between devices: 49.4 us -> 5.57 us  [to_all(): lax.all_to_all(jnp.broadcast_to(value[None], (count,) + value.shape), axi...]
    ppermute x7 -> x13, starting transfers between devices: 38.8 us -> 67.7 us  [shifted(): lax.ppermute(value, axis, [(i, (i + steps) % count) for i in range(count)])]
    ppermute x7 -> x13, waiting for transfers between devices: 12.4 us -> 36.7 us  [shifted(): lax.ppermute(value, axis, [(i, (i + steps) % count) for i in range(count)])]
    all_to_all x4 -> x3, starting transfers between devices: 32.3 us -> 22.1 us  [to_all(): lax.all_to_all(jnp.broadcast_to(value[None], (count,) + value.shape), axi...]
    all_to_all x1, blocking collectives: 17 us -> 19.4 us  [body(): parts = lax.all_to_all(parts, 'y', 0, 0)]
    add x1 -> x0, local copies, waits for them, and re-layouts: 2.24 us -> none  [body(): total = mine[3, 0] * weight_grad0 + mine[2, 0] * weight_grad1]
    mul x0 -> x1, local copies, waits for them, and re-layouts: none -> 2.24 us  [body(): total = part[0] * (step0 + weight_grad1)]
  transfers between devices with their start and end apart: 12 -> 17, of which waited for: 9 -> 10; matrix products, arithmetic and copies ran while one was open for 9% -> 7% of each run, Pallas kernels for 0% -> 0%
where the time goes in v4:
time: 209 us; the launch traced here: 208 us
  starting transfers between devices  93.9 us (45%)
  waiting for transfers between devices  54.2 us (26%)
  blocking collectives  19.4 us (9%)
  matrix products  14.5 us (7%)
  local copies, waits for them, and re-layouts  11.5 us (6%)
  between operations  7.41 us (4%)
  other arithmetic  7.22 us (3%)
    ppermute x13, starting transfers between devices, shifted(): lax.ppermute(value, axis, [(i, (i + steps) % count) for i in range(count)])  67.7 us
    ppermute x13, waiting for transfers between devices, shifted(): lax.ppermute(value, axis, [(i, (i + steps) % count) for i in range(count)])  36.7 us
    all_to_all x3, starting transfers between devices, to_all(): lax.all_to_all(jnp.broadcast_to(value[None], (count,) + value.shape), axi...  22.1 us
    all_to_all x1, blocking collectives, body(): parts = lax.all_to_all(parts, 'y', 0, 0)  19.4 us
    all_to_all x1, waiting for transfers between devices, body(): parts = lax.all_to_all(total.astype(BF16), 'z_lo', 0, 0)  12 us
    dot_general x2, matrix products, contract_rows(): lax.dot_general(left, right, (((0,), (0,)), ((), ())), preferred_element_...  9.13 us
    all_to_all x3, waiting for transfers between devices, to_all(): lax.all_to_all(jnp.broadcast_to(value[None], (count,) + value.shape), axi...  5.57 us
    dot_general x2, matrix products, forward(): jnp.dot(gathered, quotient, preferred_element_type=F32)  5.39 us
  transfers between devices with their start and end apart: 17, of which 10 were waited for; matrix products, arithmetic and copies ran while one was open for 7% of the time, Pallas kernels for 0%

profile of v4, /device:TPU:32, one launch (start us, length us, event | category | flops | bytes accessed | tf_op | source)
XLA Modules:
  0.0 208.1 jit_solution(470099732408800955)
XLA Ops:
  0.6 1.1 fusion.42
  1.8 3.4 %collective-permute-start.1 = (bf16[512,256]{0,1:T(8,128)(2,1)S(1)}, bf16[512,256]{0,1:T(8,128)(2,1)S(1)}, u32[]{:S(2)}, u32[]{:S(2)}) collective-permute-start(bf16[512,256]{0,1:T(8,128)(2,1)S(1)} %bitcast.84), channel_id=1, source_target_pairs={{0,2},{2,4},{4,6},{6,0},{1,3},{3,5},{5,7},{7,1},{8,10},{10,12},{12... | collective-permute-start | bytes 786440 | tf_op jit(solution)/shard_map/ppermute | solution.py:24
  5.3 4.6 %collective-permute-start.2 = (bf16[512,256]{0,1:T(8,128)(2,1)S(1)}, bf16[512,256]{0,1:T(8,128)(2,1)S(1)}, u32[]{:S(2)}, u32[]{:S(2)}) collective-permute-start(bf16[512,256]{0,1:T(8,128)(2,1)S(1)} %bitcast.85), channel_id=1, source_target_pairs={{0,4},{2,6},{4,0},{6,2},{1,5},{3,7},{5,1},{7,3},{8,12},{10,14},{12... | collective-permute-start | bytes 786440 | tf_op jit(solution)/shard_map/ppermute | solution.py:24
  9.9 3.3 %collective-permute-start.3 = (bf16[512,256]{0,1:T(8,128)(2,1)S(1)}, bf16[512,256]{0,1:T(8,128)(2,1)S(1)}, u32[]{:S(2)}, u32[]{:S(2)}) collective-permute-start(bf16[512,256]{0,1:T(8,128)(2,1)S(1)} %bitcast.86), channel_id=1, source_target_pairs={{0,6},{2,0},{4,2},{6,4},{1,7},{3,1},{5,3},{7,5},{8,14},{10,8},{12,... | collective-permute-start | bytes 786440 | tf_op jit(solution)/shard_map/ppermute | solution.py:24
  13.2 14.8 %collective-permute-start = (bf16[512,256]{0,1:T(8,128)(2,1)S(1)}, bf16[512,256]{0,1:T(8,128)(2,1)S(1)}, u32[]{:S(2)}, u32[]{:S(2)}) collective-permute-start(bf16[512,256]{0,1:T(8,128)(2,1)S(1)} %bitcast.87), channel_id=1, source_target_pairs={{0,1},{1,0},{2,3},{3,2},{4,5},{5,4},{6,7},{7,6},{8,9},{9,8},{10,11... | collective-permute-start | bytes 786440 | tf_op jit(solution)/shard_map/ppermute | solution.py:24
  28.1 1.3 fusion.43
  29.4 1.9 collective-permute-start.4
  31.3 5.3 %collective-permute-done.4 = f32[1]{0:T(128)} collective-permute-done((f32[1]{0:T(128)}, f32[1]{0:T(128)}, u32[]{:S(2)}, u32[]{:S(2)}) %collective-permute-start.4) | collective-permute-done | bytes 36 | tf_op jit(solution)/shard_map/ppermute | solution.py:24
  38.2 0.4 fusion.4
  38.6 12.0 %collective-permute-done = bf16[512,256]{0,1:T(8,128)(2,1)S(1)} collective-permute-done((bf16[512,256]{0,1:T(8,128)(2,1)S(1)}, bf16[512,256]{0,1:T(8,128)(2,1)S(1)}, u32[]{:S(2)}, u32[]{:S(2)}) %collective-permute-start) | collective-permute-done | bytes 262176 | tf_op jit(solution)/shard_map/ppermute | solution.py:24
  50.6 1.1 broadcast_in_dim.6
  51.7 3.5 %all-to-all-start = ((bf16[4,512,256]{1,2,0:T(8,128)(2,1)}), bf16[4,512,256]{1,2,0:T(8,128)(2,1)S(1)}, u32[]{:S(2)}, u32[]{:S(2)}) async-start(bf16[4,512,256]{1,2,0:T(8,128)(2,1)} %broadcast_in_dim.6), calls=%async_computation | async-start | bytes 2097152 | tf_op jit(solution)/shard_map/all_to_all | solution.py:33
  56.0 4.8 %collective-permute-start.5 = (f32[1]{0:T(128)}, f32[1]{0:T(128)}, u32[]{:S(2)}, u32[]{:S(2)}) collective-permute-start(f32[1]{0:T(128)} %mul.139), channel_id=1, source_target_pairs={{0,16},{8,24},{16,32},{24,40},{32,48},{40,56},{48,64},{56,72},{64,... | collective-permute-start | bytes 20 | tf_op jit(solution)/shard_map/ppermute | solution.py:24
  60.8 12.1 %collective-permute-start.8 = (bf16[512,256]{0,1:T(8,128)(2,1)S(1)}, bf16[512,256]{0,1:T(8,128)(2,1)S(1)}, u32[]{:S(2)}, u32[]{:S(2)}) collective-permute-start(bf16[512,256]{0,1:T(8,128)(2,1)S(1)} %bitcast.83), channel_id=1, source_target_pairs={{0,1},{1,0},{2,3},{3,2},{4,5},{5,4},{6,7},{7,6},{8,9},{9,8},{10,11... | collective-permute-start | bytes 786440 | tf_op jit(solution)/shard_map/ppermute | solution.py:24
  73.3 1.0 copy-done.1
  74.5 0.2 copy-done.6
  74.7 1.7 multiply_reduce_fusion.2
  76.4 0.6 broadcast_in_dim.7
  77.1 8.9 %all-to-all-start.1 = ((f32[8,3,512]{2,1,0:T(4,128)}), f32[8,3,512]{2,1,0:T(4,128)S(1)}, u32[]{:S(2)}, u32[]{:S(2)}) async-start(f32[8,3,512]{2,1,0:T(4,128)} %broadcast_in_dim.7), calls=%async_computation.1 | async-start | bytes 131072 | tf_op jit(solution)/shard_map/all_to_all | solution.py:33
  86.6 2.4 %collective-permute-done.8 = bf16[512,256]{0,1:T(8,128)(2,1)S(1)} collective-permute-done((bf16[512,256]{0,1:T(8,128)(2,1)S(1)}, bf16[512,256]{0,1:T(8,128)(2,1)S(1)}, u32[]{:S(2)}, u32[]{:S(2)}) %collective-permute-start.8) | collective-permute-done | bytes 262176 | tf_op jit(solution)/shard_map/ppermute | solution.py:24
  89.0 3.3 %collective-permute-start.9 = (bf16[2,512,256]{1,2,0:T(8,128)(2,1)S(1)}, bf16[2,512,256]{1,2,0:T(8,128)(2,1)S(1)}, u32[]{:S(2)}, u32[]{:S(2)}) collective-permute-start(bf16[2,512,256]{1,2,0:T(8,128)(2,1)S(1)} %pad_maximum_fusion.4), channel_id=1, source_target_pairs={{0,2},{2,4},{4,6},{6,0},{1,3},{3,5},{5,7},{7,1},{8,10},{10,12},{12... | collective-permute-start | bytes 1572872 | tf_op jit(solution)/shard_map/ppermute | solution.py:24
  92.3 4.6 %collective-permute-start.10 = (bf16[2,512,256]{1,2,0:T(8,128)(2,1)S(1)}, bf16[2,512,256]{1,2,0:T(8,128)(2,1)}, u32[]{:S(2)}, u32[]{:S(2)}) collective-permute-start(bf16[2,512,256]{1,2,0:T(8,128)(2,1)S(1)} %pad_maximum_fusion.4), channel_id=1, source_target_pairs={{0,4},{2,6},{4,0},{6,2},{1,5},{3,7},{5,1},{7,3},{8,12},{10,14},{12... | collective-permute-start | bytes 1572872 | tf_op jit(solution)/shard_map/ppermute | solution.py:24
  96.9 3.4 %collective-permute-start.11 = (bf16[2,512,256]{1,2,0:T(8,128)(2,1)S(1)}, bf16[2,512,256]{1,2,0:T(8,128)(2,1)}, u32[]{:S(2)}, u32[]{:S(2)}) collective-permute-start(bf16[2,512,256]{1,2,0:T(8,128)(2,1)S(1)} %pad_maximum_fusion.4), channel_id=1, source_target_pairs={{0,6},{2,0},{4,2},{6,4},{1,7},{3,1},{5,3},{7,5},{8,14},{10,8},{12,... | collective-permute-start | bytes 1572872 | tf_op jit(solution)/shard_map/ppermute | solution.py:24
  100.3 0.8 all-to-all-done.1
  101.2 3.8 %multiply_convert_fusion = (bf16[2048,288]{0,1:T(8,128)(2,1)}, f32[2048,288]{0,1:T(8,128)}) fusion(f32[]{:T(128)S(6)} %sub.52, bf16[512,2048]{0,1:T(8,128)(2,1)S(1)} %bitcast.81, f32[512,288]{0,1:T(8,128)} %get-tuple-element.41, f32[512]{0:T(512)S(1)} %bitcast.96, f32[512]{0:T(512)S(1)} %bitcast.95, f32[288]{0:T(512)S(1)} %copy-done.3, ...), kind=kOutput, calls=%fused_computation.5 | convolution fusion | flops 606486528 | bytes 6527236 | tf_op jit(solution)/shard_map/dot_general | solution.py:37
  105.0 1.9 collective-permute-start.7
  107.0 7.3 %collective-permute-done.10 = bf16[2,512,256]{1,2,0:T(8,128)(2,1)} collective-permute-done((bf16[2,512,256]{1,2,0:T(8,128)(2,1)S(1)}, bf16[2,512,256]{1,2,0:T(8,128)(2,1)}, u32[]{:S(2)}, u32[]{:S(2)}) %collective-permute-start.10) | collective-permute-done | bytes 524320 | tf_op jit(solution)/shard_map/ppermute | solution.py:24
  114.3 1.3 collective-permute-done.11
  115.6 1.5 pad_maximum_fusion.1
  117.1 1.6 rev.9
  118.7 2.3 %fusion = bf16[4,2,512,256]{2,3,1,0:T(8,128)(2,1)S(1)} fusion(s32[]{:T(128)S(6)} %select_n.49, bf16[4,2,512,256]{2,3,1,0:T(8,128)(2,1)} %rev.9), kind=kLoop, calls=%fused_computation.6 | loop fusion | flops 1048576 | bytes 4194308 | tf_op jit(solution)/shard_map/concatenate | solution.py:49
  121.4 6.0 %collective-permute-done.7 = bf16[2048,288]{0,1:T(8,128)(2,1)} collective-permute-done((bf16[2048,288]{0,1:T(8,128)(2,1)}, bf16[2048,288]{0,1:T(8,128)(2,1)}, u32[]{:S(2)}, u32[]{:S(2)}) %collective-permute-start.7) | collective-permute-done | bytes 1179680 | tf_op jit(solution)/shard_map/ppermute | solution.py:24
  127.4 3.7 %multiply_reduce_fusion = (f32[512]{0:T(512)S(1)}, f32[512]{0:T(512)S(1)}, f32[512]{0:T(512)S(1)}, f32[512,288]{0,1:T(8,128)}) fusion(f32[288]{0:T(512)S(1)} %copy-done.3, bf16[2,512,288]{1,2,0:T(8,128)(2,1)S(1)} %copy-done.7, bf16[512,2048]{0,1:T(8,128)(2,1)S(1)} %bitcast.78, bf16[2048,288]{0,1:T(8,128)(2,1)S(1)} %copy-done.2, ...), kind=kOutput, calls=%fused_computation.40 | convolution fusion | flops 609581568 | bytes 8002696 | tf_op jit(solution)/shard_map/dot_general | solution.py:61
  131.1 0.6 broadcast_in_dim.8
  131.7 9.7 %all-to-all-start.2 = ((f32[8,3,512]{2,1,0:T(4,128)}), f32[8,3,512]{2,1,0:T(4,128)S(1)}, u32[]{:S(2)}, u32[]{:S(2)}) async-start(f32[8,3,512]{2,1,0:T(4,128)} %broadcast_in_dim.8), calls=%async_computation.2 | async-start | bytes 131072 | tf_op jit(solution)/shard_map/all_to_all | solution.py:33
  143.4 7.7 %collective-permute-start.6 = (f32[1]{0:T(128)}, f32[1]{0:T(128)}, u32[]{:S(2)}, u32[]{:S(2)}) collective-permute-start(f32[1]{0:T(128)} %add.68), channel_id=1, source_target_pairs={{0,496},{8,504},{16,0},{24,8},{32,16},{40,24},{48,32},{56,40},{64,... | collective-permute-start | bytes 20 | tf_op jit(solution)/shard_map/ppermute | solution.py:24
  151.8 4.8 %all-to-all-done.2 = f32[8,3,512]{2,1,0:T(4,128)S(1)} async-done(((f32[8,3,512]{2,1,0:T(4,128)}), f32[8,3,512]{2,1,0:T(4,128)S(1)}, u32[]{:S(2)}, u32[]{:S(2)}) %all-to-all-start.2) | async-done | bytes 49184 | tf_op jit(solution)/shard_map/all_to_all | solution.py:33
  156.6 5.3 %broadcast_multiply_fusion = f32[2048,288]{0,1:T(8,128)} fusion(f32[]{:T(128)} %bitcast.19, bf16[512,2048]{0,1:T(8,128)(2,1)S(1)} %bitcast.79, f32[512,288]{0,1:T(8,128)} %get-tuple-element.44, bf16[2048,288]{0,1:T(8,128)(2,1)} %collective-permute-done.7, f32[2048,288]{0,1:T(8,128)} %get-tuple-element.43, f32[]{:T(128)} %bitcast.20, f32[512]{0:T(512)S(1)} %bitcast.94, ...), kind=kOutput, calls=%fused_computation.19 | convolution fusion | flops 608256000 | bytes 8887552 | tf_op jit(solution)/shard_map/dot_general | solution.py:37
  161.8 2.2 %copy.38 = f32[2048,288]{1,0:T(8,128)S(1)} copy(f32[2048,288]{0,1:T(8,128)} %broadcast_multiply_fusion) | data formatting | bytes 4718592 | tf_op jit(solution)/shard_map/mul | solution.py:117
  164.2 1.9 collective-permute-start.12
  166.2 2.3 %collective-permute-done.12 = bf16[8,4,32,288]{3,2,1,0:T(8,128)(2,1)S(1)} collective-permute-done((bf16[8,4,32,288]{3,2,1,0:T(8,128)(2,1)S(1)}, bf16[8,4,32,288]{3,2,1,0:T(8,128)(2,1)S(1)}, u32[]{:S(2)}, u32[]{:S(2)}) %collective-permute-start.12) | collective-permute-done | bytes 589856 | tf_op jit(solution)/shard_map/ppermute | solution.py:24
  168.4 0.4 fusion.6
  168.9 19.4 %all_to_all.25 = bf16[4,8,32,288]{3,2,1,0:T(8,128)(2,1)S(1)} all-to-all(bf16[4,8,32,288]{3,2,1,0:T(8,128)(2,1)S(1)} %copy.39), channel_id=1, replica_groups=mesh['z_lo'=8,'y'=4,'core'=2,'x'=4,'z_hi'=2] {'y'}, dimensions={0} | all-to-all | bytes 1179648 | tf_op jit(solution)/shard_map/all_to_all | solution.py:125
  188.3 0.9 reduce_sum.101
  189.2 4.1 %all-to-all-start.4 = ((bf16[8,32,288]{2,1,0:T(8,128)(2,1)}), bf16[8,32,288]{2,1,0:T(8,128)(2,1)S(1)}, u32[]{:S(2)}, u32[]{:S(2)}) async-start(bf16[8,32,288]{2,1,0:T(8,128)(2,1)} %reduce_sum.101), calls=%async_computation.4 | async-start | bytes 393216 | tf_op jit(solution)/shard_map/all_to_all | solution.py:127
  193.2 1.0 constant_dynamic-slice_fusion
  194.3 12.0 %all-to-all-done.4 = bf16[8,32,288]{2,1,0:T(8,128)(2,1)S(1)} async-done(((bf16[8,32,288]{2,1,0:T(8,128)(2,1)}), bf16[8,32,288]{2,1,0:T(8,128)(2,1)S(1)}, u32[]{:S(2)}, u32[]{:S(2)}) %all-to-all-start.4) | async-done | bytes 147488 | tf_op jit(solution)/shard_map/all_to_all | solution.py:127
  206.4 0.7 multiply_subtract_fusion
  (43 shorter events, 1.9 us)
Async XLA Ops:
  1.8 36.1 %collective-permute-start.1 = (bf16[512,256]{0,1:T(8,128)(2,1)S(1)}, bf16[512,256]{0,1:T(8,128)(2,1)S(1)}, u32[]{:S(2)}, u32[]{:S(2)}) collective-permute-start(bf16[512,256]{0,1:T(8,128)(2,1)S(1)} %bitcast.84), channel_id=1, source_target_pairs={{0,2},{2,4},{4,6},{6,0},{1,3},{3,5},{5,7},{7,1},{8,10},{10,12},{12... | collective-permute-start | bytes 786440 | tf_op jit(solution)/shard_map/ppermute | solution.py:24
  5.3 32.7 %collective-permute-start.2 = (bf16[512,256]{0,1:T(8,128)(2,1)S(1)}, bf16[512,256]{0,1:T(8,128)(2,1)S(1)}, u32[]{:S(2)}, u32[]{:S(2)}) collective-permute-start(bf16[512,256]{0,1:T(8,128)(2,1)S(1)} %bitcast.85), channel_id=1, source_target_pairs={{0,4},{2,6},{4,0},{6,2},{1,5},{3,7},{5,1},{7,3},{8,12},{10,14},{12... | collective-permute-start | bytes 786440 | tf_op jit(solution)/shard_map/ppermute | solution.py:24
  9.9 28.1 %collective-permute-start.3 = (bf16[512,256]{0,1:T(8,128)(2,1)S(1)}, bf16[512,256]{0,1:T(8,128)(2,1)S(1)}, u32[]{:S(2)}, u32[]{:S(2)}) collective-permute-start(bf16[512,256]{0,1:T(8,128)(2,1)S(1)} %bitcast.86), channel_id=1, source_target_pairs={{0,6},{2,0},{4,2},{6,4},{1,7},{3,1},{5,3},{7,5},{8,14},{10,8},{12,... | collective-permute-start | bytes 786440 | tf_op jit(solution)/shard_map/ppermute | solution.py:24
  13.2 37.4 %collective-permute-start = (bf16[512,256]{0,1:T(8,128)(2,1)S(1)}, bf16[512,256]{0,1:T(8,128)(2,1)S(1)}, u32[]{:S(2)}, u32[]{:S(2)}) collective-permute-start(bf16[512,256]{0,1:T(8,128)(2,1)S(1)} %bitcast.87), channel_id=1, source_target_pairs={{0,1},{1,0},{2,3},{3,2},{4,5},{5,4},{6,7},{7,6},{8,9},{9,8},{10,11... | collective-permute-start | bytes 786440 | tf_op jit(solution)/shard_map/ppermute | solution.py:24
  29.4 7.3 %collective-permute-start.4 = (f32[1]{0:T(128)}, f32[1]{0:T(128)}, u32[]{:S(2)}, u32[]{:S(2)}) collective-permute-start(f32[1]{0:T(128)} %bitcast.5), channel_id=1, source_target_pairs={{0,8},{8,16},{16,24},{24,32},{32,40},{40,48},{48,56},{56,64},{64,7... | collective-permute-start | bytes 20 | tf_op jit(solution)/shard_map/ppermute | solution.py:24
  51.7 21.2 %all-to-all-start = ((bf16[4,512,256]{1,2,0:T(8,128)(2,1)}), bf16[4,512,256]{1,2,0:T(8,128)(2,1)S(1)}, u32[]{:S(2)}, u32[]{:S(2)}) async-start(bf16[4,512,256]{1,2,0:T(8,128)(2,1)} %broadcast_in_dim.6), calls=%async_computation | async-start | bytes 2097152 | tf_op jit(solution)/shard_map/all_to_all | solution.py:33
  56.0 16.9 %collective-permute-start.5 = (f32[1]{0:T(128)}, f32[1]{0:T(128)}, u32[]{:S(2)}, u32[]{:S(2)}) collective-permute-start(f32[1]{0:T(128)} %mul.139), channel_id=1, source_target_pairs={{0,16},{8,24},{16,32},{24,40},{32,48},{40,56},{48,64},{56,72},{64,... | collective-permute-start | bytes 20 | tf_op jit(solution)/shard_map/ppermute | solution.py:24
  60.8 28.2 %collective-permute-start.8 = (bf16[512,256]{0,1:T(8,128)(2,1)S(1)}, bf16[512,256]{0,1:T(8,128)(2,1)S(1)}, u32[]{:S(2)}, u32[]{:S(2)}) collective-permute-start(bf16[512,256]{0,1:T(8,128)(2,1)S(1)} %bitcast.83), channel_id=1, source_target_pairs={{0,1},{1,0},{2,3},{3,2},{4,5},{5,4},{6,7},{7,6},{8,9},{9,8},{10,11... | collective-permute-start | bytes 786440 | tf_op jit(solution)/shard_map/ppermute | solution.py:24
  73.1 1.3 copy-start.1
  73.1 1.3 copy-start.3
  73.1 1.4 copy-start.4
  73.1 1.6 copy-start.6
  77.1 24.0 %all-to-all-start.1 = ((f32[8,3,512]{2,1,0:T(4,128)}), f32[8,3,512]{2,1,0:T(4,128)S(1)}, u32[]{:S(2)}, u32[]{:S(2)}) async-start(f32[8,3,512]{2,1,0:T(4,128)} %broadcast_in_dim.7), calls=%async_computation.1 | async-start | bytes 131072 | tf_op jit(solution)/shard_map/all_to_all | solution.py:33
  89.0 17.9 %collective-permute-start.9 = (bf16[2,512,256]{1,2,0:T(8,128)(2,1)S(1)}, bf16[2,512,256]{1,2,0:T(8,128)(2,1)S(1)}, u32[]{:S(2)}, u32[]{:S(2)}) collective-permute-start(bf16[2,512,256]{1,2,0:T(8,128)(2,1)S(1)} %pad_maximum_fusion.4), channel_id=1, source_target_pairs={{0,2},{2,4},{4,6},{6,0},{1,3},{3,5},{5,7},{7,1},{8,10},{10,12},{12... | collective-permute-start | bytes 1572872 | tf_op jit(solution)/shard_map/ppermute | solution.py:24
  92.3 22.0 %collective-permute-start.10 = (bf16[2,512,256]{1,2,0:T(8,128)(2,1)S(1)}, bf16[2,512,256]{1,2,0:T(8,128)(2,1)}, u32[]{:S(2)}, u32[]{:S(2)}) collective-permute-start(bf16[2,512,256]{1,2,0:T(8,128)(2,1)S(1)} %pad_maximum_fusion.4), channel_id=1, source_target_pairs={{0,4},{2,6},{4,0},{6,2},{1,5},{3,7},{5,1},{7,3},{8,12},{10,14},{12... | collective-permute-start | bytes 1572872 | tf_op jit(solution)/shard_map/ppermute | solution.py:24
  96.9 18.7 %collective-permute-start.11 = (bf16[2,512,256]{1,2,0:T(8,128)(2,1)S(1)}, bf16[2,512,256]{1,2,0:T(8,128)(2,1)}, u32[]{:S(2)}, u32[]{:S(2)}) collective-permute-start(bf16[2,512,256]{1,2,0:T(8,128)(2,1)S(1)} %pad_maximum_fusion.4), channel_id=1, source_target_pairs={{0,6},{2,0},{4,2},{6,4},{1,7},{3,1},{5,3},{7,5},{8,14},{10,8},{12,... | collective-permute-start | bytes 1572872 | tf_op jit(solution)/shard_map/ppermute | solution.py:24
  105.0 22.4 %collective-permute-start.7 = (bf16[2048,288]{0,1:T(8,128)(2,1)}, bf16[2048,288]{0,1:T(8,128)(2,1)}, u32[]{:S(2)}, u32[]{:S(2)}) collective-permute-start(bf16[2048,288]{0,1:T(8,128)(2,1)} %get-tuple-element.42), channel_id=1, source_target_pairs={{0,8},{8,16},{16,24},{24,32},{32,40},{40,48},{48,56},{56,64},{64,7... | collective-permute-start | bytes 3538952 | tf_op jit(solution)/shard_map/ppermute | solution.py:24
  121.0 6.4 %copy-start.8 = (f32[2048,288]{0,1:T(8,128)S(1)}, f32[2048,288]{0,1:T(8,128)}, u32[]{:S(2)}) copy-start(f32[2048,288]{0,1:T(8,128)} %get-tuple-element.43) | copy-start | bytes 7077892
  121.2 6.2 %copy-start.2 = (bf16[2048,288]{0,1:T(8,128)(2,1)S(1)}, bf16[2048,288]{0,1:T(8,128)(2,1)}, u32[]{:S(2)}) copy-start(bf16[2048,288]{0,1:T(8,128)(2,1)} %param.11) | copy-start | bytes 3538948
  121.2 6.2 %copy-start.5 = (bf16[2,512,288]{1,2,0:T(8,128)(2,1)S(1)}, bf16[2,512,288]{1,2,0:T(8,128)(2,1)}, u32[]{:S(2)}) copy-start(bf16[2,512,288]{1,2,0:T(8,128)(2,1)} %param.8) | copy-start | bytes 1769476
  121.2 6.2 %copy-start.7 = (bf16[2,512,288]{1,2,0:T(8,128)(2,1)S(1)}, bf16[2,512,288]{1,2,0:T(8,128)(2,1)}, u32[]{:S(2)}) copy-start(bf16[2,512,288]{1,2,0:T(8,128)(2,1)} %param.9) | copy-start | bytes 1769476
  131.7 24.8 %all-to-all-start.2 = ((f32[8,3,512]{2,1,0:T(4,128)}), f32[8,3,512]{2,1,0:T(4,128)S(1)}, u32[]{:S(2)}, u32[]{:S(2)}) async-start(f32[8,3,512]{2,1,0:T(4,128)} %broadcast_in_dim.8), calls=%async_computation.2 | async-start | bytes 131072 | tf_op jit(solution)/shard_map/all_to_all | solution.py:33
  143.4 7.7 %collective-permute-start.6 = (f32[1]{0:T(128)}, f32[1]{0:T(128)}, u32[]{:S(2)}, u32[]{:S(2)}) collective-permute-start(f32[1]{0:T(128)} %add.68), channel_id=1, source_target_pairs={{0,496},{8,504},{16,0},{24,8},{32,16},{40,24},{48,32},{56,40},{64,... | collective-permute-start | bytes 20 | tf_op jit(solution)/shard_map/ppermute | solution.py:24
  164.2 4.2 %collective-permute-start.12 = (bf16[8,4,32,288]{3,2,1,0:T(8,128)(2,1)S(1)}, bf16[8,4,32,288]{3,2,1,0:T(8,128)(2,1)S(1)}, u32[]{:S(2)}, u32[]{:S(2)}) collective-permute-start(bf16[8,4,32,288]{3,2,1,0:T(8,128)(2,1)S(1)} %fusion.5), channel_id=1, source_target_pairs={{0,8},{8,0},{1,9},{9,1},{2,10},{10,2},{3,11},{11,3},{4,12},{12,4},... | collective-permute-start | bytes 1769480 | tf_op jit(solution)/shard_map/ppermute | solution.py:24
  168.9 37.4 %copy-start = (f32[32,288]{1,0:T(8,128)S(1)}, f32[32,288]{1,0:T(8,128)}, u32[]{:S(2)}) copy-start(f32[32,288]{1,0:T(8,128)} %param.12) | copy-start | bytes 110596
  189.2 17.1 %all-to-all-start.4 = ((bf16[8,32,288]{2,1,0:T(8,128)(2,1)}), bf16[8,32,288]{2,1,0:T(8,128)(2,1)S(1)}, u32[]{:S(2)}, u32[]{:S(2)}) async-start(bf16[8,32,288]{2,1,0:T(8,128)(2,1)} %reduce_sum.101), calls=%async_computation.4 | async-start | bytes 393216 | tf_op jit(solution)/shard_map/all_to_all | solution.py:127

commit v5 on v4

--- a/solution.py
+++ b/solution.py
@@ -44,8 +44,12 @@
     return jnp.transpose(both, (2, 0, 1, 3)).reshape(TOK, 2048)
 
 
-def from_others(value, x):
-    blocks = jnp.stack([value] + [shifted(value, "x", k) for k in (1, 2, 3)])
+def along_x(value):
+    return [value] + [shifted(value, "x", k) for k in (1, 2, 3)]
+
+
+def in_order(blocks, x):
+    blocks = jnp.stack(blocks)
     twice = jnp.concatenate([blocks[::-1], blocks[::-1]])
     return lax.dynamic_slice_in_dim(twice, 3 - x, 4, 0)
 
@@ -55,6 +59,18 @@
     high = jnp.where(hi == 0, other, own)
     both = jnp.stack([low, high], axis=1)
     return jnp.transpose(both, (2, 0, 1, 3)).reshape(TOK, 2048)
+
+
+def mass_neighbours(shares, before):
+    near = {k: shifted(shares, REP, -k) for k in (-3, -2, 1, 2)}
+    return {**near, -1: before, 0: shares}
+
+
+def masses(near):
+    mass1 = {k: near[k][0] + (1.0 - near[k - 1][0]) for k in (-2, 0, 2)}
+    mass2 = {k: near[k][1] * mass1[k] + (1.0 - near[k - 2][1]) * mass1[k - 2] for k in (0, 2)}
+    own = near[0][1]
+    return mass2[0], (own / mass2[0] + (1.0 - own) / mass2[2]) / lax.axis_size(REP)
 
 
 def forward(gathered, quotient, residual, targets, gain):
@@ -84,43 +100,43 @@
     anchor = slow_weight.astype(F32)
 
     other0 = shifted(context[0], "z_hi", 1)
-    before0 = shifted(shares[0], REP, 1)
-    own0 = from_others(context[0], x)
-    mass1 = shares[0] + (1.0 - before0)
-    other0, own0, mass1 = lax.optimization_barrier((other0, own0, mass1))
+    own0 = along_x(context[0])
+    before = shifted(shares[:, 0], REP, 1)
+    other0, own0, before = lax.optimization_barrier((other0, own0, before))
     wide0 = to_all(other0, "x")
+    own0 = in_order(own0, x)
     context1 = after(context[1], other0)
     other1 = shifted(context1, "z_hi", 1)
-    mass_in = shifted((1.0 - shares[1]) * mass1, REP, 2)
-    own0, wide0, mass_in = lax.optimization_barrier((own0, wide0, mass_in))
     gathered0 = merged(own0, wide0, hi)
-    mass2 = shares[1] * mass1 + mass_in
     share0 = shares[0, 0]
 
     output0, sums0 = forward(gathered0, slow_weight, residual[0], targets[0], gain)
     totals0 = jnp.sum(to_all(sums0, TP), axis=0)
     pair1 = jnp.stack([context1, other1])
-    both1 = from_others(after(pair1, sums0), x)
+    both1 = in_order(along_x(after(pair1, sums0)), x)
     gathered1 = ordered(both1, hi)
     grad0 = backward(output0, totals0, targets[0], gain)
     weight_grad0 = contract_rows(gathered0, grad0)
 
-    incoming = shifted(((1.0 - share0) * weight_grad0).astype(BF16), REP, 1)
-    mass_later = shifted(after(mass2, weight_grad0), REP, -2)
+    pushed = ((1.0 - share0) * weight_grad0).astype(BF16)
+    incoming = shifted(pushed, REP, 1)
+    mass1 = share0 + (1.0 - before[0])
     step0 = share0 * weight_grad0 + incoming.astype(F32)
-    quotient1 = (anchor - (LR / mass1[0]) * step0).astype(BF16)
+    quotient1 = (anchor - (LR / mass1) * step0).astype(BF16)
     output1, sums1 = forward(gathered1, quotient1, residual[1], targets[1], gain)
+    near = mass_neighbours(shares[:, 0], before)
+    near = lax.optimization_barrier((near, sums1))[0]
+    mass2, part = masses(near)
     totals1 = jnp.sum(to_all(sums1, TP), axis=0)
     grad1 = backward(output1, totals1, targets[1], gain)
     weight_grad1 = contract_rows(gathered1, grad1)
-    part = (shares[1] / mass2 + (1.0 - shares[1]) / mass_later) / lax.axis_size(REP)
-    total = part[0] * (step0 + weight_grad1)
+    total = (part * (step0 + weight_grad1)).astype(BF16)
 
     width = total.shape[1]
     total = total.reshape(8, 4, 2, 32, width)
     kept = jnp.where(core == 0, total[:, :, 0], total[:, :, 1])
-    sent = jnp.where(core == 0, total[:, :, 1], total[:, :, 0]).astype(BF16)
-    total = kept + shifted(sent, "core", 1).astype(F32)
+    sent = jnp.where(core == 0, total[:, :, 1], total[:, :, 0])
+    total = kept.astype(F32) + shifted(sent, "core", 1).astype(F32)
     parts = jnp.transpose(total.astype(BF16), (1, 0, 2, 3))
     parts = lax.all_to_all(parts, "y", 0, 0)
     total = jnp.sum(parts.astype(F32), axis=0)
@@ -130,7 +146,7 @@
     anchor_rows = lax.dynamic_slice_in_dim(slow_weight, lax.axis_index(REP) * 32, 32, 0)
     new_momentum = BETA * momentum + gradient
     new_weight = anchor_rows.astype(F32) - ALPHA * LR * new_momentum
-    return (new_weight, new_momentum, mass2)
+    return (new_weight, new_momentum, mass2[None])
 
 
 def solution(mesh):

time: 209 us -> 198 us (0.947)
  waiting for transfers between devices: 54.2 us -> 40.5 us
  starting transfers between devices: 93.9 us -> 99.8 us
  matrix products: 14.5 us -> 11.8 us
    ppermute x13 -> x15, waiting for transfers between devices: 36.7 us -> 17.6 us  [shifted(): lax.ppermute(value, axis, [(i, (i + steps) % count) for i in range(count)])]
    all_to_all x3, waiting for transfers between devices: 5.57 us -> 10.9 us  [to_all(): lax.all_to_all(jnp.broadcast_to(value[None], (count,) + value.shape), axi...]
    all_to_all x3, starting transfers between devices: 22.1 us -> 25.6 us  [to_all(): lax.all_to_all(jnp.broadcast_to(value[None], (count,) + value.shape), axi...]
    all_to_all x1, starting transfers between devices: 4.05 us -> 6.73 us  [body(): parts = lax.all_to_all(total.astype(BF16), 'z_lo', 0, 0)]
    mul x1 -> x0, local copies, waits for them, and re-layouts: 2.24 us -> none  [body(): total = part[0] * (step0 + weight_grad1)]
    dot_general x2, matrix products: 9.13 us -> 7.02 us  [contract_rows(): lax.dot_general(left, right, (((0,), (0,)), ((), ())), preferred_element_...]
    ppermute x13 -> x15, starting transfers between devices: 67.7 us -> 67.5 us  [shifted(): lax.ppermute(value, axis, [(i, (i + steps) % count) for i in range(count)])]
  transfers between devices with their start and end apart: 17 -> 19, of which waited for: 10 -> 9; matrix products, arithmetic and copies ran while one was open for 7% -> 10% of each run, Pallas kernels for 0% -> 0%
where the time goes in v5:
time: 198 us; the launch traced here: 197 us
  starting transfers between devices  99.8 us (50%)
  waiting for transfers between devices  40.5 us (20%)
  blocking collectives  17.4 us (9%)
  local copies, waits for them, and re-layouts  11.8 us (6%)
  matrix products  11.8 us (6%)
  other arithmetic  7.96 us (4%)
  between operations  7.59 us (4%)
    ppermute x15, starting transfers between devices, shifted(): lax.ppermute(value, axis, [(i, (i + steps) % count) for i in range(count)])  67.5 us
    all_to_all x3, starting transfers between devices, to_all(): lax.all_to_all(jnp.broadcast_to(value[None], (count,) + value.shape), axi...  25.6 us
    ppermute x15, waiting for transfers between devices, shifted(): lax.ppermute(value, axis, [(i, (i + steps) % count) for i in range(count)])  17.6 us
    all_to_all x1, blocking collectives, body(): parts = lax.all_to_all(parts, 'y', 0, 0)  17.4 us
    all_to_all x1, waiting for transfers between devices, body(): parts = lax.all_to_all(total.astype(BF16), 'z_lo', 0, 0)  12 us
    all_to_all x3, waiting for transfers between devices, to_all(): lax.all_to_all(jnp.broadcast_to(value[None], (count,) + value.shape), axi...  10.9 us
    dot_general x2, matrix products, contract_rows(): lax.dot_general(left, right, (((0,), (0,)), ((), ())), preferred_element_...  7.02 us
    all_to_all x1, starting transfers between devices, body(): parts = lax.all_to_all(total.astype(BF16), 'z_lo', 0, 0)  6.73 us
  transfers between devices with their start and end apart: 19, of which 9 were waited for; matrix products, arithmetic and copies ran while one was open for 10% of the time, Pallas kernels for 0%

profile of v5, /device:TPU:32, one launch (start us, length us, event | category | flops | bytes accessed | tf_op | source)
XLA Modules:
  0.0 196.9 jit_solution(15618883355930959579)
XLA Ops:
  0.6 1.1 fusion.41
  1.8 14.8 %collective-permute-start.2 = (bf16[512,256]{0,1:T(8,128)(2,1)S(1)}, bf16[512,256]{0,1:T(8,128)(2,1)S(1)}, u32[]{:S(2)}, u32[]{:S(2)}) collective-permute-start(bf16[512,256]{0,1:T(8,128)(2,1)S(1)} %bitcast.90), channel_id=1, source_target_pairs={{0,1},{1,0},{2,3},{3,2},{4,5},{5,4},{6,7},{7,6},{8,9},{9,8},{10,11... | collective-permute-start | bytes 786440 | tf_op jit(solution)/shard_map/ppermute | solution.py:24
  16.7 3.4 %collective-permute-start.3 = (bf16[512,256]{0,1:T(8,128)(2,1)S(1)}, bf16[512,256]{0,1:T(8,128)(2,1)S(1)}, u32[]{:S(2)}, u32[]{:S(2)}) collective-permute-start(bf16[512,256]{0,1:T(8,128)(2,1)S(1)} %bitcast.91), channel_id=1, source_target_pairs={{0,2},{2,4},{4,6},{6,0},{1,3},{3,5},{5,7},{7,1},{8,10},{10,12},{12... | collective-permute-start | bytes 786440 | tf_op jit(solution)/shard_map/ppermute | solution.py:24
  20.1 4.6 %collective-permute-start.4 = (bf16[512,256]{0,1:T(8,128)(2,1)S(1)}, bf16[512,256]{0,1:T(8,128)(2,1)S(1)}, u32[]{:S(2)}, u32[]{:S(2)}) collective-permute-start(bf16[512,256]{0,1:T(8,128)(2,1)S(1)} %bitcast.92), channel_id=1, source_target_pairs={{0,4},{2,6},{4,0},{6,2},{1,5},{3,7},{5,1},{7,3},{8,12},{10,14},{12... | collective-permute-start | bytes 786440 | tf_op jit(solution)/shard_map/ppermute | solution.py:24
  24.7 3.3 %collective-permute-start.5 = (bf16[512,256]{0,1:T(8,128)(2,1)S(1)}, bf16[512,256]{0,1:T(8,128)(2,1)S(1)}, u32[]{:S(2)}, u32[]{:S(2)}) collective-permute-start(bf16[512,256]{0,1:T(8,128)(2,1)S(1)} %bitcast.93), channel_id=1, source_target_pairs={{0,6},{2,0},{4,2},{6,4},{1,7},{3,1},{5,3},{7,5},{8,14},{10,8},{12,... | collective-permute-start | bytes 786440 | tf_op jit(solution)/shard_map/ppermute | solution.py:24
  28.1 1.9 collective-permute-start.6
  30.0 5.2 %collective-permute-done.6 = f32[2]{0:T(128)S(1)} collective-permute-done((f32[2]{0:T(128)}, f32[2]{0:T(128)S(1)}, u32[]{:S(2)}, u32[]{:S(2)}) %collective-permute-start.6) | collective-permute-done | bytes 40 | tf_op jit(solution)/shard_map/ppermute | solution.py:24
  35.2 4.8 %collective-permute-done.2 = bf16[512,256]{0,1:T(8,128)(2,1)S(1)} collective-permute-done((bf16[512,256]{0,1:T(8,128)(2,1)S(1)}, bf16[512,256]{0,1:T(8,128)(2,1)S(1)}, u32[]{:S(2)}, u32[]{:S(2)}) %collective-permute-start.2) | collective-permute-done | bytes 262176 | tf_op jit(solution)/shard_map/ppermute | solution.py:24
  40.1 1.1 broadcast_in_dim.8
  41.1 4.3 %all-to-all-start = ((bf16[4,512,256]{1,2,0:T(8,128)(2,1)}), bf16[4,512,256]{1,2,0:T(8,128)(2,1)S(1)}, u32[]{:S(2)}, u32[]{:S(2)}) async-start(bf16[4,512,256]{1,2,0:T(8,128)(2,1)} %broadcast_in_dim.8), calls=%async_computation | async-start | bytes 2097152 | tf_op jit(solution)/shard_map/all_to_all | solution.py:33
  45.6 1.1 pad_maximum_fusion.3
  46.8 12.1 %collective-permute-start.9 = (bf16[512,256]{0,1:T(8,128)(2,1)S(1)}, bf16[512,256]{0,1:T(8,128)(2,1)S(1)}, u32[]{:S(2)}, u32[]{:S(2)}) collective-permute-start(bf16[512,256]{0,1:T(8,128)(2,1)S(1)} %bitcast.89), channel_id=1, source_target_pairs={{0,1},{1,0},{2,3},{3,2},{4,5},{5,4},{6,7},{7,6},{8,9},{9,8},{10,11... | collective-permute-start | bytes 786440 | tf_op jit(solution)/shard_map/ppermute | solution.py:24
  58.9 0.9 all-to-all-done
  60.5 1.0 copy-done.2
  61.9 1.7 multiply_reduce_fusion.2
  63.6 0.6 broadcast_in_dim.9
  64.2 12.1 %all-to-all-start.1 = ((f32[8,3,512]{2,1,0:T(4,128)}), f32[8,3,512]{2,1,0:T(4,128)S(1)}, u32[]{:S(2)}, u32[]{:S(2)}) async-start(f32[8,3,512]{2,1,0:T(4,128)} %broadcast_in_dim.9), calls=%async_computation.1 | async-start | bytes 131072 | tf_op jit(solution)/shard_map/all_to_all | solution.py:33
  76.3 2.3 %collective-permute-done.9 = bf16[512,256]{0,1:T(8,128)(2,1)S(1)} collective-permute-done((bf16[512,256]{0,1:T(8,128)(2,1)S(1)}, bf16[512,256]{0,1:T(8,128)(2,1)S(1)}, u32[]{:S(2)}, u32[]{:S(2)}) %collective-permute-start.9) | collective-permute-done | bytes 262176 | tf_op jit(solution)/shard_map/ppermute | solution.py:24
  78.7 4.4 %collective-permute-start.10 = (bf16[2,512,256]{1,2,0:T(8,128)(2,1)S(1)}, bf16[2,512,256]{1,2,0:T(8,128)(2,1)S(1)}, u32[]{:S(2)}, u32[]{:S(2)}) collective-permute-start(bf16[2,512,256]{1,2,0:T(8,128)(2,1)S(1)} %pad_maximum_fusion.4), channel_id=1, source_target_pairs={{0,2},{2,4},{4,6},{6,0},{1,3},{3,5},{5,7},{7,1},{8,10},{10,12},{12... | collective-permute-start | bytes 1572872 | tf_op jit(solution)/shard_map/ppermute | solution.py:24
  83.1 3.8 %collective-permute-start.11 = (bf16[2,512,256]{1,2,0:T(8,128)(2,1)S(1)}, bf16[2,512,256]{1,2,0:T(8,128)(2,1)}, u32[]{:S(2)}, u32[]{:S(2)}) collective-permute-start(bf16[2,512,256]{1,2,0:T(8,128)(2,1)S(1)} %pad_maximum_fusion.4), channel_id=1, source_target_pairs={{0,4},{2,6},{4,0},{6,2},{1,5},{3,7},{5,1},{7,3},{8,12},{10,14},{12... | collective-permute-start | bytes 1572872 | tf_op jit(solution)/shard_map/ppermute | solution.py:24
  86.9 3.4 %collective-permute-start.12 = (bf16[2,512,256]{1,2,0:T(8,128)(2,1)S(1)}, bf16[2,512,256]{1,2,0:T(8,128)(2,1)}, u32[]{:S(2)}, u32[]{:S(2)}) collective-permute-start(bf16[2,512,256]{1,2,0:T(8,128)(2,1)S(1)} %pad_maximum_fusion.4), channel_id=1, source_target_pairs={{0,6},{2,0},{4,2},{6,4},{1,7},{3,1},{5,3},{7,5},{8,14},{10,8},{12,... | collective-permute-start | bytes 1572872 | tf_op jit(solution)/shard_map/ppermute | solution.py:24
  90.3 1.1 all-to-all-done.1
  91.5 3.8 %multiply_convert_fusion = (bf16[2048,288]{0,1:T(8,128)(2,1)}, f32[2048,288]{0,1:T(8,128)}) fusion(f32[]{:T(128)S(6)} %sub.71, bf16[512,2048]{0,1:T(8,128)(2,1)S(1)} %bitcast.87, f32[512,288]{0,1:T(8,128)} %get-tuple-element.55, f32[512]{0:T(512)S(1)} %bitcast.102, f32[512]{0:T(512)S(1)} %bitcast.101, f32[288]{0:T(512)S(1)} %broadcast_multiply_fusion, ...), kind=kOutput, calls=%fused_computation.7 | convolution fusion | flops 606486528 | bytes 6527236 | tf_op jit(solution)/shard_map/dot_general | solution.py:37
  95.3 1.9 collective-permute-start.13
  97.2 4.8 %collective-permute-start = (f32[2]{0:T(128)S(1)}, f32[2]{0:T(128)S(1)}, u32[]{:S(2)}, u32[]{:S(2)}) collective-permute-start(f32[2]{0:T(128)S(1)} %bitcast.111), channel_id=1, source_target_pairs={{0,24},{8,32},{16,40},{24,48},{32,56},{40,64},{48,72},{56,80},{64,... | collective-permute-start | bytes 32 | tf_op jit(solution)/shard_map/ppermute | solution.py:24
  102.1 3.2 %collective-permute-start.1 = (f32[2]{0:T(128)S(1)}, f32[2]{0:T(128)S(1)}, u32[]{:S(2)}, u32[]{:S(2)}) collective-permute-start(f32[2]{0:T(128)S(1)} %bitcast.113), channel_id=1, source_target_pairs={{0,16},{8,24},{16,32},{24,40},{32,48},{40,56},{48,64},{56,72},{64,... | collective-permute-start | bytes 32 | tf_op jit(solution)/shard_map/ppermute | solution.py:24
  105.3 3.0 %collective-permute-done.11 = bf16[2,512,256]{1,2,0:T(8,128)(2,1)} collective-permute-done((bf16[2,512,256]{1,2,0:T(8,128)(2,1)S(1)}, bf16[2,512,256]{1,2,0:T(8,128)(2,1)}, u32[]{:S(2)}, u32[]{:S(2)}) %collective-permute-start.11) | collective-permute-done | bytes 524320 | tf_op jit(solution)/shard_map/ppermute | solution.py:24
  108.3 1.9 collective-permute-start.7
  110.2 1.9 collective-permute-start.8
  112.2 1.5 pad_maximum_fusion.1
  113.6 1.5 rev.9
  115.2 2.3 %fusion.2 = bf16[4,2,512,256]{2,3,1,0:T(8,128)(2,1)S(1)} fusion(s32[]{:T(128)S(6)} %select_n.51, bf16[4,2,512,256]{2,3,1,0:T(8,128)(2,1)} %rev.9), kind=kLoop, calls=%fused_computation.8 | loop fusion | flops 1048576 | bytes 4194308 | tf_op jit(solution)/shard_map/concatenate | solution.py:53
  117.9 1.3 copy-done.10
  119.9 3.1 %multiply_reduce_fusion = (f32[512]{0:T(512)S(1)}, f32[512]{0:T(512)S(1)}, f32[512]{0:T(512)S(1)}, f32[512,288]{0,1:T(8,128)}) fusion(f32[288]{0:T(512)S(1)} %copy-done.4, bf16[2,512,288]{1,2,0:T(8,128)(2,1)S(1)} %copy-done.9, bf16[512,2048]{0,1:T(8,128)(2,1)S(1)} %bitcast.84, bf16[2048,288]{0,1:T(8,128)(2,1)S(1)} %copy-done.3, ...), kind=kOutput, calls=%fused_computation.40 | convolution fusion | flops 609581568 | bytes 8002696 | tf_op jit(solution)/shard_map/dot_general | solution.py:77
  123.0 0.6 broadcast_in_dim.10
  123.6 9.2 %all-to-all-start.2 = ((f32[8,3,512]{2,1,0:T(4,128)}), f32[8,3,512]{2,1,0:T(4,128)S(1)}, u32[]{:S(2)}, u32[]{:S(2)}) async-start(f32[8,3,512]{2,1,0:T(4,128)} %broadcast_in_dim.10), calls=%async_computation.2 | async-start | bytes 131072 | tf_op jit(solution)/shard_map/all_to_all | solution.py:33
  135.5 0.6 fusion.42
  139.3 8.9 %all-to-all-done.2 = f32[8,3,512]{2,1,0:T(4,128)S(1)} async-done(((f32[8,3,512]{2,1,0:T(4,128)}), f32[8,3,512]{2,1,0:T(4,128)S(1)}, u32[]{:S(2)}, u32[]{:S(2)}) %all-to-all-start.2) | async-done | bytes 49184 | tf_op jit(solution)/shard_map/all_to_all | solution.py:33
  148.2 3.2 %fusion.1 = bf16[2048,288]{0,1:T(8,128)(2,1)S(1)} fusion(bf16[512,2048]{0,1:T(8,128)(2,1)S(1)} %bitcast.85, bf16[2048,288]{0,1:T(8,128)(2,1)} %collective-permute-done.13, f32[2048,288]{0,1:T(8,128)} %get-tuple-element.57, f32[]{:T(128)S(6)} %div.99, f32[]{:T(128)S(1)} %bitcast.118, f32[512,288]{0,1:T(8,128)} %get-tuple-element.58, f32[512]{0:T(512)S(1)} %bitcast.100, ...), kind=kOutput, calls=%fused_computation.4 | convolution fusion | flops 608845824 | bytes 7706888 | tf_op jit(solution)/shard_map/dot_general | solution.py:37
  151.4 0.8 copy.38
  152.4 1.9 collective-permute-start.14
  154.3 2.3 %collective-permute-done.14 = bf16[8,4,32,288]{3,2,1,0:T(8,128)(2,1)S(1)} collective-permute-done((bf16[8,4,32,288]{3,2,1,0:T(8,128)(2,1)S(1)}, bf16[8,4,32,288]{3,2,1,0:T(8,128)(2,1)S(1)}, u32[]{:S(2)}, u32[]{:S(2)}) %collective-permute-start.14) | collective-permute-done | bytes 589856 | tf_op jit(solution)/shard_map/ppermute | solution.py:24
  157.0 17.4 %all_to_all.25 = bf16[4,8,32,288]{3,2,1,0:T(8,128)(2,1)S(1)} all-to-all(bf16[4,8,32,288]{3,2,1,0:T(8,128)(2,1)S(1)} %copy.39), channel_id=1, replica_groups=mesh['z_lo'=8,'y'=4,'core'=2,'x'=4,'z_hi'=2] {'y'}, dimensions={0} | all-to-all | bytes 1179648 | tf_op jit(solution)/shard_map/all_to_all | solution.py:141
  174.4 0.9 reduce_sum.101
  175.2 6.7 %all-to-all-start.4 = ((bf16[8,32,288]{2,1,0:T(8,128)(2,1)}), bf16[8,32,288]{2,1,0:T(8,128)(2,1)S(1)}, u32[]{:S(2)}, u32[]{:S(2)}) async-start(bf16[8,32,288]{2,1,0:T(8,128)(2,1)} %reduce_sum.101), calls=%async_computation.4 | async-start | bytes 393216 | tf_op jit(solution)/shard_map/all_to_all | solution.py:143
  182.0 1.0 constant_dynamic-slice_fusion
  183.0 12.0 %all-to-all-done.4 = bf16[8,32,288]{2,1,0:T(8,128)(2,1)S(1)} async-done(((bf16[8,32,288]{2,1,0:T(8,128)(2,1)}), bf16[8,32,288]{2,1,0:T(8,128)(2,1)S(1)}, u32[]{:S(2)}, u32[]{:S(2)}) %all-to-all-start.4) | async-done | bytes 147488 | tf_op jit(solution)/shard_map/all_to_all | solution.py:143
  195.1 0.7 multiply_subtract_fusion
  (51 shorter events, 3.8 us)
Async XLA Ops:
  1.8 38.2 %collective-permute-start.2 = (bf16[512,256]{0,1:T(8,128)(2,1)S(1)}, bf16[512,256]{0,1:T(8,128)(2,1)S(1)}, u32[]{:S(2)}, u32[]{:S(2)}) collective-permute-start(bf16[512,256]{0,1:T(8,128)(2,1)S(1)} %bitcast.90), channel_id=1, source_target_pairs={{0,1},{1,0},{2,3},{3,2},{4,5},{5,4},{6,7},{7,6},{8,9},{9,8},{10,11... | collective-permute-start | bytes 786440 | tf_op jit(solution)/shard_map/ppermute | solution.py:24
  16.7 23.4 %collective-permute-start.3 = (bf16[512,256]{0,1:T(8,128)(2,1)S(1)}, bf16[512,256]{0,1:T(8,128)(2,1)S(1)}, u32[]{:S(2)}, u32[]{:S(2)}) collective-permute-start(bf16[512,256]{0,1:T(8,128)(2,1)S(1)} %bitcast.91), channel_id=1, source_target_pairs={{0,2},{2,4},{4,6},{6,0},{1,3},{3,5},{5,7},{7,1},{8,10},{10,12},{12... | collective-permute-start | bytes 786440 | tf_op jit(solution)/shard_map/ppermute | solution.py:24
  20.1 20.0 %collective-permute-start.4 = (bf16[512,256]{0,1:T(8,128)(2,1)S(1)}, bf16[512,256]{0,1:T(8,128)(2,1)S(1)}, u32[]{:S(2)}, u32[]{:S(2)}) collective-permute-start(bf16[512,256]{0,1:T(8,128)(2,1)S(1)} %bitcast.92), channel_id=1, source_target_pairs={{0,4},{2,6},{4,0},{6,2},{1,5},{3,7},{5,1},{7,3},{8,12},{10,14},{12... | collective-permute-start | bytes 786440 | tf_op jit(solution)/shard_map/ppermute | solution.py:24
  24.7 15.3 %collective-permute-start.5 = (bf16[512,256]{0,1:T(8,128)(2,1)S(1)}, bf16[512,256]{0,1:T(8,128)(2,1)S(1)}, u32[]{:S(2)}, u32[]{:S(2)}) collective-permute-start(bf16[512,256]{0,1:T(8,128)(2,1)S(1)} %bitcast.93), channel_id=1, source_target_pairs={{0,6},{2,0},{4,2},{6,4},{1,7},{3,1},{5,3},{7,5},{8,14},{10,8},{12,... | collective-permute-start | bytes 786440 | tf_op jit(solution)/shard_map/ppermute | solution.py:24
  28.1 7.2 %collective-permute-start.6 = (f32[2]{0:T(128)}, f32[2]{0:T(128)S(1)}, u32[]{:S(2)}, u32[]{:S(2)}) collective-permute-start(f32[2]{0:T(128)} %bitcast.109), channel_id=1, source_target_pairs={{0,8},{8,16},{16,24},{24,32},{32,40},{40,48},{48,56},{56,64},{64,7... | collective-permute-start | bytes 32 | tf_op jit(solution)/shard_map/ppermute | solution.py:24
  40.1 5.5 %copy-start = (bf16[512,256]{0,1:T(8,128)(2,1)}, bf16[512,256]{0,1:T(8,128)(2,1)S(1)}, u32[]{:S(2)}) copy-start(bf16[512,256]{0,1:T(8,128)(2,1)S(1)} %collective-permute-done.5) | copy-start | bytes 786436
  41.1 18.6 %all-to-all-start = ((bf16[4,512,256]{1,2,0:T(8,128)(2,1)}), bf16[4,512,256]{1,2,0:T(8,128)(2,1)S(1)}, u32[]{:S(2)}, u32[]{:S(2)}) async-start(bf16[4,512,256]{1,2,0:T(8,128)(2,1)} %broadcast_in_dim.8), calls=%async_computation | async-start | bytes 2097152 | tf_op jit(solution)/shard_map/all_to_all | solution.py:33
  46.8 31.9 %collective-permute-start.9 = (bf16[512,256]{0,1:T(8,128)(2,1)S(1)}, bf16[512,256]{0,1:T(8,128)(2,1)S(1)}, u32[]{:S(2)}, u32[]{:S(2)}) collective-permute-start(bf16[512,256]{0,1:T(8,128)(2,1)S(1)} %bitcast.89), channel_id=1, source_target_pairs={{0,1},{1,0},{2,3},{3,2},{4,5},{5,4},{6,7},{7,6},{8,9},{9,8},{10,11... | collective-permute-start | bytes 786440 | tf_op jit(solution)/shard_map/ppermute | solution.py:24
  60.2 1.3 copy-start.2
  60.2 1.3 copy-start.4
  60.2 1.4 copy-start.6
  60.3 1.6 copy-start.8
  61.9 14.4 %copy-start.5 = (f32[2,1]{0,1:T(1,128)S(1)}, f32[2,1]{0,1:T(1,128)}, u32[]{:S(2)}) copy-start(f32[2,1]{0,1:T(1,128)} %param.13) | copy-start | bytes 28
  64.2 27.2 %all-to-all-start.1 = ((f32[8,3,512]{2,1,0:T(4,128)}), f32[8,3,512]{2,1,0:T(4,128)S(1)}, u32[]{:S(2)}, u32[]{:S(2)}) async-start(f32[8,3,512]{2,1,0:T(4,128)} %broadcast_in_dim.9), calls=%async_computation.1 | async-start | bytes 131072 | tf_op jit(solution)/shard_map/all_to_all | solution.py:33
  78.7 23.4 %collective-permute-start.10 = (bf16[2,512,256]{1,2,0:T(8,128)(2,1)S(1)}, bf16[2,512,256]{1,2,0:T(8,128)(2,1)S(1)}, u32[]{:S(2)}, u32[]{:S(2)}) collective-permute-start(bf16[2,512,256]{1,2,0:T(8,128)(2,1)S(1)} %pad_maximum_fusion.4), channel_id=1, source_target_pairs={{0,2},{2,4},{4,6},{6,0},{1,3},{3,5},{5,7},{7,1},{8,10},{10,12},{12... | collective-permute-start | bytes 1572872 | tf_op jit(solution)/shard_map/ppermute | solution.py:24
  83.1 25.2 %collective-permute-start.11 = (bf16[2,512,256]{1,2,0:T(8,128)(2,1)S(1)}, bf16[2,512,256]{1,2,0:T(8,128)(2,1)}, u32[]{:S(2)}, u32[]{:S(2)}) collective-permute-start(bf16[2,512,256]{1,2,0:T(8,128)(2,1)S(1)} %pad_maximum_fusion.4), channel_id=1, source_target_pairs={{0,4},{2,6},{4,0},{6,2},{1,5},{3,7},{5,1},{7,3},{8,12},{10,14},{12... | collective-permute-start | bytes 1572872 | tf_op jit(solution)/shard_map/ppermute | solution.py:24
  86.9 23.3 %collective-permute-start.12 = (bf16[2,512,256]{1,2,0:T(8,128)(2,1)S(1)}, bf16[2,512,256]{1,2,0:T(8,128)(2,1)}, u32[]{:S(2)}, u32[]{:S(2)}) collective-permute-start(bf16[2,512,256]{1,2,0:T(8,128)(2,1)S(1)} %pad_maximum_fusion.4), channel_id=1, source_target_pairs={{0,6},{2,0},{4,2},{6,4},{1,7},{3,1},{5,3},{7,5},{8,14},{10,8},{12,... | collective-permute-start | bytes 1572872 | tf_op jit(solution)/shard_map/ppermute | solution.py:24
  95.3 22.6 %collective-permute-start.13 = (bf16[2048,288]{0,1:T(8,128)(2,1)}, bf16[2048,288]{0,1:T(8,128)(2,1)}, u32[]{:S(2)}, u32[]{:S(2)}) collective-permute-start(bf16[2048,288]{0,1:T(8,128)(2,1)} %get-tuple-element.56), channel_id=1, source_target_pairs={{0,8},{8,16},{16,24},{24,32},{32,40},{40,48},{48,56},{56,64},{64,7... | collective-permute-start | bytes 3538952 | tf_op jit(solution)/shard_map/ppermute | solution.py:24
  97.2 35.6 %collective-permute-start = (f32[2]{0:T(128)S(1)}, f32[2]{0:T(128)S(1)}, u32[]{:S(2)}, u32[]{:S(2)}) collective-permute-start(f32[2]{0:T(128)S(1)} %bitcast.111), channel_id=1, source_target_pairs={{0,24},{8,32},{16,40},{24,48},{32,56},{40,64},{48,72},{56,80},{64,... | collective-permute-start | bytes 32 | tf_op jit(solution)/shard_map/ppermute | solution.py:24
  102.1 30.7 %collective-permute-start.1 = (f32[2]{0:T(128)S(1)}, f32[2]{0:T(128)S(1)}, u32[]{:S(2)}, u32[]{:S(2)}) collective-permute-start(f32[2]{0:T(128)S(1)} %bitcast.113), channel_id=1, source_target_pairs={{0,16},{8,24},{16,32},{24,40},{32,48},{40,56},{48,64},{56,72},{64,... | collective-permute-start | bytes 32 | tf_op jit(solution)/shard_map/ppermute | solution.py:24
  108.3 24.5 %collective-permute-start.7 = (f32[2]{0:T(128)S(1)}, f32[2]{0:T(128)S(1)}, u32[]{:S(2)}, u32[]{:S(2)}) collective-permute-start(f32[2]{0:T(128)S(1)} %bitcast.114), channel_id=1, source_target_pairs={{0,504},{8,0},{16,8},{24,16},{32,24},{40,32},{48,40},{56,48},{64,5... | collective-permute-start | bytes 32 | tf_op jit(solution)/shard_map/ppermute | solution.py:24
  110.2 22.6 %collective-permute-start.8 = (f32[2]{0:T(128)S(1)}, f32[2]{0:T(128)S(1)}, u32[]{:S(2)}, u32[]{:S(2)}) collective-permute-start(f32[2]{0:T(128)S(1)} %bitcast.115), channel_id=1, source_target_pairs={{0,496},{8,504},{16,0},{24,8},{32,16},{40,24},{48,32},{56,40},{64,... | collective-permute-start | bytes 32 | tf_op jit(solution)/shard_map/ppermute | solution.py:24
  117.5 1.7 copy-start.10
  117.7 1.9 copy-start.3
  117.7 2.0 %copy-start.7 = (bf16[2,512,288]{1,2,0:T(8,128)(2,1)S(1)}, bf16[2,512,288]{1,2,0:T(8,128)(2,1)}, u32[]{:S(2)}) copy-start(bf16[2,512,288]{1,2,0:T(8,128)(2,1)} %param.8) | copy-start | bytes 1769476
  117.7 2.2 %copy-start.9 = (bf16[2,512,288]{1,2,0:T(8,128)(2,1)S(1)}, bf16[2,512,288]{1,2,0:T(8,128)(2,1)}, u32[]{:S(2)}) copy-start(bf16[2,512,288]{1,2,0:T(8,128)(2,1)} %param.9) | copy-start | bytes 1769476
  123.6 24.6 %all-to-all-start.2 = ((f32[8,3,512]{2,1,0:T(4,128)}), f32[8,3,512]{2,1,0:T(4,128)S(1)}, u32[]{:S(2)}, u32[]{:S(2)}) async-start(f32[8,3,512]{2,1,0:T(4,128)} %broadcast_in_dim.10), calls=%async_computation.2 | async-start | bytes 131072 | tf_op jit(solution)/shard_map/all_to_all | solution.py:33
  152.4 4.2 %collective-permute-start.14 = (bf16[8,4,32,288]{3,2,1,0:T(8,128)(2,1)S(1)}, bf16[8,4,32,288]{3,2,1,0:T(8,128)(2,1)S(1)}, u32[]{:S(2)}, u32[]{:S(2)}) collective-permute-start(bf16[8,4,32,288]{3,2,1,0:T(8,128)(2,1)S(1)} %select_bitcast_fusion.2), channel_id=1, source_target_pairs={{0,8},{8,0},{1,9},{9,1},{2,10},{10,2},{3,11},{11,3},{4,12},{12,4},... | collective-permute-start | bytes 1769480 | tf_op jit(solution)/shard_map/ppermute | solution.py:24
  157.0 38.1 %copy-start.1 = (f32[32,288]{1,0:T(8,128)S(1)}, f32[32,288]{1,0:T(8,128)}, u32[]{:S(2)}) copy-start(f32[32,288]{1,0:T(8,128)} %param.12) | copy-start | bytes 110596
  175.2 19.8 %all-to-all-start.4 = ((bf16[8,32,288]{2,1,0:T(8,128)(2,1)}), bf16[8,32,288]{2,1,0:T(8,128)(2,1)S(1)}, u32[]{:S(2)}, u32[]{:S(2)}) async-start(bf16[8,32,288]{2,1,0:T(8,128)(2,1)} %reduce_sum.101), calls=%async_computation.4 | async-start | bytes 393216 | tf_op jit(solution)/shard_map/all_to_all | solution.py:143

commit v6 on v5

--- a/solution.py
+++ b/solution.py
@@ -49,28 +49,18 @@
 
 
 def in_order(blocks, x):
-    blocks = jnp.stack(blocks)
-    twice = jnp.concatenate([blocks[::-1], blocks[::-1]])
-    return lax.dynamic_slice_in_dim(twice, 3 - x, 4, 0)
+    placed = jnp.broadcast_to(blocks[0][None], (4,) + blocks[0].shape)
+    for k in (2, 1, 3):
+        placed = lax.dynamic_update_slice_in_dim(placed, blocks[k][None], (x - k) & 3, 0)
+    return placed
 
 
-def merged(own, other, hi):
-    low = jnp.where(hi == 0, own, other)
-    high = jnp.where(hi == 0, other, own)
-    both = jnp.stack([low, high], axis=1)
-    return jnp.transpose(both, (2, 0, 1, 3)).reshape(TOK, 2048)
+def by_half(own, other, hi):
+    return jnp.where(hi == 0, jnp.stack([own, other]), jnp.stack([other, own]))
 
 
-def mass_neighbours(shares, before):
-    near = {k: shifted(shares, REP, -k) for k in (-3, -2, 1, 2)}
-    return {**near, -1: before, 0: shares}
-
-
-def masses(near):
-    mass1 = {k: near[k][0] + (1.0 - near[k - 1][0]) for k in (-2, 0, 2)}
-    mass2 = {k: near[k][1] * mass1[k] + (1.0 - near[k - 2][1]) * mass1[k - 2] for k in (0, 2)}
-    own = near[0][1]
-    return mass2[0], (own / mass2[0] + (1.0 - own) / mass2[2]) / lax.axis_size(REP)
+def laid_out(blocks):
+    return jnp.transpose(blocks, (2, 0, 1, 3)).reshape(TOK, 2048)
 
 
 def forward(gathered, quotient, residual, targets, gain):
@@ -101,32 +91,34 @@
 
     other0 = shifted(context[0], "z_hi", 1)
     own0 = along_x(context[0])
-    before = shifted(shares[:, 0], REP, 1)
+    before = shifted(shares[0], REP, 1)
     other0, own0, before = lax.optimization_barrier((other0, own0, before))
     wide0 = to_all(other0, "x")
     own0 = in_order(own0, x)
     context1 = after(context[1], other0)
     other1 = shifted(context1, "z_hi", 1)
-    gathered0 = merged(own0, wide0, hi)
+    gathered0 = laid_out(jnp.where(hi == 0, jnp.stack([own0, wide0], 1), jnp.stack([wide0, own0], 1)))
     share0 = shares[0, 0]
 
     output0, sums0 = forward(gathered0, slow_weight, residual[0], targets[0], gain)
     totals0 = jnp.sum(to_all(sums0, TP), axis=0)
-    pair1 = jnp.stack([context1, other1])
+    pair1 = by_half(context1, other1, hi)
     both1 = in_order(along_x(after(pair1, sums0)), x)
-    gathered1 = ordered(both1, hi)
+    gathered1 = laid_out(both1)
     grad0 = backward(output0, totals0, targets[0], gain)
     weight_grad0 = contract_rows(gathered0, grad0)
 
     pushed = ((1.0 - share0) * weight_grad0).astype(BF16)
     incoming = shifted(pushed, REP, 1)
+    mass_in = shifted((1.0 - shares[1]) * (shares[0] + (1.0 - before)), REP, 2)
+    incoming, mass_in = lax.optimization_barrier((incoming, mass_in))
     mass1 = share0 + (1.0 - before[0])
     step0 = share0 * weight_grad0 + incoming.astype(F32)
     quotient1 = (anchor - (LR / mass1) * step0).astype(BF16)
     output1, sums1 = forward(gathered1, quotient1, residual[1], targets[1], gain)
-    near = mass_neighbours(shares[:, 0], before)
-    near = lax.optimization_barrier((near, sums1))[0]
-    mass2, part = masses(near)
+    mass2 = shares[1] * (shares[0] + (1.0 - before)) + mass_in
+    mass_later = shifted(mass2, REP, -2)
+    part = ((shares[1] / mass2 + (1.0 - shares[1]) / mass_later) / lax.axis_size(REP))[0]
     totals1 = jnp.sum(to_all(sums1, TP), axis=0)
     grad1 = backward(output1, totals1, targets[1], gain)
     weight_grad1 = contract_rows(gathered1, grad1)
@@ -146,7 +138,7 @@
     anchor_rows = lax.dynamic_slice_in_dim(slow_weight, lax.axis_index(REP) * 32, 32, 0)
     new_momentum = BETA * momentum + gradient
     new_weight = anchor_rows.astype(F32) - ALPHA * LR * new_momentum
-    return (new_weight, new_momentum, mass2[None])
+    return (new_weight, new_momentum, mass2)
 
 
 def solution(mesh):

time: 198 us -> 192 us (0.970)
  starting transfers between devices: 99.8 us -> 92.9 us
  other arithmetic: 7.96 us -> 3.46 us
  waiting for transfers between devices: 40.5 us -> 44.9 us
    all_to_all x3, waiting for transfers between devices: 10.9 us -> 16.7 us  [to_all(): lax.all_to_all(jnp.broadcast_to(value[None], (count,) + value.shape), axi...]
    another operation x6 -> x0, other arithmetic: 3.44 us -> none  [the longest x2 2.55 us: in_order(): blocks = jnp.stack(blocks)]
    ppermute x15 -> x13, starting transfers between devices: 67.5 us -> 64.3 us  [shifted(): lax.ppermute(value, axis, [(i, (i + steps) % count) for i in range(count)])]
    all_to_all x3, starting transfers between devices: 25.6 us -> 23 us  [to_all(): lax.all_to_all(jnp.broadcast_to(value[None], (count,) + value.shape), axi...]
    concatenate x1 -> x0, other arithmetic: 2.33 us -> none  [in_order(): twice = jnp.concatenate([blocks[::-1], blocks[::-1]])]
    dynamic_update_slice x0 -> x6, local copies, waits for them, and re-layouts: none -> 2.28 us  [in_order(): lax.dynamic_update_slice_in_dim(placed, blocks[k][None], x - k & 3, 0)]
    ppermute x15 -> x13, waiting for transfers between devices: 17.6 us -> 16.9 us  [shifted(): lax.ppermute(value, axis, [(i, (i + steps) % count) for i in range(count)])]
  transfers between devices with their start and end apart: 19 -> 17, of which waited for: 9 -> 11; matrix products, arithmetic and copies ran while one was open for 10% -> 6% of each run, Pallas kernels for 0% -> 0%
where the time goes in v6:
time: 192 us; the launch traced here: 191 us
  starting transfers between devices  92.9 us (48%)
  waiting for transfers between devices  44.9 us (23%)
  blocking collectives  17.2 us (9%)
  matrix products  12.8 us (7%)
  local copies, waits for them, and re-layouts  11.6 us (6%)
  between operations  8.14 us (4%)
  other arithmetic  3.46 us (2%)
    ppermute x13, starting transfers between devices, shifted(): lax.ppermute(value, axis, [(i, (i + steps) % count) for i in range(count)])  64.3 us
    all_to_all x3, starting transfers between devices, to_all(): lax.all_to_all(jnp.broadcast_to(value[None], (count,) + value.shape), axi...  23 us
    all_to_all x1, blocking collectives, body(): parts = lax.all_to_all(parts, 'y', 0, 0)  17.2 us
    ppermute x13, waiting for transfers between devices, shifted(): lax.ppermute(value, axis, [(i, (i + steps) % count) for i in range(count)])  16.9 us
    all_to_all x3, waiting for transfers between devices, to_all(): lax.all_to_all(jnp.broadcast_to(value[None], (count,) + value.shape), axi...  16.7 us
    all_to_all x1, waiting for transfers between devices, body(): parts = lax.all_to_all(total.astype(BF16), 'z_lo', 0, 0)  11.4 us
    dot_general x2, matrix products, contract_rows(): lax.dot_general(left, right, (((0,), (0,)), ((), ())), preferred_element_...  8.16 us
    all_to_all x1, starting transfers between devices, body(): parts = lax.all_to_all(total.astype(BF16), 'z_lo', 0, 0)  5.64 us
  transfers between devices with their start and end apart: 17, of which 11 were waited for; matrix products, arithmetic and copies ran while one was open for 6% of the time, Pallas kernels for 0%

profile of v6, /device:TPU:32, one launch (start us, length us, event | category | flops | bytes accessed | tf_op | source)
XLA Modules:
  0.0 191.0 jit_solution(17374982944087644508)
XLA Ops:
  0.6 1.1 fusion.39
  1.8 14.8 %collective-permute-start = (bf16[512,256]{0,1:T(8,128)(2,1)S(1)}, bf16[512,256]{0,1:T(8,128)(2,1)S(1)}, u32[]{:S(2)}, u32[]{:S(2)}) collective-permute-start(bf16[512,256]{0,1:T(8,128)(2,1)S(1)} %bitcast.80), channel_id=1, source_target_pairs={{0,1},{1,0},{2,3},{3,2},{4,5},{5,4},{6,7},{7,6},{8,9},{9,8},{10,11... | collective-permute-start | bytes 786440 | tf_op jit(solution)/shard_map/ppermute | solution.py:24
  16.7 3.4 %collective-permute-start.1 = (bf16[512,256]{0,1:T(8,128)(2,1)S(1)}, bf16[512,256]{0,1:T(8,128)(2,1)S(1)}, u32[]{:S(2)}, u32[]{:S(2)}) collective-permute-start(bf16[512,256]{0,1:T(8,128)(2,1)S(1)} %bitcast.81), channel_id=1, source_target_pairs={{0,2},{2,4},{4,6},{6,0},{1,3},{3,5},{5,7},{7,1},{8,10},{10,12},{12... | collective-permute-start | bytes 786440 | tf_op jit(solution)/shard_map/ppermute | solution.py:24
  20.1 4.6 %collective-permute-start.2 = (bf16[512,256]{0,1:T(8,128)(2,1)S(1)}, bf16[512,256]{0,1:T(8,128)(2,1)S(1)}, u32[]{:S(2)}, u32[]{:S(2)}) collective-permute-start(bf16[512,256]{0,1:T(8,128)(2,1)S(1)} %bitcast.82), channel_id=1, source_target_pairs={{0,4},{2,6},{4,0},{6,2},{1,5},{3,7},{5,1},{7,3},{8,12},{10,14},{12... | collective-permute-start | bytes 786440 | tf_op jit(solution)/shard_map/ppermute | solution.py:24
  24.7 3.3 %collective-permute-start.3 = (bf16[512,256]{0,1:T(8,128)(2,1)S(1)}, bf16[512,256]{0,1:T(8,128)(2,1)S(1)}, u32[]{:S(2)}, u32[]{:S(2)}) collective-permute-start(bf16[512,256]{0,1:T(8,128)(2,1)S(1)} %bitcast.83), channel_id=1, source_target_pairs={{0,6},{2,0},{4,2},{6,4},{1,7},{3,1},{5,3},{7,5},{8,14},{10,8},{12,... | collective-permute-start | bytes 786440 | tf_op jit(solution)/shard_map/ppermute | solution.py:24
  28.1 1.3 fusion.40
  29.4 1.9 collective-permute-start.4
  31.3 5.3 %collective-permute-done.4 = f32[1]{0:T(128)} collective-permute-done((f32[1]{0:T(128)}, f32[1]{0:T(128)}, u32[]{:S(2)}, u32[]{:S(2)}) %collective-permute-start.4) | collective-permute-done | bytes 36 | tf_op jit(solution)/shard_map/ppermute | solution.py:24
  36.6 3.4 %collective-permute-done = bf16[512,256]{0,1:T(8,128)(2,1)S(1)} collective-permute-done((bf16[512,256]{0,1:T(8,128)(2,1)S(1)}, bf16[512,256]{0,1:T(8,128)(2,1)S(1)}, u32[]{:S(2)}, u32[]{:S(2)}) %collective-permute-start) | collective-permute-done | bytes 262176 | tf_op jit(solution)/shard_map/ppermute | solution.py:24
  40.1 1.1 broadcast_in_dim.14
  41.1 4.3 %all-to-all-start = ((bf16[4,512,256]{1,2,0:T(8,128)(2,1)}), bf16[4,512,256]{1,2,0:T(8,128)(2,1)S(1)}, u32[]{:S(2)}, u32[]{:S(2)}) async-start(bf16[4,512,256]{1,2,0:T(8,128)(2,1)} %broadcast_in_dim.14), calls=%async_computation | async-start | bytes 2097152 | tf_op jit(solution)/shard_map/all_to_all | solution.py:33
  45.6 12.1 %collective-permute-start.8 = (bf16[512,256]{0,1:T(8,128)(2,1)S(1)}, bf16[512,256]{0,1:T(8,128)(2,1)}, u32[]{:S(2)}, u32[]{:S(2)}) collective-permute-start(bf16[512,256]{0,1:T(8,128)(2,1)S(1)} %bitcast.85), channel_id=1, source_target_pairs={{0,1},{1,0},{2,3},{3,2},{4,5},{5,4},{6,7},{7,6},{8,9},{9,8},{10,11... | collective-permute-start | bytes 786440 | tf_op jit(solution)/shard_map/ppermute | solution.py:24
  57.9 1.9 all-to-all-done
  60.1 1.0 copy-done.2
  61.1 0.6 copy-done.5
  61.7 0.4 copy-done.7
  62.1 0.9 multiply_reduce_fusion.2
  63.1 0.6 broadcast_in_dim.15
  63.7 12.1 %all-to-all-start.1 = ((f32[8,3,512]{2,1,0:T(4,128)}), f32[8,3,512]{2,1,0:T(4,128)S(1)}, u32[]{:S(2)}, u32[]{:S(2)}) async-start(f32[8,3,512]{2,1,0:T(4,128)} %broadcast_in_dim.15), calls=%async_computation.1 | async-start | bytes 131072 | tf_op jit(solution)/shard_map/all_to_all | solution.py:33
  76.4 1.2 collective-permute-done.8
  77.6 1.1 maximum_select_fusion.1
  78.7 5.2 %collective-permute-start.9 = (bf16[2,512,256]{1,2,0:T(8,128)(2,1)S(1)}, bf16[2,512,256]{1,2,0:T(8,128)(2,1)S(1)}, u32[]{:S(2)}, u32[]{:S(2)}) collective-permute-start(bf16[2,512,256]{1,2,0:T(8,128)(2,1)S(1)} %maximum_select_fusion.1), channel_id=1, source_target_pairs={{0,4},{2,6},{4,0},{6,2},{1,5},{3,7},{5,1},{7,3},{8,12},{10,14},{12... | collective-permute-start | bytes 1572872 | tf_op jit(solution)/shard_map/ppermute | solution.py:24
  83.8 7.2 %all-to-all-done.1 = f32[8,3,512]{2,1,0:T(4,128)S(1)} async-done(((f32[8,3,512]{2,1,0:T(4,128)}), f32[8,3,512]{2,1,0:T(4,128)S(1)}, u32[]{:S(2)}, u32[]{:S(2)}) %all-to-all-start.1) | async-done | bytes 49184 | tf_op jit(solution)/shard_map/all_to_all | solution.py:33
  91.1 4.3 %multiply_convert_fusion.1 = (bf16[2048,288]{0,1:T(8,128)(2,1)}, f32[2048,288]{0,1:T(8,128)}) fusion(f32[]{:T(128)S(6)} %sub.60, bf16[512,2048]{0,1:T(8,128)(2,1)} %bitcast.79, f32[512,288]{0,1:T(8,128)S(1)} %get-tuple-element.39, f32[512]{0:T(512)S(1)} %bitcast.89, f32[512]{0:T(512)S(1)} %bitcast.88, f32[288]{0:T(512)S(1)} %copy-done.4, ...), kind=kOutput, calls=%fused_computation.4 | convolution fusion | flops 606486528 | bytes 6529028 | tf_op jit(solution)/shard_map/dot_general | solution.py:37
  95.4 1.9 collective-permute-start.5
  97.3 2.5 %collective-permute-start.10 = (bf16[2,512,256]{1,2,0:T(8,128)(2,1)S(1)}, bf16[2,512,256]{1,2,0:T(8,128)(2,1)}, u32[]{:S(2)}, u32[]{:S(2)}) collective-permute-start(bf16[2,512,256]{1,2,0:T(8,128)(2,1)S(1)} %maximum_select_fusion.1), channel_id=1, source_target_pairs={{0,2},{2,4},{4,6},{6,0},{1,3},{3,5},{5,7},{7,1},{8,10},{10,12},{12... | collective-permute-start | bytes 1572872 | tf_op jit(solution)/shard_map/ppermute | solution.py:24
  99.8 4.6 %collective-permute-start.11 = (bf16[2,512,256]{1,2,0:T(8,128)(2,1)S(1)}, bf16[2,512,256]{1,2,0:T(8,128)(2,1)}, u32[]{:S(2)}, u32[]{:S(2)}) collective-permute-start(bf16[2,512,256]{1,2,0:T(8,128)(2,1)S(1)} %maximum_select_fusion.1), channel_id=1, source_target_pairs={{0,6},{2,0},{4,2},{6,4},{1,7},{3,1},{5,3},{7,5},{8,14},{10,8},{12,... | collective-permute-start | bytes 1572872 | tf_op jit(solution)/shard_map/ppermute | solution.py:24
  106.3 4.8 %collective-permute-start.6 = (f32[1]{0:T(128)}, f32[1]{0:T(128)}, u32[]{:S(2)}, u32[]{:S(2)}) collective-permute-start(f32[1]{0:T(128)} %mul.152), channel_id=1, source_target_pairs={{0,16},{8,24},{16,32},{24,40},{32,48},{40,56},{48,64},{56,72},{64,... | collective-permute-start | bytes 20 | tf_op jit(solution)/shard_map/ppermute | solution.py:24
  112.1 2.6 %collective-permute-done.10 = bf16[2,512,256]{1,2,0:T(8,128)(2,1)} collective-permute-done((bf16[2,512,256]{1,2,0:T(8,128)(2,1)S(1)}, bf16[2,512,256]{1,2,0:T(8,128)(2,1)}, u32[]{:S(2)}, u32[]{:S(2)}) %collective-permute-start.10) | collective-permute-done | bytes 524320 | tf_op jit(solution)/shard_map/ppermute | solution.py:24
  114.6 1.1 bitcast_dynamic-update-slice_fusion.1
  115.7 0.6 collective-permute-done.11
  116.3 1.1 bitcast_dynamic-update-slice_fusion
  117.5 3.7 %multiply_reduce_fusion = (f32[512]{0:T(512)S(1)}, f32[512]{0:T(512)S(1)}, f32[512]{0:T(512)S(1)}, f32[512,288]{0,1:T(8,128)}) fusion(f32[288]{0:T(512)S(1)} %copy-done.4, bf16[2,512,288]{1,2,0:T(8,128)(2,1)S(1)} %copy-done.9, bf16[512,2048]{0,1:T(8,128)(2,1)S(1)} %bitcast.76, bf16[2048,288]{0,1:T(8,128)(2,1)S(1)} %copy-done.3, ...), kind=kOutput, calls=%fused_computation.26 | convolution fusion | flops 609581568 | bytes 8002696 | tf_op jit(solution)/shard_map/dot_general | solution.py:67
  121.2 0.6 broadcast_in_dim.20
  121.8 6.7 %all-to-all-start.2 = ((f32[8,3,512]{2,1,0:T(4,128)}), f32[8,3,512]{2,1,0:T(4,128)S(1)}, u32[]{:S(2)}, u32[]{:S(2)}) async-start(f32[8,3,512]{2,1,0:T(4,128)} %broadcast_in_dim.20), calls=%async_computation.2 | async-start | bytes 131072 | tf_op jit(solution)/shard_map/all_to_all | solution.py:33
  129.8 3.2 %collective-permute-start.7 = (f32[1]{0:T(128)}, f32[1]{0:T(128)}, u32[]{:S(2)}, u32[]{:S(2)}) collective-permute-start(f32[1]{0:T(128)} %add.86), channel_id=1, source_target_pairs={{0,496},{8,504},{16,0},{24,8},{32,16},{40,24},{48,32},{56,40},{64,... | collective-permute-start | bytes 20 | tf_op jit(solution)/shard_map/ppermute | solution.py:24
  133.7 1.5 collective-permute-done.7
  135.9 7.6 %all-to-all-done.2 = f32[8,3,512]{2,1,0:T(4,128)S(1)} async-done(((f32[8,3,512]{2,1,0:T(4,128)}), f32[8,3,512]{2,1,0:T(4,128)S(1)}, u32[]{:S(2)}, u32[]{:S(2)}) %all-to-all-start.2) | async-done | bytes 49184 | tf_op jit(solution)/shard_map/all_to_all | solution.py:33
  143.6 3.9 %multiply_convert_fusion = bf16[2048,288]{0,1:T(8,128)(2,1)S(1)} fusion(f32[]{:T(128)} %bitcast.18, bf16[512,2048]{0,1:T(8,128)(2,1)S(1)} %bitcast.77, f32[512,288]{0,1:T(8,128)} %get-tuple-element.42, bf16[2048,288]{0,1:T(8,128)(2,1)} %collective-permute-done.5, f32[2048,288]{0,1:T(8,128)} %get-tuple-element.41, f32[]{:T(128)} %bitcast.3, ...), kind=kOutput, calls=%fused_computation.1 | convolution fusion | flops 608845824 | bytes 7707904 | tf_op jit(solution)/shard_map/dot_general | solution.py:37
  147.5 0.8 copy.34
  148.4 1.9 %collective-permute-start.12 = (bf16[8,4,32,288]{3,2,1,0:T(8,128)(2,1)S(1)}, bf16[8,4,32,288]{3,2,1,0:T(8,128)(2,1)S(1)}, u32[]{:S(2)}, u32[]{:S(2)}) collective-permute-start(bf16[8,4,32,288]{3,2,1,0:T(8,128)(2,1)S(1)} %select_bitcast_fusion), channel_id=1, source_target_pairs={{0,8},{8,0},{1,9},{9,1},{2,10},{10,2},{3,11},{11,3},{4,12},{12,4},... | collective-permute-start | bytes 1769480 | tf_op jit(solution)/shard_map/ppermute | solution.py:24
  150.4 2.3 %collective-permute-done.12 = bf16[8,4,32,288]{3,2,1,0:T(8,128)(2,1)S(1)} collective-permute-done((bf16[8,4,32,288]{3,2,1,0:T(8,128)(2,1)S(1)}, bf16[8,4,32,288]{3,2,1,0:T(8,128)(2,1)S(1)}, u32[]{:S(2)}, u32[]{:S(2)}) %collective-permute-start.12) | collective-permute-done | bytes 589856 | tf_op jit(solution)/shard_map/ppermute | solution.py:24
  153.0 17.2 %all_to_all.25 = bf16[4,8,32,288]{3,2,1,0:T(8,128)(2,1)S(1)} all-to-all(bf16[4,8,32,288]{3,2,1,0:T(8,128)(2,1)S(1)} %copy.35), channel_id=1, replica_groups=mesh['z_lo'=8,'y'=4,'core'=2,'x'=4,'z_hi'=2] {'y'}, dimensions={0} | all-to-all | bytes 1179648 | tf_op jit(solution)/shard_map/all_to_all | solution.py:133
  170.2 0.9 reduce_sum.101
  171.1 5.6 %all-to-all-start.4 = ((bf16[8,32,288]{2,1,0:T(8,128)(2,1)}), bf16[8,32,288]{2,1,0:T(8,128)(2,1)S(1)}, u32[]{:S(2)}, u32[]{:S(2)}) async-start(bf16[8,32,288]{2,1,0:T(8,128)(2,1)} %reduce_sum.101), calls=%async_computation.4 | async-start | bytes 393216 | tf_op jit(solution)/shard_map/all_to_all | solution.py:135
  176.7 1.0 constant_dynamic-slice_fusion
  177.8 11.4 %all-to-all-done.4 = bf16[8,32,288]{2,1,0:T(8,128)(2,1)S(1)} async-done(((bf16[8,32,288]{2,1,0:T(8,128)(2,1)}), bf16[8,32,288]{2,1,0:T(8,128)(2,1)S(1)}, u32[]{:S(2)}, u32[]{:S(2)}) %all-to-all-start.4) | async-done | bytes 147488 | tf_op jit(solution)/shard_map/all_to_all | solution.py:135
  189.2 0.7 multiply_subtract_fusion
  (46 shorter events, 1.7 us)
Async XLA Ops:
  1.8 38.2 %collective-permute-start = (bf16[512,256]{0,1:T(8,128)(2,1)S(1)}, bf16[512,256]{0,1:T(8,128)(2,1)S(1)}, u32[]{:S(2)}, u32[]{:S(2)}) collective-permute-start(bf16[512,256]{0,1:T(8,128)(2,1)S(1)} %bitcast.80), channel_id=1, source_target_pairs={{0,1},{1,0},{2,3},{3,2},{4,5},{5,4},{6,7},{7,6},{8,9},{9,8},{10,11... | collective-permute-start | bytes 786440 | tf_op jit(solution)/shard_map/ppermute | solution.py:24
  16.7 23.4 %collective-permute-start.1 = (bf16[512,256]{0,1:T(8,128)(2,1)S(1)}, bf16[512,256]{0,1:T(8,128)(2,1)S(1)}, u32[]{:S(2)}, u32[]{:S(2)}) collective-permute-start(bf16[512,256]{0,1:T(8,128)(2,1)S(1)} %bitcast.81), channel_id=1, source_target_pairs={{0,2},{2,4},{4,6},{6,0},{1,3},{3,5},{5,7},{7,1},{8,10},{10,12},{12... | collective-permute-start | bytes 786440 | tf_op jit(solution)/shard_map/ppermute | solution.py:24
  20.1 20.0 %collective-permute-start.2 = (bf16[512,256]{0,1:T(8,128)(2,1)S(1)}, bf16[512,256]{0,1:T(8,128)(2,1)S(1)}, u32[]{:S(2)}, u32[]{:S(2)}) collective-permute-start(bf16[512,256]{0,1:T(8,128)(2,1)S(1)} %bitcast.82), channel_id=1, source_target_pairs={{0,4},{2,6},{4,0},{6,2},{1,5},{3,7},{5,1},{7,3},{8,12},{10,14},{12... | collective-permute-start | bytes 786440 | tf_op jit(solution)/shard_map/ppermute | solution.py:24
  24.7 15.3 %collective-permute-start.3 = (bf16[512,256]{0,1:T(8,128)(2,1)S(1)}, bf16[512,256]{0,1:T(8,128)(2,1)S(1)}, u32[]{:S(2)}, u32[]{:S(2)}) collective-permute-start(bf16[512,256]{0,1:T(8,128)(2,1)S(1)} %bitcast.83), channel_id=1, source_target_pairs={{0,6},{2,0},{4,2},{6,4},{1,7},{3,1},{5,3},{7,5},{8,14},{10,8},{12,... | collective-permute-start | bytes 786440 | tf_op jit(solution)/shard_map/ppermute | solution.py:24
  29.4 7.2 %collective-permute-start.4 = (f32[1]{0:T(128)}, f32[1]{0:T(128)}, u32[]{:S(2)}, u32[]{:S(2)}) collective-permute-start(f32[1]{0:T(128)} %bitcast.1), channel_id=1, source_target_pairs={{0,8},{8,16},{16,24},{24,32},{32,40},{40,48},{48,56},{56,64},{64,7... | collective-permute-start | bytes 20 | tf_op jit(solution)/shard_map/ppermute | solution.py:24
  41.1 18.6 %all-to-all-start = ((bf16[4,512,256]{1,2,0:T(8,128)(2,1)}), bf16[4,512,256]{1,2,0:T(8,128)(2,1)S(1)}, u32[]{:S(2)}, u32[]{:S(2)}) async-start(bf16[4,512,256]{1,2,0:T(8,128)(2,1)} %broadcast_in_dim.14), calls=%async_computation | async-start | bytes 2097152 | tf_op jit(solution)/shard_map/all_to_all | solution.py:33
  45.6 32.0 %collective-permute-start.8 = (bf16[512,256]{0,1:T(8,128)(2,1)S(1)}, bf16[512,256]{0,1:T(8,128)(2,1)}, u32[]{:S(2)}, u32[]{:S(2)}) collective-permute-start(bf16[512,256]{0,1:T(8,128)(2,1)S(1)} %bitcast.85), channel_id=1, source_target_pairs={{0,1},{1,0},{2,3},{3,2},{4,5},{5,4},{6,7},{7,6},{8,9},{9,8},{10,11... | collective-permute-start | bytes 786440 | tf_op jit(solution)/shard_map/ppermute | solution.py:24
  59.8 1.3 copy-start.2
  59.8 1.3 copy-start.4
  59.8 2.0 %copy-start.5 = (bf16[2,512,288]{1,2,0:T(8,128)(2,1)S(1)}, bf16[2,512,288]{1,2,0:T(8,128)(2,1)}, u32[]{:S(2)}) copy-start(bf16[2,512,288]{1,2,0:T(8,128)(2,1)} %param.8) | copy-start | bytes 1769476
  59.8 2.4 %copy-start.7 = (bf16[2,512,288]{1,2,0:T(8,128)(2,1)S(1)}, bf16[2,512,288]{1,2,0:T(8,128)(2,1)}, u32[]{:S(2)}) copy-start(bf16[2,512,288]{1,2,0:T(8,128)(2,1)} %param.9) | copy-start | bytes 1769476
  60.1 3.0 %copy-start = (bf16[4,2,512,256]{2,3,1,0:T(8,128)(2,1)}, bf16[4,2,512,256]{2,3,1,0:T(8,128)(2,1)S(1)}, u32[]{:S(2)}) copy-start(bf16[4,2,512,256]{2,3,1,0:T(8,128)(2,1)S(1)} %maximum_select_fusion) | copy-start | bytes 6291460
  62.1 28.9 %copy-start.8 = (bf16[2,512,288]{1,2,0:T(8,128)(2,1)S(1)}, bf16[2,512,288]{1,2,0:T(8,128)(2,1)}, u32[]{:S(2)}) copy-start(bf16[2,512,288]{1,2,0:T(8,128)(2,1)} %param.9) | copy-start | bytes 1769476
  63.7 27.3 %all-to-all-start.1 = ((f32[8,3,512]{2,1,0:T(4,128)}), f32[8,3,512]{2,1,0:T(4,128)S(1)}, u32[]{:S(2)}, u32[]{:S(2)}) async-start(f32[8,3,512]{2,1,0:T(4,128)} %broadcast_in_dim.15), calls=%async_computation.1 | async-start | bytes 131072 | tf_op jit(solution)/shard_map/all_to_all | solution.py:33
  78.7 33.1 %collective-permute-start.9 = (bf16[2,512,256]{1,2,0:T(8,128)(2,1)S(1)}, bf16[2,512,256]{1,2,0:T(8,128)(2,1)S(1)}, u32[]{:S(2)}, u32[]{:S(2)}) collective-permute-start(bf16[2,512,256]{1,2,0:T(8,128)(2,1)S(1)} %maximum_select_fusion.1), channel_id=1, source_target_pairs={{0,4},{2,6},{4,0},{6,2},{1,5},{3,7},{5,1},{7,3},{8,12},{10,14},{12... | collective-permute-start | bytes 1572872 | tf_op jit(solution)/shard_map/ppermute | solution.py:24
  95.4 22.0 %collective-permute-start.5 = (bf16[2048,288]{0,1:T(8,128)(2,1)}, bf16[2048,288]{0,1:T(8,128)(2,1)}, u32[]{:S(2)}, u32[]{:S(2)}) collective-permute-start(bf16[2048,288]{0,1:T(8,128)(2,1)} %get-tuple-element.40), channel_id=1, source_target_pairs={{0,8},{8,16},{16,24},{24,32},{32,40},{40,48},{48,56},{56,64},{64,7... | collective-permute-start | bytes 3538952 | tf_op jit(solution)/shard_map/ppermute | solution.py:24
  97.3 17.3 %collective-permute-start.10 = (bf16[2,512,256]{1,2,0:T(8,128)(2,1)S(1)}, bf16[2,512,256]{1,2,0:T(8,128)(2,1)}, u32[]{:S(2)}, u32[]{:S(2)}) collective-permute-start(bf16[2,512,256]{1,2,0:T(8,128)(2,1)S(1)} %maximum_select_fusion.1), channel_id=1, source_target_pairs={{0,2},{2,4},{4,6},{6,0},{1,3},{3,5},{5,7},{7,1},{8,10},{10,12},{12... | collective-permute-start | bytes 1572872 | tf_op jit(solution)/shard_map/ppermute | solution.py:24
  99.8 16.5 %collective-permute-start.11 = (bf16[2,512,256]{1,2,0:T(8,128)(2,1)S(1)}, bf16[2,512,256]{1,2,0:T(8,128)(2,1)}, u32[]{:S(2)}, u32[]{:S(2)}) collective-permute-start(bf16[2,512,256]{1,2,0:T(8,128)(2,1)S(1)} %maximum_select_fusion.1), channel_id=1, source_target_pairs={{0,6},{2,0},{4,2},{6,4},{1,7},{3,1},{5,3},{7,5},{8,14},{10,8},{12,... | collective-permute-start | bytes 1572872 | tf_op jit(solution)/shard_map/ppermute | solution.py:24
  106.3 11.1 %collective-permute-start.6 = (f32[1]{0:T(128)}, f32[1]{0:T(128)}, u32[]{:S(2)}, u32[]{:S(2)}) collective-permute-start(f32[1]{0:T(128)} %mul.152), channel_id=1, source_target_pairs={{0,16},{8,24},{16,32},{24,40},{32,48},{40,56},{48,64},{56,72},{64,... | collective-permute-start | bytes 20 | tf_op jit(solution)/shard_map/ppermute | solution.py:24
  111.8 5.7 %copy-start.10 = (f32[2048,288]{0,1:T(8,128)S(1)}, f32[2048,288]{0,1:T(8,128)}, u32[]{:S(2)}) copy-start(f32[2048,288]{0,1:T(8,128)} %get-tuple-element.41) | copy-start | bytes 7077892
  112.0 5.5 %copy-start.3 = (bf16[2048,288]{0,1:T(8,128)(2,1)S(1)}, bf16[2048,288]{0,1:T(8,128)(2,1)}, u32[]{:S(2)}) copy-start(bf16[2048,288]{0,1:T(8,128)(2,1)} %param.11) | copy-start | bytes 3538948
  112.0 5.5 %copy-start.6 = (bf16[2,512,288]{1,2,0:T(8,128)(2,1)S(1)}, bf16[2,512,288]{1,2,0:T(8,128)(2,1)}, u32[]{:S(2)}) copy-start(bf16[2,512,288]{1,2,0:T(8,128)(2,1)} %param.8) | copy-start | bytes 1769476
  112.0 5.5 %copy-start.9 = (bf16[2,512,288]{1,2,0:T(8,128)(2,1)S(1)}, bf16[2,512,288]{1,2,0:T(8,128)(2,1)}, u32[]{:S(2)}) copy-start(bf16[2,512,288]{1,2,0:T(8,128)(2,1)} %param.9) | copy-start | bytes 1769476
  121.8 21.7 %all-to-all-start.2 = ((f32[8,3,512]{2,1,0:T(4,128)}), f32[8,3,512]{2,1,0:T(4,128)S(1)}, u32[]{:S(2)}, u32[]{:S(2)}) async-start(f32[8,3,512]{2,1,0:T(4,128)} %broadcast_in_dim.20), calls=%async_computation.2 | async-start | bytes 131072 | tf_op jit(solution)/shard_map/all_to_all | solution.py:33
  129.8 5.4 %collective-permute-start.7 = (f32[1]{0:T(128)}, f32[1]{0:T(128)}, u32[]{:S(2)}, u32[]{:S(2)}) collective-permute-start(f32[1]{0:T(128)} %add.86), channel_id=1, source_target_pairs={{0,496},{8,504},{16,0},{24,8},{32,16},{40,24},{48,32},{56,40},{64,... | collective-permute-start | bytes 20 | tf_op jit(solution)/shard_map/ppermute | solution.py:24
  148.4 4.2 %collective-permute-start.12 = (bf16[8,4,32,288]{3,2,1,0:T(8,128)(2,1)S(1)}, bf16[8,4,32,288]{3,2,1,0:T(8,128)(2,1)S(1)}, u32[]{:S(2)}, u32[]{:S(2)}) collective-permute-start(bf16[8,4,32,288]{3,2,1,0:T(8,128)(2,1)S(1)} %select_bitcast_fusion), channel_id=1, source_target_pairs={{0,8},{8,0},{1,9},{9,1},{2,10},{10,2},{3,11},{11,3},{4,12},{12,4},... | collective-permute-start | bytes 1769480 | tf_op jit(solution)/shard_map/ppermute | solution.py:24
  153.0 36.2 %copy-start.1 = (f32[32,288]{1,0:T(8,128)S(1)}, f32[32,288]{1,0:T(8,128)}, u32[]{:S(2)}) copy-start(f32[32,288]{1,0:T(8,128)} %param.12) | copy-start | bytes 110596
  171.1 18.1 %all-to-all-start.4 = ((bf16[8,32,288]{2,1,0:T(8,128)(2,1)}), bf16[8,32,288]{2,1,0:T(8,128)(2,1)S(1)}, u32[]{:S(2)}, u32[]{:S(2)}) async-start(bf16[8,32,288]{2,1,0:T(8,128)(2,1)} %reduce_sum.101), calls=%async_computation.4 | async-start | bytes 393216 | tf_op jit(solution)/shard_map/all_to_all | solution.py:135

commit v7 on v6

--- a/solution.py
+++ b/solution.py
@@ -92,7 +92,9 @@
     other0 = shifted(context[0], "z_hi", 1)
     own0 = along_x(context[0])
     before = shifted(shares[0], REP, 1)
-    other0, own0, before = lax.optimization_barrier((other0, own0, before))
+    mass1 = shares[0] + (1.0 - before)
+    leaving = (1.0 - shares[1]) * mass1
+    other0, own0, mass1, leaving = lax.optimization_barrier((other0, own0, mass1, leaving))
     wide0 = to_all(other0, "x")
     own0 = in_order(own0, x)
     context1 = after(context[1], other0)
@@ -103,20 +105,19 @@
     output0, sums0 = forward(gathered0, slow_weight, residual[0], targets[0], gain)
     totals0 = jnp.sum(to_all(sums0, TP), axis=0)
     pair1 = by_half(context1, other1, hi)
-    both1 = in_order(along_x(after(pair1, sums0)), x)
+    both1 = in_order(lax.optimization_barrier(along_x(after(pair1, sums0))), x)
     gathered1 = laid_out(both1)
     grad0 = backward(output0, totals0, targets[0], gain)
     weight_grad0 = contract_rows(gathered0, grad0)
 
     pushed = ((1.0 - share0) * weight_grad0).astype(BF16)
     incoming = shifted(pushed, REP, 1)
-    mass_in = shifted((1.0 - shares[1]) * (shares[0] + (1.0 - before)), REP, 2)
+    mass_in = shifted(leaving, REP, 2)
     incoming, mass_in = lax.optimization_barrier((incoming, mass_in))
-    mass1 = share0 + (1.0 - before[0])
     step0 = share0 * weight_grad0 + incoming.astype(F32)
-    quotient1 = (anchor - (LR / mass1) * step0).astype(BF16)
+    quotient1 = (anchor - (LR / mass1[0]) * step0).astype(BF16)
     output1, sums1 = forward(gathered1, quotient1, residual[1], targets[1], gain)
-    mass2 = shares[1] * (shares[0] + (1.0 - before)) + mass_in
+    mass2 = shares[1] * mass1 + mass_in
     mass_later = shifted(mass2, REP, -2)
     part = ((shares[1] / mass2 + (1.0 - shares[1]) / mass_later) / lax.axis_size(REP))[0]
     totals1 = jnp.sum(to_all(sums1, TP), axis=0)

time: 192 us -> 193 us (level)
  starting transfers between devices: 92.9 us -> 96.4 us
    all_to_all x3, waiting for transfers between devices: 16.7 us -> 10.6 us  [to_all(): lax.all_to_all(jnp.broadcast_to(value[None], (count,) + value.shape), axi...]
    ppermute x13, waiting for transfers between devices: 16.9 us -> 22.1 us  [shifted(): lax.ppermute(value, axis, [(i, (i + steps) % count) for i in range(count)])]
    all_to_all x3, starting transfers between devices: 23 us -> 27.5 us  [to_all(): lax.all_to_all(jnp.broadcast_to(value[None], (count,) + value.shape), axi...]
where the time goes in v7:
time: 193 us; the launch traced here: 192 us
  starting transfers between devices  96.4 us (50%)
  waiting for transfers between devices  44.7 us (23%)
  blocking collectives  15.9 us (8%)
  matrix products  12.8 us (7%)
  local copies, waits for them, and re-layouts  11.6 us (6%)
  between operations  7.49 us (4%)
  other arithmetic  3.46 us (2%)
    ppermute x13, starting transfers between devices, shifted(): lax.ppermute(value, axis, [(i, (i + steps) % count) for i in range(count)])  63.3 us
    all_to_all x3, starting transfers between devices, to_all(): lax.all_to_all(jnp.broadcast_to(value[None], (count,) + value.shape), axi...  27.5 us
    ppermute x13, waiting for transfers between devices, shifted(): lax.ppermute(value, axis, [(i, (i + steps) % count) for i in range(count)])  22.1 us
    all_to_all x1, blocking collectives, body(): parts = lax.all_to_all(parts, 'y', 0, 0)  15.9 us
    all_to_all x1, waiting for transfers between devices, body(): parts = lax.all_to_all(total.astype(BF16), 'z_lo', 0, 0)  11.9 us
    all_to_all x3, waiting for transfers between devices, to_all(): lax.all_to_all(jnp.broadcast_to(value[None], (count,) + value.shape), axi...  10.6 us
    dot_general x2, matrix products, contract_rows(): lax.dot_general(left, right, (((0,), (0,)), ((), ())), preferred_element_...  7.77 us
    all_to_all x1, starting transfers between devices, body(): parts = lax.all_to_all(total.astype(BF16), 'z_lo', 0, 0)  5.63 us
  transfers between devices with their start and end apart: 17, of which 11 were waited for; matrix products, arithmetic and copies ran while one was open for 6% of the time, Pallas kernels for 0%

profile of v7, /device:TPU:32, one launch (start us, length us, event | category | flops | bytes accessed | tf_op | source)
XLA Modules:
  0.0 192.2 jit_solution(16193762304135301685)
XLA Ops:
  0.6 1.1 fusion.39
  1.8 14.8 %collective-permute-start = (bf16[512,256]{0,1:T(8,128)(2,1)S(1)}, bf16[512,256]{0,1:T(8,128)(2,1)S(1)}, u32[]{:S(2)}, u32[]{:S(2)}) collective-permute-start(bf16[512,256]{0,1:T(8,128)(2,1)S(1)} %bitcast.80), channel_id=1, source_target_pairs={{0,1},{1,0},{2,3},{3,2},{4,5},{5,4},{6,7},{7,6},{8,9},{9,8},{10,11... | collective-permute-start | bytes 786440 | tf_op jit(solution)/shard_map/ppermute | solution.py:24
  16.7 3.4 %collective-permute-start.1 = (bf16[512,256]{0,1:T(8,128)(2,1)S(1)}, bf16[512,256]{0,1:T(8,128)(2,1)S(1)}, u32[]{:S(2)}, u32[]{:S(2)}) collective-permute-start(bf16[512,256]{0,1:T(8,128)(2,1)S(1)} %bitcast.81), channel_id=1, source_target_pairs={{0,2},{2,4},{4,6},{6,0},{1,3},{3,5},{5,7},{7,1},{8,10},{10,12},{12... | collective-permute-start | bytes 786440 | tf_op jit(solution)/shard_map/ppermute | solution.py:24
  20.1 4.6 %collective-permute-start.2 = (bf16[512,256]{0,1:T(8,128)(2,1)S(1)}, bf16[512,256]{0,1:T(8,128)(2,1)S(1)}, u32[]{:S(2)}, u32[]{:S(2)}) collective-permute-start(bf16[512,256]{0,1:T(8,128)(2,1)S(1)} %bitcast.82), channel_id=1, source_target_pairs={{0,4},{2,6},{4,0},{6,2},{1,5},{3,7},{5,1},{7,3},{8,12},{10,14},{12... | collective-permute-start | bytes 786440 | tf_op jit(solution)/shard_map/ppermute | solution.py:24
  24.7 3.3 %collective-permute-start.3 = (bf16[512,256]{0,1:T(8,128)(2,1)S(1)}, bf16[512,256]{0,1:T(8,128)(2,1)S(1)}, u32[]{:S(2)}, u32[]{:S(2)}) collective-permute-start(bf16[512,256]{0,1:T(8,128)(2,1)S(1)} %bitcast.83), channel_id=1, source_target_pairs={{0,6},{2,0},{4,2},{6,4},{1,7},{3,1},{5,3},{7,5},{8,14},{10,8},{12,... | collective-permute-start | bytes 786440 | tf_op jit(solution)/shard_map/ppermute | solution.py:24
  28.1 1.3 fusion.40
  29.4 1.9 collective-permute-start.4
  32.0 4.7 %collective-permute-done.4 = f32[1]{0:T(128)} collective-permute-done((f32[1]{0:T(128)}, f32[1]{0:T(128)}, u32[]{:S(2)}, u32[]{:S(2)}) %collective-permute-start.4) | collective-permute-done | bytes 36 | tf_op jit(solution)/shard_map/ppermute | solution.py:24
  37.9 2.1 %collective-permute-done = bf16[512,256]{0,1:T(8,128)(2,1)S(1)} collective-permute-done((bf16[512,256]{0,1:T(8,128)(2,1)S(1)}, bf16[512,256]{0,1:T(8,128)(2,1)S(1)}, u32[]{:S(2)}, u32[]{:S(2)}) %collective-permute-start) | collective-permute-done | bytes 262176 | tf_op jit(solution)/shard_map/ppermute | solution.py:24
  40.1 1.1 broadcast_in_dim.14
  41.1 4.3 %all-to-all-start = ((bf16[4,512,256]{1,2,0:T(8,128)(2,1)}), bf16[4,512,256]{1,2,0:T(8,128)(2,1)S(1)}, u32[]{:S(2)}, u32[]{:S(2)}) async-start(bf16[4,512,256]{1,2,0:T(8,128)(2,1)} %broadcast_in_dim.14), calls=%async_computation | async-start | bytes 2097152 | tf_op jit(solution)/shard_map/all_to_all | solution.py:33
  45.6 12.1 %collective-permute-start.8 = (bf16[512,256]{0,1:T(8,128)(2,1)S(1)}, bf16[512,256]{0,1:T(8,128)(2,1)}, u32[]{:S(2)}, u32[]{:S(2)}) collective-permute-start(bf16[512,256]{0,1:T(8,128)(2,1)S(1)} %bitcast.85), channel_id=1, source_target_pairs={{0,1},{1,0},{2,3},{3,2},{4,5},{5,4},{6,7},{7,6},{8,9},{9,8},{10,11... | collective-permute-start | bytes 786440 | tf_op jit(solution)/shard_map/ppermute | solution.py:24
  57.9 1.9 all-to-all-done
  60.1 1.0 copy-done.4
  61.1 0.6 copy-done.8
  61.7 0.4 copy-done.10
  62.1 0.9 multiply_reduce_fusion.2
  63.1 0.6 broadcast_in_dim.15
  63.7 12.1 %all-to-all-start.1 = ((f32[8,3,512]{2,1,0:T(4,128)}), f32[8,3,512]{2,1,0:T(4,128)S(1)}, u32[]{:S(2)}, u32[]{:S(2)}) async-start(f32[8,3,512]{2,1,0:T(4,128)} %broadcast_in_dim.15), calls=%async_computation.1 | async-start | bytes 131072 | tf_op jit(solution)/shard_map/all_to_all | solution.py:33
  76.4 1.0 collective-permute-done.8
  77.5 1.1 maximum_select_fusion.1
  78.6 5.2 %collective-permute-start.10 = (bf16[2,512,256]{1,2,0:T(8,128)(2,1)S(1)}, bf16[2,512,256]{1,2,0:T(8,128)(2,1)S(1)}, u32[]{:S(2)}, u32[]{:S(2)}) collective-permute-start(bf16[2,512,256]{1,2,0:T(8,128)(2,1)S(1)} %maximum_select_fusion.1), channel_id=1, source_target_pairs={{0,4},{2,6},{4,0},{6,2},{1,5},{3,7},{5,1},{7,3},{8,12},{10,14},{12... | collective-permute-start | bytes 1572872 | tf_op jit(solution)/shard_map/ppermute | solution.py:24
  83.7 4.2 %collective-permute-start.11 = (bf16[2,512,256]{1,2,0:T(8,128)(2,1)S(1)}, bf16[2,512,256]{1,2,0:T(8,128)(2,1)S(1)}, u32[]{:S(2)}, u32[]{:S(2)}) collective-permute-start(bf16[2,512,256]{1,2,0:T(8,128)(2,1)S(1)} %maximum_select_fusion.1), channel_id=1, source_target_pairs={{0,6},{2,0},{4,2},{6,4},{1,7},{3,1},{5,3},{7,5},{8,14},{10,8},{12,... | collective-permute-start | bytes 1572872 | tf_op jit(solution)/shard_map/ppermute | solution.py:24
  87.9 1.9 collective-permute-start.9
  89.8 1.2 all-to-all-done.1
  91.1 3.9 %multiply_convert_fusion.1 = (bf16[2048,288]{0,1:T(8,128)(2,1)S(1)}, f32[2048,288]{0,1:T(8,128)}) fusion(f32[]{:T(128)S(6)} %sub.56, bf16[512,2048]{0,1:T(8,128)(2,1)} %bitcast.79, f32[512,288]{0,1:T(8,128)S(1)} %get-tuple-element.49, f32[512]{0:T(512)S(1)} %bitcast.89, f32[512]{0:T(512)S(1)} %bitcast.88, f32[288]{0:T(512)S(1)} %copy-done.6, ...), kind=kOutput, calls=%fused_computation.4 | convolution fusion | flops 606486528 | bytes 6529028 | tf_op jit(solution)/shard_map/dot_general | solution.py:37
  95.0 1.9 collective-permute-start.5
  96.9 4.8 %collective-permute-start.6 = (f32[1]{0:T(128)}, f32[1]{0:T(128)}, u32[]{:S(2)}, u32[]{:S(2)}) collective-permute-start(f32[1]{0:T(128)} %mul.138), channel_id=1, source_target_pairs={{0,16},{8,24},{16,32},{24,40},{32,48},{40,56},{48,64},{56,72},{64,... | collective-permute-start | bytes 20 | tf_op jit(solution)/shard_map/ppermute | solution.py:24
  101.7 5.9 %collective-permute-done.11 = bf16[2,512,256]{1,2,0:T(8,128)(2,1)S(1)} collective-permute-done((bf16[2,512,256]{1,2,0:T(8,128)(2,1)S(1)}, bf16[2,512,256]{1,2,0:T(8,128)(2,1)S(1)}, u32[]{:S(2)}, u32[]{:S(2)}) %collective-permute-start.11) | collective-permute-done | bytes 524320 | tf_op jit(solution)/shard_map/ppermute | solution.py:24
  107.8 0.9 copy-done.2
  108.7 1.2 bitcast_dynamic-update-slice_fusion.1
  110.0 4.6 %collective-permute-done.5 = bf16[2048,288]{0,1:T(8,128)(2,1)S(1)} collective-permute-done((bf16[2048,288]{0,1:T(8,128)(2,1)S(1)}, bf16[2048,288]{0,1:T(8,128)(2,1)S(1)}, u32[]{:S(2)}, u32[]{:S(2)}) %collective-permute-start.5) | collective-permute-done | bytes 1179680 | tf_op jit(solution)/shard_map/ppermute | solution.py:24
  114.6 4.1 %multiply_reduce_fusion = (f32[512]{0:T(512)S(1)}, f32[512]{0:T(512)S(1)}, f32[512]{0:T(512)S(1)}, f32[512,288]{0,1:T(8,128)}) fusion(f32[288]{0:T(512)S(1)} %copy-done.6, bf16[2,512,288]{1,2,0:T(8,128)(2,1)S(1)} %copy-done.12, bf16[512,2048]{0,1:T(8,128)(2,1)S(1)} %bitcast.76, bf16[2048,288]{0,1:T(8,128)(2,1)S(1)} %copy-done.5, ...), kind=kOutput, calls=%fused_computation.26 | convolution fusion | flops 609581568 | bytes 8002696 | tf_op jit(solution)/shard_map/dot_general | solution.py:67
  118.8 0.6 broadcast_in_dim.20
  119.4 11.1 %all-to-all-start.2 = ((f32[8,3,512]{2,1,0:T(4,128)}), f32[8,3,512]{2,1,0:T(4,128)S(1)}, u32[]{:S(2)}, u32[]{:S(2)}) async-start(f32[8,3,512]{2,1,0:T(4,128)} %broadcast_in_dim.20), calls=%async_computation.2 | async-start | bytes 131072 | tf_op jit(solution)/shard_map/all_to_all | solution.py:33
  131.8 3.2 %collective-permute-start.7 = (f32[1]{0:T(128)}, f32[1]{0:T(128)}, u32[]{:S(2)}, u32[]{:S(2)}) collective-permute-start(f32[1]{0:T(128)} %add.82), channel_id=1, source_target_pairs={{0,496},{8,504},{16,0},{24,8},{32,16},{40,24},{48,32},{56,40},{64,... | collective-permute-start | bytes 20 | tf_op jit(solution)/shard_map/ppermute | solution.py:24
  135.7 1.5 collective-permute-done.7
  138.0 7.6 %all-to-all-done.2 = f32[8,3,512]{2,1,0:T(4,128)S(1)} async-done(((f32[8,3,512]{2,1,0:T(4,128)}), f32[8,3,512]{2,1,0:T(4,128)S(1)}, u32[]{:S(2)}, u32[]{:S(2)}) %all-to-all-start.2) | async-done | bytes 49184 | tf_op jit(solution)/shard_map/all_to_all | solution.py:33
  145.6 3.9 %multiply_convert_fusion = bf16[2048,288]{0,1:T(8,128)(2,1)S(1)} fusion(f32[]{:T(128)} %bitcast.18, bf16[512,2048]{0,1:T(8,128)(2,1)S(1)} %bitcast.77, f32[512,288]{0,1:T(8,128)} %get-tuple-element.52, bf16[2048,288]{0,1:T(8,128)(2,1)} %copy-done.7, f32[2048,288]{0,1:T(8,128)} %get-tuple-element.51, f32[]{:T(128)} %bitcast.3, f32[512]{0:T(512)S(1)} %bitcast.87, ...), kind=kOutput, calls=%fused_computation.1 | convolution fusion | flops 608845824 | bytes 7707904 | tf_op jit(solution)/shard_map/dot_general | solution.py:37
  149.5 0.8 copy.34
  150.4 1.9 collective-permute-start.12
  152.3 2.3 %collective-permute-done.12 = bf16[8,4,32,288]{3,2,1,0:T(8,128)(2,1)S(1)} collective-permute-done((bf16[8,4,32,288]{3,2,1,0:T(8,128)(2,1)S(1)}, bf16[8,4,32,288]{3,2,1,0:T(8,128)(2,1)S(1)}, u32[]{:S(2)}, u32[]{:S(2)}) %collective-permute-start.12) | collective-permute-done | bytes 589856 | tf_op jit(solution)/shard_map/ppermute | solution.py:24
  155.0 15.9 %all_to_all.25 = bf16[4,8,32,288]{3,2,1,0:T(8,128)(2,1)S(1)} all-to-all(bf16[4,8,32,288]{3,2,1,0:T(8,128)(2,1)S(1)} %copy.35), channel_id=1, replica_groups=mesh['z_lo'=8,'y'=4,'core'=2,'x'=4,'z_hi'=2] {'y'}, dimensions={0} | all-to-all | bytes 1179648 | tf_op jit(solution)/shard_map/all_to_all | solution.py:134
  170.9 0.9 reduce_sum.101
  171.8 5.6 %all-to-all-start.4 = ((bf16[8,32,288]{2,1,0:T(8,128)(2,1)}), bf16[8,32,288]{2,1,0:T(8,128)(2,1)S(1)}, u32[]{:S(2)}, u32[]{:S(2)}) async-start(bf16[8,32,288]{2,1,0:T(8,128)(2,1)} %reduce_sum.101), calls=%async_computation.4 | async-start | bytes 393216 | tf_op jit(solution)/shard_map/all_to_all | solution.py:136
  177.4 1.0 constant_dynamic-slice_fusion
  178.5 11.9 %all-to-all-done.4 = bf16[8,32,288]{2,1,0:T(8,128)(2,1)S(1)} async-done(((bf16[8,32,288]{2,1,0:T(8,128)(2,1)}), bf16[8,32,288]{2,1,0:T(8,128)(2,1)S(1)}, u32[]{:S(2)}, u32[]{:S(2)}) %all-to-all-start.4) | async-done | bytes 147488 | tf_op jit(solution)/shard_map/all_to_all | solution.py:136
  190.5 0.7 multiply_subtract_fusion
  (50 shorter events, 1.8 us)
Async XLA Ops:
  1.8 38.2 %collective-permute-start = (bf16[512,256]{0,1:T(8,128)(2,1)S(1)}, bf16[512,256]{0,1:T(8,128)(2,1)S(1)}, u32[]{:S(2)}, u32[]{:S(2)}) collective-permute-start(bf16[512,256]{0,1:T(8,128)(2,1)S(1)} %bitcast.80), channel_id=1, source_target_pairs={{0,1},{1,0},{2,3},{3,2},{4,5},{5,4},{6,7},{7,6},{8,9},{9,8},{10,11... | collective-permute-start | bytes 786440 | tf_op jit(solution)/shard_map/ppermute | solution.py:24
  16.7 23.4 %collective-permute-start.1 = (bf16[512,256]{0,1:T(8,128)(2,1)S(1)}, bf16[512,256]{0,1:T(8,128)(2,1)S(1)}, u32[]{:S(2)}, u32[]{:S(2)}) collective-permute-start(bf16[512,256]{0,1:T(8,128)(2,1)S(1)} %bitcast.81), channel_id=1, source_target_pairs={{0,2},{2,4},{4,6},{6,0},{1,3},{3,5},{5,7},{7,1},{8,10},{10,12},{12... | collective-permute-start | bytes 786440 | tf_op jit(solution)/shard_map/ppermute | solution.py:24
  20.1 20.0 %collective-permute-start.2 = (bf16[512,256]{0,1:T(8,128)(2,1)S(1)}, bf16[512,256]{0,1:T(8,128)(2,1)S(1)}, u32[]{:S(2)}, u32[]{:S(2)}) collective-permute-start(bf16[512,256]{0,1:T(8,128)(2,1)S(1)} %bitcast.82), channel_id=1, source_target_pairs={{0,4},{2,6},{4,0},{6,2},{1,5},{3,7},{5,1},{7,3},{8,12},{10,14},{12... | collective-permute-start | bytes 786440 | tf_op jit(solution)/shard_map/ppermute | solution.py:24
  24.7 15.3 %collective-permute-start.3 = (bf16[512,256]{0,1:T(8,128)(2,1)S(1)}, bf16[512,256]{0,1:T(8,128)(2,1)S(1)}, u32[]{:S(2)}, u32[]{:S(2)}) collective-permute-start(bf16[512,256]{0,1:T(8,128)(2,1)S(1)} %bitcast.83), channel_id=1, source_target_pairs={{0,6},{2,0},{4,2},{6,4},{1,7},{3,1},{5,3},{7,5},{8,14},{10,8},{12,... | collective-permute-start | bytes 786440 | tf_op jit(solution)/shard_map/ppermute | solution.py:24
  29.4 7.2 %collective-permute-start.4 = (f32[1]{0:T(128)}, f32[1]{0:T(128)}, u32[]{:S(2)}, u32[]{:S(2)}) collective-permute-start(f32[1]{0:T(128)} %bitcast.2), channel_id=1, source_target_pairs={{0,8},{8,16},{16,24},{24,32},{32,40},{40,48},{48,56},{56,64},{64,7... | collective-permute-start | bytes 20 | tf_op jit(solution)/shard_map/ppermute | solution.py:24
  41.1 18.6 %all-to-all-start = ((bf16[4,512,256]{1,2,0:T(8,128)(2,1)}), bf16[4,512,256]{1,2,0:T(8,128)(2,1)S(1)}, u32[]{:S(2)}, u32[]{:S(2)}) async-start(bf16[4,512,256]{1,2,0:T(8,128)(2,1)} %broadcast_in_dim.14), calls=%async_computation | async-start | bytes 2097152 | tf_op jit(solution)/shard_map/all_to_all | solution.py:33
  45.6 31.9 %collective-permute-start.8 = (bf16[512,256]{0,1:T(8,128)(2,1)S(1)}, bf16[512,256]{0,1:T(8,128)(2,1)}, u32[]{:S(2)}, u32[]{:S(2)}) collective-permute-start(bf16[512,256]{0,1:T(8,128)(2,1)S(1)} %bitcast.85), channel_id=1, source_target_pairs={{0,1},{1,0},{2,3},{3,2},{4,5},{5,4},{6,7},{7,6},{8,9},{9,8},{10,11... | collective-permute-start | bytes 786440 | tf_op jit(solution)/shard_map/ppermute | solution.py:24
  59.8 1.3 copy-start.4
  59.8 1.3 copy-start.6
  59.8 2.0 %copy-start.8 = (bf16[2,512,288]{1,2,0:T(8,128)(2,1)S(1)}, bf16[2,512,288]{1,2,0:T(8,128)(2,1)}, u32[]{:S(2)}) copy-start(bf16[2,512,288]{1,2,0:T(8,128)(2,1)} %param.8) | copy-start | bytes 1769476
  59.8 2.4 %copy-start.10 = (bf16[2,512,288]{1,2,0:T(8,128)(2,1)S(1)}, bf16[2,512,288]{1,2,0:T(8,128)(2,1)}, u32[]{:S(2)}) copy-start(bf16[2,512,288]{1,2,0:T(8,128)(2,1)} %param.9) | copy-start | bytes 1769476
  60.1 3.0 %copy-start = (bf16[4,2,512,256]{2,3,1,0:T(8,128)(2,1)}, bf16[4,2,512,256]{2,3,1,0:T(8,128)(2,1)S(1)}, u32[]{:S(2)}) copy-start(bf16[4,2,512,256]{2,3,1,0:T(8,128)(2,1)S(1)} %maximum_select_fusion) | copy-start | bytes 6291460
  62.1 28.9 %copy-start.11 = (bf16[2,512,288]{1,2,0:T(8,128)(2,1)S(1)}, bf16[2,512,288]{1,2,0:T(8,128)(2,1)}, u32[]{:S(2)}) copy-start(bf16[2,512,288]{1,2,0:T(8,128)(2,1)} %param.9) | copy-start | bytes 1769476
  63.7 27.3 %all-to-all-start.1 = ((f32[8,3,512]{2,1,0:T(4,128)}), f32[8,3,512]{2,1,0:T(4,128)S(1)}, u32[]{:S(2)}, u32[]{:S(2)}) async-start(f32[8,3,512]{2,1,0:T(4,128)} %broadcast_in_dim.15), calls=%async_computation.1 | async-start | bytes 131072 | tf_op jit(solution)/shard_map/all_to_all | solution.py:33
  78.6 23.2 %collective-permute-start.10 = (bf16[2,512,256]{1,2,0:T(8,128)(2,1)S(1)}, bf16[2,512,256]{1,2,0:T(8,128)(2,1)S(1)}, u32[]{:S(2)}, u32[]{:S(2)}) collective-permute-start(bf16[2,512,256]{1,2,0:T(8,128)(2,1)S(1)} %maximum_select_fusion.1), channel_id=1, source_target_pairs={{0,4},{2,6},{4,0},{6,2},{1,5},{3,7},{5,1},{7,3},{8,12},{10,14},{12... | collective-permute-start | bytes 1572872 | tf_op jit(solution)/shard_map/ppermute | solution.py:24
  83.7 23.9 %collective-permute-start.11 = (bf16[2,512,256]{1,2,0:T(8,128)(2,1)S(1)}, bf16[2,512,256]{1,2,0:T(8,128)(2,1)S(1)}, u32[]{:S(2)}, u32[]{:S(2)}) collective-permute-start(bf16[2,512,256]{1,2,0:T(8,128)(2,1)S(1)} %maximum_select_fusion.1), channel_id=1, source_target_pairs={{0,6},{2,0},{4,2},{6,4},{1,7},{3,1},{5,3},{7,5},{8,14},{10,8},{12,... | collective-permute-start | bytes 1572872 | tf_op jit(solution)/shard_map/ppermute | solution.py:24
  87.9 19.7 %collective-permute-start.9 = (bf16[2,512,256]{1,2,0:T(8,128)(2,1)S(1)}, bf16[2,512,256]{1,2,0:T(8,128)(2,1)}, u32[]{:S(2)}, u32[]{:S(2)}) collective-permute-start(bf16[2,512,256]{1,2,0:T(8,128)(2,1)S(1)} %maximum_select_fusion.1), channel_id=1, source_target_pairs={{0,2},{2,4},{4,6},{6,0},{1,3},{3,5},{5,7},{7,1},{8,10},{10,12},{12... | collective-permute-start | bytes 1572872 | tf_op jit(solution)/shard_map/ppermute | solution.py:24
  95.0 19.6 %collective-permute-start.5 = (bf16[2048,288]{0,1:T(8,128)(2,1)S(1)}, bf16[2048,288]{0,1:T(8,128)(2,1)S(1)}, u32[]{:S(2)}, u32[]{:S(2)}) collective-permute-start(bf16[2048,288]{0,1:T(8,128)(2,1)S(1)} %get-tuple-element.50), channel_id=1, source_target_pairs={{0,8},{8,16},{16,24},{24,32},{32,40},{40,48},{48,56},{56,64},{64,7... | collective-permute-start | bytes 3538952 | tf_op jit(solution)/shard_map/ppermute | solution.py:24
  96.9 13.1 %collective-permute-start.6 = (f32[1]{0:T(128)}, f32[1]{0:T(128)}, u32[]{:S(2)}, u32[]{:S(2)}) collective-permute-start(f32[1]{0:T(128)} %mul.138), channel_id=1, source_target_pairs={{0,16},{8,24},{16,32},{24,40},{32,48},{40,56},{48,64},{56,72},{64,... | collective-permute-start | bytes 20 | tf_op jit(solution)/shard_map/ppermute | solution.py:24
  101.7 5.9 %copy-start.1 = (bf16[2,512,256]{1,2,0:T(8,128)(2,1)}, bf16[2,512,256]{1,2,0:T(8,128)(2,1)S(1)}, u32[]{:S(2)}) copy-start(bf16[2,512,256]{1,2,0:T(8,128)(2,1)S(1)} %collective-permute-done.10) | copy-start | bytes 1572868
  107.6 1.0 copy-start.2
  108.7 6.0 %copy-start.5 = (bf16[2048,288]{0,1:T(8,128)(2,1)S(1)}, bf16[2048,288]{0,1:T(8,128)(2,1)}, u32[]{:S(2)}) copy-start(bf16[2048,288]{0,1:T(8,128)(2,1)} %param.11) | copy-start | bytes 3538948
  108.7 6.0 %copy-start.9 = (bf16[2,512,288]{1,2,0:T(8,128)(2,1)S(1)}, bf16[2,512,288]{1,2,0:T(8,128)(2,1)}, u32[]{:S(2)}) copy-start(bf16[2,512,288]{1,2,0:T(8,128)(2,1)} %param.8) | copy-start | bytes 1769476
  108.7 6.0 %copy-start.12 = (bf16[2,512,288]{1,2,0:T(8,128)(2,1)S(1)}, bf16[2,512,288]{1,2,0:T(8,128)(2,1)}, u32[]{:S(2)}) copy-start(bf16[2,512,288]{1,2,0:T(8,128)(2,1)} %param.9) | copy-start | bytes 1769476
  114.6 4.1 %copy-start.7 = (bf16[2048,288]{0,1:T(8,128)(2,1)}, bf16[2048,288]{0,1:T(8,128)(2,1)S(1)}, u32[]{:S(2)}) copy-start(bf16[2048,288]{0,1:T(8,128)(2,1)S(1)} %collective-permute-done.5) | copy-start | bytes 3538948
  119.4 26.2 %all-to-all-start.2 = ((f32[8,3,512]{2,1,0:T(4,128)}), f32[8,3,512]{2,1,0:T(4,128)S(1)}, u32[]{:S(2)}, u32[]{:S(2)}) async-start(f32[8,3,512]{2,1,0:T(4,128)} %broadcast_in_dim.20), calls=%async_computation.2 | async-start | bytes 131072 | tf_op jit(solution)/shard_map/all_to_all | solution.py:33
  131.8 5.4 %collective-permute-start.7 = (f32[1]{0:T(128)}, f32[1]{0:T(128)}, u32[]{:S(2)}, u32[]{:S(2)}) collective-permute-start(f32[1]{0:T(128)} %add.82), channel_id=1, source_target_pairs={{0,496},{8,504},{16,0},{24,8},{32,16},{40,24},{48,32},{56,40},{64,... | collective-permute-start | bytes 20 | tf_op jit(solution)/shard_map/ppermute | solution.py:24
  150.4 4.2 %collective-permute-start.12 = (bf16[8,4,32,288]{3,2,1,0:T(8,128)(2,1)S(1)}, bf16[8,4,32,288]{3,2,1,0:T(8,128)(2,1)S(1)}, u32[]{:S(2)}, u32[]{:S(2)}) collective-permute-start(bf16[8,4,32,288]{3,2,1,0:T(8,128)(2,1)S(1)} %select_bitcast_fusion), channel_id=1, source_target_pairs={{0,8},{8,0},{1,9},{9,1},{2,10},{10,2},{3,11},{11,3},{4,12},{12,4},... | collective-permute-start | bytes 1769480 | tf_op jit(solution)/shard_map/ppermute | solution.py:24
  155.0 35.4 %copy-start.3 = (f32[32,288]{1,0:T(8,128)S(1)}, f32[32,288]{1,0:T(8,128)}, u32[]{:S(2)}) copy-start(f32[32,288]{1,0:T(8,128)} %param.12) | copy-start | bytes 110596
  171.8 18.6 %all-to-all-start.4 = ((bf16[8,32,288]{2,1,0:T(8,128)(2,1)}), bf16[8,32,288]{2,1,0:T(8,128)(2,1)S(1)}, u32[]{:S(2)}, u32[]{:S(2)}) async-start(bf16[8,32,288]{2,1,0:T(8,128)(2,1)} %reduce_sum.101), calls=%async_computation.4 | async-start | bytes 393216 | tf_op jit(solution)/shard_map/all_to_all | solution.py:136

commit v8 on v6

--- a/solution.py
+++ b/solution.py
@@ -63,6 +63,18 @@
     return jnp.transpose(blocks, (2, 0, 1, 3)).reshape(TOK, 2048)
 
 
+def mass_neighbours(shares, before):
+    near = {k: shifted(shares, REP, -k) for k in (-3, -2, 1, 2)}
+    return {**near, -1: before, 0: shares}
+
+
+def masses(near):
+    mass1 = {k: near[k][0] + (1.0 - near[k - 1][0]) for k in (-2, 0, 2)}
+    mass2 = {k: near[k][1] * mass1[k] + (1.0 - near[k - 2][1]) * mass1[k - 2] for k in (0, 2)}
+    own = near[0][1]
+    return mass2[0], (own / mass2[0] + (1.0 - own) / mass2[2]) / lax.axis_size(REP)
+
+
 def forward(gathered, quotient, residual, targets, gain):
     output = residual.astype(F32) + jnp.dot(gathered, quotient, preferred_element_type=F32)
     scaled = gain * output
@@ -91,10 +103,11 @@
 
     other0 = shifted(context[0], "z_hi", 1)
     own0 = along_x(context[0])
-    before = shifted(shares[0], REP, 1)
-    other0, own0, before = lax.optimization_barrier((other0, own0, before))
-    wide0 = to_all(other0, "x")
+    other0, own0, late_shares = lax.optimization_barrier((other0, own0, shares))
+    before = shifted(late_shares[:, 0], REP, 1)
+    wide0, before = lax.optimization_barrier((to_all(other0, "x"), before))
     own0 = in_order(own0, x)
+    mass1 = shares[0, 0] + (1.0 - before[0])
     context1 = after(context[1], other0)
     other1 = shifted(context1, "z_hi", 1)
     gathered0 = laid_out(jnp.where(hi == 0, jnp.stack([own0, wide0], 1), jnp.stack([wide0, own0], 1)))
@@ -103,22 +116,19 @@
     output0, sums0 = forward(gathered0, slow_weight, residual[0], targets[0], gain)
     totals0 = jnp.sum(to_all(sums0, TP), axis=0)
     pair1 = by_half(context1, other1, hi)
-    both1 = in_order(along_x(after(pair1, sums0)), x)
+    both1 = in_order(lax.optimization_barrier(along_x(after(pair1, sums0))), x)
     gathered1 = laid_out(both1)
     grad0 = backward(output0, totals0, targets[0], gain)
     weight_grad0 = contract_rows(gathered0, grad0)
 
     pushed = ((1.0 - share0) * weight_grad0).astype(BF16)
     incoming = shifted(pushed, REP, 1)
-    mass_in = shifted((1.0 - shares[1]) * (shares[0] + (1.0 - before)), REP, 2)
-    incoming, mass_in = lax.optimization_barrier((incoming, mass_in))
-    mass1 = share0 + (1.0 - before[0])
     step0 = share0 * weight_grad0 + incoming.astype(F32)
     quotient1 = (anchor - (LR / mass1) * step0).astype(BF16)
     output1, sums1 = forward(gathered1, quotient1, residual[1], targets[1], gain)
-    mass2 = shares[1] * (shares[0] + (1.0 - before)) + mass_in
-    mass_later = shifted(mass2, REP, -2)
-    part = ((shares[1] / mass2 + (1.0 - shares[1]) / mass_later) / lax.axis_size(REP))[0]
+    near = mass_neighbours(shares[:, 0], before)
+    near = lax.optimization_barrier((near, sums1))[0]
+    mass2, part = masses(near)
     totals1 = jnp.sum(to_all(sums1, TP), axis=0)
     grad1 = backward(output1, totals1, targets[1], gain)
     weight_grad1 = contract_rows(gathered1, grad1)
@@ -138,7 +148,7 @@
     anchor_rows = lax.dynamic_slice_in_dim(slow_weight, lax.axis_index(REP) * 32, 32, 0)
     new_momentum = BETA * momentum + gradient
     new_weight = anchor_rows.astype(F32) - ALPHA * LR * new_momentum
-    return (new_weight, new_momentum, mass2)
+    return (new_weight, new_momentum, mass2[None])
 
 
 def solution(mesh):

time: 192 us -> 205 us (1.068)
  starting transfers between devices: 92.9 us -> 107 us
    all_to_all x1, starting transfers between devices: 5.64 us -> 17.1 us  [body(): parts = lax.all_to_all(total.astype(BF16), 'z_lo', 0, 0)]
    all_to_all x3, waiting for transfers between devices: 16.7 us -> 10.4 us  [to_all(): lax.all_to_all(jnp.broadcast_to(value[None], (count,) + value.shape), axi...]
    ppermute x13 -> x15, waiting for transfers between devices: 16.9 us -> 22.5 us  [shifted(): lax.ppermute(value, axis, [(i, (i + steps) % count) for i in range(count)])]
    ppermute x13 -> x15, starting transfers between devices: 64.3 us -> 68.7 us  [shifted(): lax.ppermute(value, axis, [(i, (i + steps) % count) for i in range(count)])]
    all_to_all x3, starting transfers between devices: 23 us -> 20.7 us  [to_all(): lax.all_to_all(jnp.broadcast_to(value[None], (count,) + value.shape), axi...]
    unnamed x25 -> x35, local copies, waits for them, and re-layouts: 2.46 us -> 4.54 us
    dynamic_update_slice x6, local copies, waits for them, and re-layouts: 2.28 us -> 0.19 us  [in_order(): lax.dynamic_update_slice_in_dim(placed, blocks[k][None], x - k & 3, 0)]
  transfers between devices with their start and end apart: 17 -> 19, of which waited for: 11 -> 9; matrix products, arithmetic and copies ran while one was open for 6% -> 7% of each run, Pallas kernels for 0% -> 0%
where the time goes in v8:
time: 205 us; the launch traced here: 204 us
  starting transfers between devices  107 us (52%)
  waiting for transfers between devices  44.9 us (22%)
  blocking collectives  17.3 us (8%)
  matrix products  12.5 us (6%)
  local copies, waits for them, and re-layouts  11.5 us (6%)
  between operations  7.68 us (4%)
  other arithmetic  3.47 us (2%)
    ppermute x15, starting transfers between devices, shifted(): lax.ppermute(value, axis, [(i, (i + steps) % count) for i in range(count)])  68.7 us
    ppermute x15, waiting for transfers between devices, shifted(): lax.ppermute(value, axis, [(i, (i + steps) % count) for i in range(count)])  22.5 us
    all_to_all x3, starting transfers between devices, to_all(): lax.all_to_all(jnp.broadcast_to(value[None], (count,) + value.shape), axi...  20.7 us
    all_to_all x1, blocking collectives, body(): parts = lax.all_to_all(parts, 'y', 0, 0)  17.3 us
    all_to_all x1, starting transfers between devices, body(): parts = lax.all_to_all(total.astype(BF16), 'z_lo', 0, 0)  17.1 us
    all_to_all x1, waiting for transfers between devices, body(): parts = lax.all_to_all(total.astype(BF16), 'z_lo', 0, 0)  12 us
    all_to_all x3, waiting for transfers between devices, to_all(): lax.all_to_all(jnp.broadcast_to(value[None], (count,) + value.shape), axi...  10.4 us
    dot_general x2, matrix products, contract_rows(): lax.dot_general(left, right, (((0,), (0,)), ((), ())), preferred_element_...  7.63 us
  transfers between devices with their start and end apart: 19, of which 9 were waited for; matrix products, arithmetic and copies ran while one was open for 7% of the time, Pallas kernels for 0%

profile of v8, /device:TPU:32, one launch (start us, length us, event | category | flops | bytes accessed | tf_op | source)
XLA Modules:
  0.0 203.8 jit_solution(14074627123467087442)
XLA Ops:
  0.6 1.1 fusion.39
  1.9 14.8 %collective-permute-start.2 = (bf16[512,256]{0,1:T(8,128)(2,1)S(1)}, bf16[512,256]{0,1:T(8,128)(2,1)S(1)}, u32[]{:S(2)}, u32[]{:S(2)}) collective-permute-start(bf16[512,256]{0,1:T(8,128)(2,1)S(1)} %bitcast.89), channel_id=1, source_target_pairs={{0,1},{1,0},{2,3},{3,2},{4,5},{5,4},{6,7},{7,6},{8,9},{9,8},{10,11... | collective-permute-start | bytes 786440 | tf_op jit(solution)/shard_map/ppermute | solution.py:24
  16.7 3.4 %collective-permute-start.3 = (bf16[512,256]{0,1:T(8,128)(2,1)S(1)}, bf16[512,256]{0,1:T(8,128)(2,1)S(1)}, u32[]{:S(2)}, u32[]{:S(2)}) collective-permute-start(bf16[512,256]{0,1:T(8,128)(2,1)S(1)} %bitcast.90), channel_id=1, source_target_pairs={{0,2},{2,4},{4,6},{6,0},{1,3},{3,5},{5,7},{7,1},{8,10},{10,12},{12... | collective-permute-start | bytes 786440 | tf_op jit(solution)/shard_map/ppermute | solution.py:24
  20.1 4.6 %collective-permute-start.4 = (bf16[512,256]{0,1:T(8,128)(2,1)S(1)}, bf16[512,256]{0,1:T(8,128)(2,1)S(1)}, u32[]{:S(2)}, u32[]{:S(2)}) collective-permute-start(bf16[512,256]{0,1:T(8,128)(2,1)S(1)} %bitcast.91), channel_id=1, source_target_pairs={{0,4},{2,6},{4,0},{6,2},{1,5},{3,7},{5,1},{7,3},{8,12},{10,14},{12... | collective-permute-start | bytes 786440 | tf_op jit(solution)/shard_map/ppermute | solution.py:24
  24.7 3.3 %collective-permute-start.5 = (bf16[512,256]{0,1:T(8,128)(2,1)S(1)}, bf16[512,256]{0,1:T(8,128)(2,1)S(1)}, u32[]{:S(2)}, u32[]{:S(2)}) collective-permute-start(bf16[512,256]{0,1:T(8,128)(2,1)S(1)} %bitcast.92), channel_id=1, source_target_pairs={{0,6},{2,0},{4,2},{6,4},{1,7},{3,1},{5,3},{7,5},{8,14},{10,8},{12,... | collective-permute-start | bytes 786440 | tf_op jit(solution)/shard_map/ppermute | solution.py:24
  28.1 12.0 %collective-permute-done.2 = bf16[512,256]{0,1:T(8,128)(2,1)S(1)} collective-permute-done((bf16[512,256]{0,1:T(8,128)(2,1)S(1)}, bf16[512,256]{0,1:T(8,128)(2,1)S(1)}, u32[]{:S(2)}, u32[]{:S(2)}) %collective-permute-start.2) | collective-permute-done | bytes 262176 | tf_op jit(solution)/shard_map/ppermute | solution.py:24
  40.1 1.1 broadcast_in_dim.16
  41.1 4.3 %all-to-all-start = ((bf16[4,512,256]{1,2,0:T(8,128)(2,1)}), bf16[4,512,256]{1,2,0:T(8,128)(2,1)S(1)}, u32[]{:S(2)}, u32[]{:S(2)}) async-start(bf16[4,512,256]{1,2,0:T(8,128)(2,1)} %broadcast_in_dim.16), calls=%async_computation | async-start | bytes 2097152 | tf_op jit(solution)/shard_map/all_to_all | solution.py:33
  45.6 12.1 %collective-permute-start.9 = (bf16[512,256]{0,1:T(8,128)(2,1)S(1)}, bf16[512,256]{0,1:T(8,128)(2,1)}, u32[]{:S(2)}, u32[]{:S(2)}) collective-permute-start(bf16[512,256]{0,1:T(8,128)(2,1)S(1)} %bitcast.94), channel_id=1, source_target_pairs={{0,1},{1,0},{2,3},{3,2},{4,5},{5,4},{6,7},{7,6},{8,9},{9,8},{10,11... | collective-permute-start | bytes 786440 | tf_op jit(solution)/shard_map/ppermute | solution.py:24
  57.7 1.9 collective-permute-start.6
  59.8 4.9 %collective-permute-done.6 = f32[2]{0:T(128)S(1)} collective-permute-done((f32[2]{0:T(128)S(1)}, f32[2]{0:T(128)S(1)}, u32[]{:S(2)}, u32[]{:S(2)}) %collective-permute-start.6) | collective-permute-done | bytes 40 | tf_op jit(solution)/shard_map/ppermute | solution.py:24
  65.1 1.0 copy-done.6
  66.1 0.7 copy-done.10
  67.1 1.7 multiply_reduce_fusion.2
  68.9 0.6 broadcast_in_dim.21
  69.5 7.1 %all-to-all-start.1 = ((f32[8,3,512]{2,1,0:T(4,128)}), f32[8,3,512]{2,1,0:T(4,128)S(1)}, u32[]{:S(2)}, u32[]{:S(2)}) async-start(f32[8,3,512]{2,1,0:T(4,128)} %broadcast_in_dim.21), calls=%async_computation.1 | async-start | bytes 131072 | tf_op jit(solution)/shard_map/all_to_all | solution.py:33
  76.6 0.6 collective-permute-done.9
  77.2 1.1 maximum_select_fusion.1
  78.3 4.3 %collective-permute-start.10 = (bf16[2,512,256]{1,2,0:T(8,128)(2,1)S(1)}, bf16[2,512,256]{1,2,0:T(8,128)(2,1)S(1)}, u32[]{:S(2)}, u32[]{:S(2)}) collective-permute-start(bf16[2,512,256]{1,2,0:T(8,128)(2,1)S(1)} %maximum_select_fusion.1), channel_id=1, source_target_pairs={{0,2},{2,4},{4,6},{6,0},{1,3},{3,5},{5,7},{7,1},{8,10},{10,12},{12... | collective-permute-start | bytes 1572872 | tf_op jit(solution)/shard_map/ppermute | solution.py:24
  82.6 4.0 %collective-permute-start.11 = (bf16[2,512,256]{1,2,0:T(8,128)(2,1)S(1)}, bf16[2,512,256]{1,2,0:T(8,128)(2,1)S(1)}, u32[]{:S(2)}, u32[]{:S(2)}) collective-permute-start(bf16[2,512,256]{1,2,0:T(8,128)(2,1)S(1)} %maximum_select_fusion.1), channel_id=1, source_target_pairs={{0,4},{2,6},{4,0},{6,2},{1,5},{3,7},{5,1},{7,3},{8,12},{10,14},{12... | collective-permute-start | bytes 1572872 | tf_op jit(solution)/shard_map/ppermute | solution.py:24
  86.6 3.4 %collective-permute-start.12 = (bf16[2,512,256]{1,2,0:T(8,128)(2,1)S(1)}, bf16[2,512,256]{1,2,0:T(8,128)(2,1)S(1)}, u32[]{:S(2)}, u32[]{:S(2)}) collective-permute-start(bf16[2,512,256]{1,2,0:T(8,128)(2,1)S(1)} %maximum_select_fusion.1), channel_id=1, source_target_pairs={{0,6},{2,0},{4,2},{6,4},{1,7},{3,1},{5,3},{7,5},{8,14},{10,8},{12,... | collective-permute-start | bytes 1572872 | tf_op jit(solution)/shard_map/ppermute | solution.py:24
  90.0 1.8 all-to-all-done.1
  91.8 4.4 %multiply_convert_fusion = (bf16[2048,288]{0,1:T(8,128)(2,1)}, f32[2048,288]{0,1:T(8,128)}) fusion(f32[]{:T(128)S(6)} %sub.81, bf16[512,2048]{0,1:T(8,128)(2,1)} %bitcast.88, f32[512,288]{0,1:T(8,128)} %get-tuple-element.63, f32[512]{0:T(512)S(1)} %bitcast.98, f32[512]{0:T(512)S(1)} %bitcast.97, f32[288]{0:T(512)S(1)} %broadcast_multiply_fusion, ...), kind=kOutput, calls=%fused_computation.5 | convolution fusion | flops 606486528 | bytes 6529028 | tf_op jit(solution)/shard_map/dot_general | solution.py:37
  96.2 1.9 collective-permute-start.13
  98.1 4.8 %collective-permute-start = (f32[2]{0:T(128)S(1)}, f32[2]{0:T(128)S(1)}, u32[]{:S(2)}, u32[]{:S(2)}) collective-permute-start(f32[2]{0:T(128)S(1)} %bitcast.107), channel_id=1, source_target_pairs={{0,24},{8,32},{16,40},{24,48},{32,56},{40,64},{48,72},{56,80},{64,... | collective-permute-start | bytes 32 | tf_op jit(solution)/shard_map/ppermute | solution.py:24
  103.0 3.2 %collective-permute-start.1 = (f32[2]{0:T(128)S(1)}, f32[2]{0:T(128)S(1)}, u32[]{:S(2)}, u32[]{:S(2)}) collective-permute-start(f32[2]{0:T(128)S(1)} %bitcast.109), channel_id=1, source_target_pairs={{0,16},{8,24},{16,32},{24,40},{32,48},{40,56},{48,64},{56,72},{64,... | collective-permute-start | bytes 32 | tf_op jit(solution)/shard_map/ppermute | solution.py:24
  106.2 1.6 collective-permute-done.11
  107.8 3.0 %collective-permute-start.7 = (f32[2]{0:T(128)S(1)}, f32[2]{0:T(128)S(1)}, u32[]{:S(2)}, u32[]{:S(2)}) collective-permute-start(f32[2]{0:T(128)S(1)} %bitcast.110), channel_id=1, source_target_pairs={{0,504},{8,0},{16,8},{24,16},{32,24},{40,32},{48,40},{56,48},{64,5... | collective-permute-start | bytes 32 | tf_op jit(solution)/shard_map/ppermute | solution.py:24
  110.8 0.8 copy-done.1
  111.6 2.1 %collective-permute-start.8 = (f32[2]{0:T(128)S(1)}, f32[2]{0:T(128)S(1)}, u32[]{:S(2)}, u32[]{:S(2)}) collective-permute-start(f32[2]{0:T(128)S(1)} %bitcast.111), channel_id=1, source_target_pairs={{0,496},{8,504},{16,0},{24,8},{32,16},{40,24},{48,32},{56,40},{64,... | collective-permute-start | bytes 32 | tf_op jit(solution)/shard_map/ppermute | solution.py:24
  114.0 0.8 copy-done.4
  115.0 1.2 collective-permute-done.13
  116.6 3.1 %multiply_reduce_fusion = (f32[512]{0:T(512)S(1)}, f32[512]{0:T(512)S(1)}, f32[512]{0:T(512)S(1)}, f32[512,288]{0,1:T(8,128)}) fusion(f32[288]{0:T(512)S(1)} %copy-done.8, bf16[2,512,288]{1,2,0:T(8,128)(2,1)S(1)} %copy-done.14, bf16[512,2048]{0,1:T(8,128)(2,1)S(1)} %bitcast.85, bf16[2048,288]{0,1:T(8,128)(2,1)S(1)} %copy-done.7, ...), kind=kOutput, calls=%fused_computation.27 | convolution fusion | flops 609581568 | bytes 8002696 | tf_op jit(solution)/shard_map/dot_general | solution.py:79
  119.8 0.6 broadcast_in_dim.22
  120.4 9.4 %all-to-all-start.2 = ((f32[8,3,512]{2,1,0:T(4,128)}), f32[8,3,512]{2,1,0:T(4,128)S(1)}, u32[]{:S(2)}, u32[]{:S(2)}) async-start(f32[8,3,512]{2,1,0:T(4,128)} %broadcast_in_dim.22), calls=%async_computation.2 | async-start | bytes 131072 | tf_op jit(solution)/shard_map/all_to_all | solution.py:33
  129.8 0.6 fusion.42
  132.3 0.6 fusion.40
  136.3 8.6 %all-to-all-done.2 = f32[8,3,512]{2,1,0:T(4,128)S(1)} async-done(((f32[8,3,512]{2,1,0:T(4,128)}), f32[8,3,512]{2,1,0:T(4,128)S(1)}, u32[]{:S(2)}, u32[]{:S(2)}) %all-to-all-start.2) | async-done | bytes 49184 | tf_op jit(solution)/shard_map/all_to_all | solution.py:33
  144.9 3.2 %fusion.1 = bf16[2048,288]{0,1:T(8,128)(2,1)S(1)} fusion(bf16[512,2048]{0,1:T(8,128)(2,1)S(1)} %bitcast.86, bf16[2048,288]{0,1:T(8,128)(2,1)} %collective-permute-done.13, f32[2048,288]{0,1:T(8,128)} %get-tuple-element.65, f32[]{:T(128)S(6)} %div.99, f32[]{:T(128)S(1)} %bitcast.114, f32[512,288]{0,1:T(8,128)} %get-tuple-element.66, f32[512]{0:T(512)S(1)} %bitcast.96, ...), kind=kOutput, calls=%fused_computation.2 | convolution fusion | flops 608845824 | bytes 7706888 | tf_op jit(solution)/shard_map/dot_general | solution.py:37
  148.1 0.8 copy.34
  149.1 1.9 collective-permute-start.14
  151.0 2.3 %collective-permute-done.14 = bf16[8,4,32,288]{3,2,1,0:T(8,128)(2,1)S(1)} collective-permute-done((bf16[8,4,32,288]{3,2,1,0:T(8,128)(2,1)S(1)}, bf16[8,4,32,288]{3,2,1,0:T(8,128)(2,1)S(1)}, u32[]{:S(2)}, u32[]{:S(2)}) %collective-permute-start.14) | collective-permute-done | bytes 589856 | tf_op jit(solution)/shard_map/ppermute | solution.py:24
  153.7 17.3 %all_to_all.25 = bf16[4,8,32,288]{3,2,1,0:T(8,128)(2,1)S(1)} all-to-all(bf16[4,8,32,288]{3,2,1,0:T(8,128)(2,1)S(1)} %copy.35), channel_id=1, replica_groups=mesh['z_lo'=8,'y'=4,'core'=2,'x'=4,'z_hi'=2] {'y'}, dimensions={0} | all-to-all | bytes 1179648 | tf_op jit(solution)/shard_map/all_to_all | solution.py:143
  171.0 0.9 reduce_sum.101
  171.8 17.1 %all-to-all-start.4 = ((bf16[8,32,288]{2,1,0:T(8,128)(2,1)}), bf16[8,32,288]{2,1,0:T(8,128)(2,1)S(1)}, u32[]{:S(2)}, u32[]{:S(2)}) async-start(bf16[8,32,288]{2,1,0:T(8,128)(2,1)} %reduce_sum.101), calls=%async_computation.4 | async-start | bytes 393216 | tf_op jit(solution)/shard_map/all_to_all | solution.py:145
  188.9 1.0 constant_dynamic-slice_fusion
  190.0 12.0 %all-to-all-done.4 = bf16[8,32,288]{2,1,0:T(8,128)(2,1)S(1)} async-done(((bf16[8,32,288]{2,1,0:T(8,128)(2,1)}), bf16[8,32,288]{2,1,0:T(8,128)(2,1)S(1)}, u32[]{:S(2)}, u32[]{:S(2)}) %all-to-all-start.4) | async-done | bytes 147488 | tf_op jit(solution)/shard_map/all_to_all | solution.py:145
  202.0 0.7 multiply_subtract_fusion
  (61 shorter events, 2.7 us)
Async XLA Ops:
  1.8 55.9 %copy-start.9 = (f32[2,1]{0,1:T(1,128)S(1)}, f32[2,1]{0,1:T(1,128)}, u32[]{:S(2)}) copy-start(f32[2,1]{0,1:T(1,128)} %param.13) | copy-start | bytes 28
  1.9 38.2 %collective-permute-start.2 = (bf16[512,256]{0,1:T(8,128)(2,1)S(1)}, bf16[512,256]{0,1:T(8,128)(2,1)S(1)}, u32[]{:S(2)}, u32[]{:S(2)}) collective-permute-start(bf16[512,256]{0,1:T(8,128)(2,1)S(1)} %bitcast.89), channel_id=1, source_target_pairs={{0,1},{1,0},{2,3},{3,2},{4,5},{5,4},{6,7},{7,6},{8,9},{9,8},{10,11... | collective-permute-start | bytes 786440 | tf_op jit(solution)/shard_map/ppermute | solution.py:24
  16.7 23.4 %collective-permute-start.3 = (bf16[512,256]{0,1:T(8,128)(2,1)S(1)}, bf16[512,256]{0,1:T(8,128)(2,1)S(1)}, u32[]{:S(2)}, u32[]{:S(2)}) collective-permute-start(bf16[512,256]{0,1:T(8,128)(2,1)S(1)} %bitcast.90), channel_id=1, source_target_pairs={{0,2},{2,4},{4,6},{6,0},{1,3},{3,5},{5,7},{7,1},{8,10},{10,12},{12... | collective-permute-start | bytes 786440 | tf_op jit(solution)/shard_map/ppermute | solution.py:24
  20.1 20.0 %collective-permute-start.4 = (bf16[512,256]{0,1:T(8,128)(2,1)S(1)}, bf16[512,256]{0,1:T(8,128)(2,1)S(1)}, u32[]{:S(2)}, u32[]{:S(2)}) collective-permute-start(bf16[512,256]{0,1:T(8,128)(2,1)S(1)} %bitcast.91), channel_id=1, source_target_pairs={{0,4},{2,6},{4,0},{6,2},{1,5},{3,7},{5,1},{7,3},{8,12},{10,14},{12... | collective-permute-start | bytes 786440 | tf_op jit(solution)/shard_map/ppermute | solution.py:24
  24.7 15.3 %collective-permute-start.5 = (bf16[512,256]{0,1:T(8,128)(2,1)S(1)}, bf16[512,256]{0,1:T(8,128)(2,1)S(1)}, u32[]{:S(2)}, u32[]{:S(2)}) collective-permute-start(bf16[512,256]{0,1:T(8,128)(2,1)S(1)} %bitcast.92), channel_id=1, source_target_pairs={{0,6},{2,0},{4,2},{6,4},{1,7},{3,1},{5,3},{7,5},{8,14},{10,8},{12,... | collective-permute-start | bytes 786440 | tf_op jit(solution)/shard_map/ppermute | solution.py:24
  41.1 23.6 %all-to-all-start = ((bf16[4,512,256]{1,2,0:T(8,128)(2,1)}), bf16[4,512,256]{1,2,0:T(8,128)(2,1)S(1)}, u32[]{:S(2)}, u32[]{:S(2)}) async-start(bf16[4,512,256]{1,2,0:T(8,128)(2,1)} %broadcast_in_dim.16), calls=%async_computation | async-start | bytes 2097152 | tf_op jit(solution)/shard_map/all_to_all | solution.py:33
  45.6 31.7 %collective-permute-start.9 = (bf16[512,256]{0,1:T(8,128)(2,1)S(1)}, bf16[512,256]{0,1:T(8,128)(2,1)}, u32[]{:S(2)}, u32[]{:S(2)}) collective-permute-start(bf16[512,256]{0,1:T(8,128)(2,1)S(1)} %bitcast.94), channel_id=1, source_target_pairs={{0,1},{1,0},{2,3},{3,2},{4,5},{5,4},{6,7},{7,6},{8,9},{9,8},{10,11... | collective-permute-start | bytes 786440 | tf_op jit(solution)/shard_map/ppermute | solution.py:24
  57.7 7.0 %collective-permute-start.6 = (f32[2]{0:T(128)S(1)}, f32[2]{0:T(128)S(1)}, u32[]{:S(2)}, u32[]{:S(2)}) collective-permute-start(f32[2]{0:T(128)S(1)} %bitcast.105), channel_id=1, source_target_pairs={{0,8},{8,16},{16,24},{24,32},{32,40},{40,48},{48,56},{56,64},{64,7... | collective-permute-start | bytes 32 | tf_op jit(solution)/shard_map/ppermute | solution.py:24
  64.8 1.3 copy-start.6
  64.8 1.3 copy-start.8
  64.8 2.0 copy-start.10
  64.8 2.4 %copy-start.12 = (bf16[2,512,288]{1,2,0:T(8,128)(2,1)S(1)}, bf16[2,512,288]{1,2,0:T(8,128)(2,1)}, u32[]{:S(2)}) copy-start(bf16[2,512,288]{1,2,0:T(8,128)(2,1)} %param.9) | copy-start | bytes 1769476
  65.1 3.8 %copy-start = (bf16[4,2,512,256]{2,3,1,0:T(8,128)(2,1)}, bf16[4,2,512,256]{2,3,1,0:T(8,128)(2,1)S(1)}, u32[]{:S(2)}) copy-start(bf16[4,2,512,256]{2,3,1,0:T(8,128)(2,1)S(1)} %maximum_select_fusion) | copy-start | bytes 6291460
  67.1 24.7 %copy-start.13 = (bf16[2,512,288]{1,2,0:T(8,128)(2,1)S(1)}, bf16[2,512,288]{1,2,0:T(8,128)(2,1)}, u32[]{:S(2)}) copy-start(bf16[2,512,288]{1,2,0:T(8,128)(2,1)} %param.9) | copy-start | bytes 1769476
  69.5 22.2 %all-to-all-start.1 = ((f32[8,3,512]{2,1,0:T(4,128)}), f32[8,3,512]{2,1,0:T(4,128)S(1)}, u32[]{:S(2)}, u32[]{:S(2)}) async-start(f32[8,3,512]{2,1,0:T(4,128)} %broadcast_in_dim.21), calls=%async_computation.1 | async-start | bytes 131072 | tf_op jit(solution)/shard_map/all_to_all | solution.py:33
  78.3 24.7 %collective-permute-start.10 = (bf16[2,512,256]{1,2,0:T(8,128)(2,1)S(1)}, bf16[2,512,256]{1,2,0:T(8,128)(2,1)S(1)}, u32[]{:S(2)}, u32[]{:S(2)}) collective-permute-start(bf16[2,512,256]{1,2,0:T(8,128)(2,1)S(1)} %maximum_select_fusion.1), channel_id=1, source_target_pairs={{0,2},{2,4},{4,6},{6,0},{1,3},{3,5},{5,7},{7,1},{8,10},{10,12},{12... | collective-permute-start | bytes 1572872 | tf_op jit(solution)/shard_map/ppermute | solution.py:24
  82.6 25.2 %collective-permute-start.11 = (bf16[2,512,256]{1,2,0:T(8,128)(2,1)S(1)}, bf16[2,512,256]{1,2,0:T(8,128)(2,1)S(1)}, u32[]{:S(2)}, u32[]{:S(2)}) collective-permute-start(bf16[2,512,256]{1,2,0:T(8,128)(2,1)S(1)} %maximum_select_fusion.1), channel_id=1, source_target_pairs={{0,4},{2,6},{4,0},{6,2},{1,5},{3,7},{5,1},{7,3},{8,12},{10,14},{12... | collective-permute-start | bytes 1572872 | tf_op jit(solution)/shard_map/ppermute | solution.py:24
  86.6 24.2 %collective-permute-start.12 = (bf16[2,512,256]{1,2,0:T(8,128)(2,1)S(1)}, bf16[2,512,256]{1,2,0:T(8,128)(2,1)S(1)}, u32[]{:S(2)}, u32[]{:S(2)}) collective-permute-start(bf16[2,512,256]{1,2,0:T(8,128)(2,1)S(1)} %maximum_select_fusion.1), channel_id=1, source_target_pairs={{0,6},{2,0},{4,2},{6,4},{1,7},{3,1},{5,3},{7,5},{8,14},{10,8},{12,... | collective-permute-start | bytes 1572872 | tf_op jit(solution)/shard_map/ppermute | solution.py:24
  96.2 20.0 %collective-permute-start.13 = (bf16[2048,288]{0,1:T(8,128)(2,1)}, bf16[2048,288]{0,1:T(8,128)(2,1)}, u32[]{:S(2)}, u32[]{:S(2)}) collective-permute-start(bf16[2048,288]{0,1:T(8,128)(2,1)} %get-tuple-element.64), channel_id=1, source_target_pairs={{0,8},{8,16},{16,24},{24,32},{32,40},{40,48},{48,56},{56,64},{64,7... | collective-permute-start | bytes 3538952 | tf_op jit(solution)/shard_map/ppermute | solution.py:24
  98.1 21.6 %collective-permute-start = (f32[2]{0:T(128)S(1)}, f32[2]{0:T(128)S(1)}, u32[]{:S(2)}, u32[]{:S(2)}) collective-permute-start(f32[2]{0:T(128)S(1)} %bitcast.107), channel_id=1, source_target_pairs={{0,24},{8,32},{16,40},{24,48},{32,56},{40,64},{48,72},{56,80},{64,... | collective-permute-start | bytes 32 | tf_op jit(solution)/shard_map/ppermute | solution.py:24
  103.0 16.7 %collective-permute-start.1 = (f32[2]{0:T(128)S(1)}, f32[2]{0:T(128)S(1)}, u32[]{:S(2)}, u32[]{:S(2)}) collective-permute-start(f32[2]{0:T(128)S(1)} %bitcast.109), channel_id=1, source_target_pairs={{0,16},{8,24},{16,32},{24,40},{32,48},{40,56},{48,64},{56,72},{64,... | collective-permute-start | bytes 32 | tf_op jit(solution)/shard_map/ppermute | solution.py:24
  107.8 3.0 %copy-start.3 = (bf16[2,512,256]{1,2,0:T(8,128)(2,1)}, bf16[2,512,256]{1,2,0:T(8,128)(2,1)S(1)}, u32[]{:S(2)}) copy-start(bf16[2,512,256]{1,2,0:T(8,128)(2,1)S(1)} %collective-permute-done.11) | copy-start | bytes 1572868
  107.8 11.9 %collective-permute-start.7 = (f32[2]{0:T(128)S(1)}, f32[2]{0:T(128)S(1)}, u32[]{:S(2)}, u32[]{:S(2)}) collective-permute-start(f32[2]{0:T(128)S(1)} %bitcast.110), channel_id=1, source_target_pairs={{0,504},{8,0},{16,8},{24,16},{32,24},{40,32},{48,40},{56,48},{64,5... | collective-permute-start | bytes 32 | tf_op jit(solution)/shard_map/ppermute | solution.py:24
  110.8 0.8 copy-start.1
  111.6 8.1 %collective-permute-start.8 = (f32[2]{0:T(128)S(1)}, f32[2]{0:T(128)S(1)}, u32[]{:S(2)}, u32[]{:S(2)}) collective-permute-start(f32[2]{0:T(128)S(1)} %bitcast.111), channel_id=1, source_target_pairs={{0,496},{8,504},{16,0},{24,8},{32,16},{40,24},{48,32},{56,40},{64,... | collective-permute-start | bytes 32 | tf_op jit(solution)/shard_map/ppermute | solution.py:24
  113.8 1.0 copy-start.4
  113.8 1.2 copy-start.2
  113.8 2.4 %copy-start.15 = (f32[2048,288]{0,1:T(8,128)S(1)}, f32[2048,288]{0,1:T(8,128)}, u32[]{:S(2)}) copy-start(f32[2048,288]{0,1:T(8,128)} %get-tuple-element.65) | copy-start | bytes 7077892
  114.8 1.5 copy-start.7
  114.8 1.6 copy-start.11
  114.8 1.8 copy-start.14
  120.4 24.4 %all-to-all-start.2 = ((f32[8,3,512]{2,1,0:T(4,128)}), f32[8,3,512]{2,1,0:T(4,128)S(1)}, u32[]{:S(2)}, u32[]{:S(2)}) async-start(f32[8,3,512]{2,1,0:T(4,128)} %broadcast_in_dim.22), calls=%async_computation.2 | async-start | bytes 131072 | tf_op jit(solution)/shard_map/all_to_all | solution.py:33
  149.1 4.2 %collective-permute-start.14 = (bf16[8,4,32,288]{3,2,1,0:T(8,128)(2,1)S(1)}, bf16[8,4,32,288]{3,2,1,0:T(8,128)(2,1)S(1)}, u32[]{:S(2)}, u32[]{:S(2)}) collective-permute-start(bf16[8,4,32,288]{3,2,1,0:T(8,128)(2,1)S(1)} %select_bitcast_fusion), channel_id=1, source_target_pairs={{0,8},{8,0},{1,9},{9,1},{2,10},{10,2},{3,11},{11,3},{4,12},{12,4},... | collective-permute-start | bytes 1769480 | tf_op jit(solution)/shard_map/ppermute | solution.py:24
  153.7 48.3 %copy-start.5 = (f32[32,288]{1,0:T(8,128)S(1)}, f32[32,288]{1,0:T(8,128)}, u32[]{:S(2)}) copy-start(f32[32,288]{1,0:T(8,128)} %param.12) | copy-start | bytes 110596
  171.8 30.2 %all-to-all-start.4 = ((bf16[8,32,288]{2,1,0:T(8,128)(2,1)}), bf16[8,32,288]{2,1,0:T(8,128)(2,1)S(1)}, u32[]{:S(2)}, u32[]{:S(2)}) async-start(bf16[8,32,288]{2,1,0:T(8,128)(2,1)} %reduce_sum.101), calls=%async_computation.4 | async-start | bytes 393216 | tf_op jit(solution)/shard_map/all_to_all | solution.py:145

commit v9 on v7

--- a/solution.py
+++ b/solution.py
@@ -48,7 +48,12 @@
     return [value] + [shifted(value, "x", k) for k in (1, 2, 3)]
 
 
-def in_order(blocks, x):
+def in_order(blocks, x, together=()):
+    blocks = list(blocks)
+    if together:
+        waited = lax.optimization_barrier(tuple(blocks[k] for k in together))
+        for k, block in zip(together, waited):
+            blocks[k] = block
     placed = jnp.broadcast_to(blocks[0][None], (4,) + blocks[0].shape)
     for k in (2, 1, 3):
         placed = lax.dynamic_update_slice_in_dim(placed, blocks[k][None], (x - k) & 3, 0)
@@ -105,7 +110,7 @@
     output0, sums0 = forward(gathered0, slow_weight, residual[0], targets[0], gain)
     totals0 = jnp.sum(to_all(sums0, TP), axis=0)
     pair1 = by_half(context1, other1, hi)
-    both1 = in_order(lax.optimization_barrier(along_x(after(pair1, sums0))), x)
+    both1 = in_order(along_x(after(pair1, sums0)), x, (1, 2))
     gathered1 = laid_out(both1)
     grad0 = backward(output0, totals0, targets[0], gain)
     weight_grad0 = contract_rows(gathered0, grad0)

time: 193 us -> 188 us (0.974)
  starting transfers between devices: 96.4 us -> 92.6 us
  matrix products: 12.8 us -> 9.66 us
    all_to_all x3, waiting for transfers between devices: 10.6 us -> 14.6 us  [to_all(): lax.all_to_all(jnp.broadcast_to(value[None], (count,) + value.shape), axi...]
    all_to_all x3, starting transfers between devices: 27.5 us -> 24.3 us  [to_all(): lax.all_to_all(jnp.broadcast_to(value[None], (count,) + value.shape), axi...]
  transfers between devices with their start and end apart: 17 -> 17, of which waited for: 11 -> 12; matrix products, arithmetic and copies ran while one was open for 6% -> 5% of each run, Pallas kernels for 0% -> 0%
where the time goes in v9:
time: 188 us; the launch traced here: 187 us
  starting transfers between devices  92.6 us (49%)
  waiting for transfers between devices  46.1 us (25%)
  blocking collectives  16.7 us (9%)
  local copies, waits for them, and re-layouts  10.7 us (6%)
  matrix products  9.66 us (5%)
  between operations  7.27 us (4%)
  other arithmetic  3.46 us (2%)
    ppermute x13, starting transfers between devices, shifted(): lax.ppermute(value, axis, [(i, (i + steps) % count) for i in range(count)])  62.7 us
    all_to_all x3, starting transfers between devices, to_all(): lax.all_to_all(jnp.broadcast_to(value[None], (count,) + value.shape), axi...  24.3 us
    ppermute x13, waiting for transfers between devices, shifted(): lax.ppermute(value, axis, [(i, (i + steps) % count) for i in range(count)])  20.2 us
    all_to_all x1, blocking collectives, body(): parts = lax.all_to_all(parts, 'y', 0, 0)  16.7 us
    all_to_all x3, waiting for transfers between devices, to_all(): lax.all_to_all(jnp.broadcast_to(value[None], (count,) + value.shape), axi...  14.6 us
    all_to_all x1, waiting for transfers between devices, body(): parts = lax.all_to_all(total.astype(BF16), 'z_lo', 0, 0)  11.4 us
    dot_general x2, matrix products, contract_rows(): lax.dot_general(left, right, (((0,), (0,)), ((), ())), preferred_element_...  6.34 us
    all_to_all x1, starting transfers between devices, body(): parts = lax.all_to_all(total.astype(BF16), 'z_lo', 0, 0)  5.63 us
  transfers between devices with their start and end apart: 17, of which 12 were waited for; matrix products, arithmetic and copies ran while one was open for 5% of the time, Pallas kernels for 0%

profile of v9, /device:TPU:32, one launch (start us, length us, event | category | flops | bytes accessed | tf_op | source)
XLA Modules:
  0.0 186.5 jit_solution(15149817735445908882)
XLA Ops:
  0.6 1.1 fusion.39
  1.8 14.8 %collective-permute-start = (bf16[512,256]{0,1:T(8,128)(2,1)S(1)}, bf16[512,256]{0,1:T(8,128)(2,1)S(1)}, u32[]{:S(2)}, u32[]{:S(2)}) collective-permute-start(bf16[512,256]{0,1:T(8,128)(2,1)S(1)} %bitcast.80), channel_id=1, source_target_pairs={{0,1},{1,0},{2,3},{3,2},{4,5},{5,4},{6,7},{7,6},{8,9},{9,8},{10,11... | collective-permute-start | bytes 786440 | tf_op jit(solution)/shard_map/ppermute | solution.py:24
  16.7 3.4 %collective-permute-start.1 = (bf16[512,256]{0,1:T(8,128)(2,1)S(1)}, bf16[512,256]{0,1:T(8,128)(2,1)S(1)}, u32[]{:S(2)}, u32[]{:S(2)}) collective-permute-start(bf16[512,256]{0,1:T(8,128)(2,1)S(1)} %bitcast.81), channel_id=1, source_target_pairs={{0,2},{2,4},{4,6},{6,0},{1,3},{3,5},{5,7},{7,1},{8,10},{10,12},{12... | collective-permute-start | bytes 786440 | tf_op jit(solution)/shard_map/ppermute | solution.py:24
  20.1 4.6 %collective-permute-start.2 = (bf16[512,256]{0,1:T(8,128)(2,1)S(1)}, bf16[512,256]{0,1:T(8,128)(2,1)S(1)}, u32[]{:S(2)}, u32[]{:S(2)}) collective-permute-start(bf16[512,256]{0,1:T(8,128)(2,1)S(1)} %bitcast.82), channel_id=1, source_target_pairs={{0,4},{2,6},{4,0},{6,2},{1,5},{3,7},{5,1},{7,3},{8,12},{10,14},{12... | collective-permute-start | bytes 786440 | tf_op jit(solution)/shard_map/ppermute | solution.py:24
  24.7 3.3 %collective-permute-start.3 = (bf16[512,256]{0,1:T(8,128)(2,1)S(1)}, bf16[512,256]{0,1:T(8,128)(2,1)S(1)}, u32[]{:S(2)}, u32[]{:S(2)}) collective-permute-start(bf16[512,256]{0,1:T(8,128)(2,1)S(1)} %bitcast.83), channel_id=1, source_target_pairs={{0,6},{2,0},{4,2},{6,4},{1,7},{3,1},{5,3},{7,5},{8,14},{10,8},{12,... | collective-permute-start | bytes 786440 | tf_op jit(solution)/shard_map/ppermute | solution.py:24
  28.1 1.3 fusion.40
  29.4 1.9 %collective-permute-start.4 = (f32[1]{0:T(128)}, f32[1]{0:T(128)}, u32[]{:S(2)}, u32[]{:S(2)}) collective-permute-start(f32[1]{0:T(128)} %bitcast.2), channel_id=1, source_target_pairs={{0,8},{8,16},{16,24},{24,32},{32,40},{40,48},{48,56},{56,64},{64,7... | collective-permute-start | bytes 20 | tf_op jit(solution)/shard_map/ppermute | solution.py:24
  32.0 4.5 %collective-permute-done.4 = f32[1]{0:T(128)} collective-permute-done((f32[1]{0:T(128)}, f32[1]{0:T(128)}, u32[]{:S(2)}, u32[]{:S(2)}) %collective-permute-start.4) | collective-permute-done | bytes 36 | tf_op jit(solution)/shard_map/ppermute | solution.py:24
  37.8 2.3 %collective-permute-done = bf16[512,256]{0,1:T(8,128)(2,1)S(1)} collective-permute-done((bf16[512,256]{0,1:T(8,128)(2,1)S(1)}, bf16[512,256]{0,1:T(8,128)(2,1)S(1)}, u32[]{:S(2)}, u32[]{:S(2)}) %collective-permute-start) | collective-permute-done | bytes 262176 | tf_op jit(solution)/shard_map/ppermute | solution.py:24
  40.1 1.1 broadcast_in_dim.14
  41.1 4.3 %all-to-all-start = ((bf16[4,512,256]{1,2,0:T(8,128)(2,1)}), bf16[4,512,256]{1,2,0:T(8,128)(2,1)S(1)}, u32[]{:S(2)}, u32[]{:S(2)}) async-start(bf16[4,512,256]{1,2,0:T(8,128)(2,1)} %broadcast_in_dim.14), calls=%async_computation | async-start | bytes 2097152 | tf_op jit(solution)/shard_map/all_to_all | solution.py:33
  45.6 12.1 %collective-permute-start.8 = (bf16[512,256]{0,1:T(8,128)(2,1)S(1)}, bf16[512,256]{0,1:T(8,128)(2,1)}, u32[]{:S(2)}, u32[]{:S(2)}) collective-permute-start(bf16[512,256]{0,1:T(8,128)(2,1)S(1)} %bitcast.85), channel_id=1, source_target_pairs={{0,1},{1,0},{2,3},{3,2},{4,5},{5,4},{6,7},{7,6},{8,9},{9,8},{10,11... | collective-permute-start | bytes 786440 | tf_op jit(solution)/shard_map/ppermute | solution.py:24
  57.9 1.9 %all-to-all-done = bf16[4,512,256]{1,2,0:T(8,128)(2,1)S(1)} async-done(((bf16[4,512,256]{1,2,0:T(8,128)(2,1)}), bf16[4,512,256]{1,2,0:T(8,128)(2,1)S(1)}, u32[]{:S(2)}, u32[]{:S(2)}) %all-to-all-start) | async-done | bytes 1048608 | tf_op jit(solution)/shard_map/all_to_all | solution.py:33
  60.1 1.0 copy-done.2
  61.1 0.6 copy-done.6
  61.7 0.4 copy-done.8
  62.1 0.9 multiply_reduce_fusion.2
  63.1 0.6 broadcast_in_dim.15
  63.7 12.1 %all-to-all-start.1 = ((f32[8,3,512]{2,1,0:T(4,128)}), f32[8,3,512]{2,1,0:T(4,128)S(1)}, u32[]{:S(2)}, u32[]{:S(2)}) async-start(f32[8,3,512]{2,1,0:T(4,128)} %broadcast_in_dim.15), calls=%async_computation.1 | async-start | bytes 131072 | tf_op jit(solution)/shard_map/all_to_all | solution.py:33
  76.4 1.1 collective-permute-done.8
  77.5 1.1 maximum_select_fusion.1
  78.6 5.2 %collective-permute-start.10 = (bf16[2,512,256]{1,2,0:T(8,128)(2,1)S(1)}, bf16[2,512,256]{1,2,0:T(8,128)(2,1)S(1)}, u32[]{:S(2)}, u32[]{:S(2)}) collective-permute-start(bf16[2,512,256]{1,2,0:T(8,128)(2,1)S(1)} %maximum_select_fusion.1), channel_id=1, source_target_pairs={{0,4},{2,6},{4,0},{6,2},{1,5},{3,7},{5,1},{7,3},{8,12},{10,14},{12... | collective-permute-start | bytes 1572872 | tf_op jit(solution)/shard_map/ppermute | solution.py:24
  83.8 2.5 %collective-permute-start.9 = (bf16[2,512,256]{1,2,0:T(8,128)(2,1)S(1)}, bf16[2,512,256]{1,2,0:T(8,128)(2,1)}, u32[]{:S(2)}, u32[]{:S(2)}) collective-permute-start(bf16[2,512,256]{1,2,0:T(8,128)(2,1)S(1)} %maximum_select_fusion.1), channel_id=1, source_target_pairs={{0,2},{2,4},{4,6},{6,0},{1,3},{3,5},{5,7},{7,1},{8,10},{10,12},{12... | collective-permute-start | bytes 1572872 | tf_op jit(solution)/shard_map/ppermute | solution.py:24
  86.3 4.8 %all-to-all-done.1 = f32[8,3,512]{2,1,0:T(4,128)S(1)} async-done(((f32[8,3,512]{2,1,0:T(4,128)}), f32[8,3,512]{2,1,0:T(4,128)S(1)}, u32[]{:S(2)}, u32[]{:S(2)}) %all-to-all-start.1) | async-done | bytes 49184 | tf_op jit(solution)/shard_map/all_to_all | solution.py:33
  91.1 2.5 %multiply_convert_fusion.1 = (bf16[2048,288]{0,1:T(8,128)(2,1)S(1)}, f32[2048,288]{0,1:T(8,128)S(1)}) fusion(f32[]{:T(128)S(6)} %sub.56, bf16[512,2048]{0,1:T(8,128)(2,1)} %bitcast.79, f32[512,288]{0,1:T(8,128)S(1)} %get-tuple-element.45, f32[512]{0:T(512)S(1)} %bitcast.89, f32[512]{0:T(512)S(1)} %bitcast.88, f32[288]{0:T(512)S(1)} %copy-done.4, ...), kind=kOutput, calls=%fused_computation.4 | convolution fusion | flops 606486528 | bytes 6529028 | tf_op jit(solution)/shard_map/dot_general | solution.py:37
  93.6 1.9 %collective-permute-start.5 = (bf16[2048,288]{0,1:T(8,128)(2,1)S(1)}, bf16[2048,288]{0,1:T(8,128)(2,1)S(1)}, u32[]{:S(2)}, u32[]{:S(2)}) collective-permute-start(bf16[2048,288]{0,1:T(8,128)(2,1)S(1)} %get-tuple-element.46), channel_id=1, source_target_pairs={{0,8},{8,16},{16,24},{24,32},{32,40},{40,48},{48,56},{56,64},{64,7... | collective-permute-start | bytes 3538952 | tf_op jit(solution)/shard_map/ppermute | solution.py:24
  95.6 3.0 %collective-permute-start.11 = (bf16[2,512,256]{1,2,0:T(8,128)(2,1)S(1)}, bf16[2,512,256]{1,2,0:T(8,128)(2,1)S(1)}, u32[]{:S(2)}, u32[]{:S(2)}) collective-permute-start(bf16[2,512,256]{1,2,0:T(8,128)(2,1)S(1)} %maximum_select_fusion.1), channel_id=1, source_target_pairs={{0,6},{2,0},{4,2},{6,4},{1,7},{3,1},{5,3},{7,5},{8,14},{10,8},{12,... | collective-permute-start | bytes 1572872 | tf_op jit(solution)/shard_map/ppermute | solution.py:24
  98.6 4.8 %collective-permute-start.6 = (f32[1]{0:T(128)}, f32[1]{0:T(128)}, u32[]{:S(2)}, u32[]{:S(2)}) collective-permute-start(f32[1]{0:T(128)} %mul.138), channel_id=1, source_target_pairs={{0,16},{8,24},{16,32},{24,40},{32,48},{40,56},{48,64},{56,72},{64,... | collective-permute-start | bytes 20 | tf_op jit(solution)/shard_map/ppermute | solution.py:24
  103.4 4.0 %collective-permute-done.9 = bf16[2,512,256]{1,2,0:T(8,128)(2,1)} collective-permute-done((bf16[2,512,256]{1,2,0:T(8,128)(2,1)S(1)}, bf16[2,512,256]{1,2,0:T(8,128)(2,1)}, u32[]{:S(2)}, u32[]{:S(2)}) %collective-permute-start.9) | collective-permute-done | bytes 524320 | tf_op jit(solution)/shard_map/ppermute | solution.py:24
  107.6 1.2 bitcast_dynamic-update-slice_fusion.1
  108.9 2.7 %collective-permute-done.11 = bf16[2,512,256]{1,2,0:T(8,128)(2,1)S(1)} collective-permute-done((bf16[2,512,256]{1,2,0:T(8,128)(2,1)S(1)}, bf16[2,512,256]{1,2,0:T(8,128)(2,1)S(1)}, u32[]{:S(2)}, u32[]{:S(2)}) %collective-permute-start.11) | collective-permute-done | bytes 524320 | tf_op jit(solution)/shard_map/ppermute | solution.py:24
  111.7 1.6 collective-permute-done.5
  113.3 2.4 %multiply_reduce_fusion = (f32[512]{0:T(512)S(1)}, f32[512]{0:T(512)S(1)}, f32[512]{0:T(512)S(1)}, f32[512,288]{0,1:T(8,128)}) fusion(f32[288]{0:T(512)S(1)} %copy-done.4, bf16[2,512,288]{1,2,0:T(8,128)(2,1)S(1)} %copy-done.10, bf16[512,2048]{0,1:T(8,128)(2,1)S(1)} %bitcast.76, bf16[2048,288]{0,1:T(8,128)(2,1)S(1)} %copy-done.3, ...), kind=kOutput, calls=%fused_computation.26 | convolution fusion | flops 609581568 | bytes 8002696 | tf_op jit(solution)/shard_map/dot_general | solution.py:72
  115.7 0.6 broadcast_in_dim.20
  116.3 8.0 %all-to-all-start.2 = ((f32[8,3,512]{2,1,0:T(4,128)}), f32[8,3,512]{2,1,0:T(4,128)S(1)}, u32[]{:S(2)}, u32[]{:S(2)}) async-start(f32[8,3,512]{2,1,0:T(4,128)} %broadcast_in_dim.20), calls=%async_computation.2 | async-start | bytes 131072 | tf_op jit(solution)/shard_map/all_to_all | solution.py:33
  125.5 3.2 %collective-permute-start.7 = (f32[1]{0:T(128)}, f32[1]{0:T(128)}, u32[]{:S(2)}, u32[]{:S(2)}) collective-permute-start(f32[1]{0:T(128)} %add.82), channel_id=1, source_target_pairs={{0,496},{8,504},{16,0},{24,8},{32,16},{40,24},{48,32},{56,40},{64,... | collective-permute-start | bytes 20 | tf_op jit(solution)/shard_map/ppermute | solution.py:24
  129.4 1.7 collective-permute-done.7
  131.7 7.9 %all-to-all-done.2 = f32[8,3,512]{2,1,0:T(4,128)S(1)} async-done(((f32[8,3,512]{2,1,0:T(4,128)}), f32[8,3,512]{2,1,0:T(4,128)S(1)}, u32[]{:S(2)}, u32[]{:S(2)}) %all-to-all-start.2) | async-done | bytes 49184 | tf_op jit(solution)/shard_map/all_to_all | solution.py:33
  139.6 3.9 %multiply_convert_fusion = bf16[2048,288]{0,1:T(8,128)(2,1)S(1)} fusion(f32[]{:T(128)} %bitcast.18, bf16[512,2048]{0,1:T(8,128)(2,1)S(1)} %bitcast.77, f32[512,288]{0,1:T(8,128)} %get-tuple-element.48, bf16[2048,288]{0,1:T(8,128)(2,1)} %copy-done.5, f32[2048,288]{0,1:T(8,128)} %copy-done.11, f32[]{:T(128)} %bitcast.3, f32[512]{0:T(512)S(1)} %bitcast.87, ...), kind=kOutput, calls=%fused_computation.1 | convolution fusion | flops 608845824 | bytes 7707904 | tf_op jit(solution)/shard_map/dot_general | solution.py:37
  143.5 0.8 copy.34
  144.5 1.9 %collective-permute-start.12 = (bf16[8,4,32,288]{3,2,1,0:T(8,128)(2,1)S(1)}, bf16[8,4,32,288]{3,2,1,0:T(8,128)(2,1)S(1)}, u32[]{:S(2)}, u32[]{:S(2)}) collective-permute-start(bf16[8,4,32,288]{3,2,1,0:T(8,128)(2,1)S(1)} %select_bitcast_fusion), channel_id=1, source_target_pairs={{0,8},{8,0},{1,9},{9,1},{2,10},{10,2},{3,11},{11,3},{4,12},{12,4},... | collective-permute-start | bytes 1769480 | tf_op jit(solution)/shard_map/ppermute | solution.py:24
  146.4 2.3 %collective-permute-done.12 = bf16[8,4,32,288]{3,2,1,0:T(8,128)(2,1)S(1)} collective-permute-done((bf16[8,4,32,288]{3,2,1,0:T(8,128)(2,1)S(1)}, bf16[8,4,32,288]{3,2,1,0:T(8,128)(2,1)S(1)}, u32[]{:S(2)}, u32[]{:S(2)}) %collective-permute-start.12) | collective-permute-done | bytes 589856 | tf_op jit(solution)/shard_map/ppermute | solution.py:24
  149.1 16.7 %all_to_all.25 = bf16[4,8,32,288]{3,2,1,0:T(8,128)(2,1)S(1)} all-to-all(bf16[4,8,32,288]{3,2,1,0:T(8,128)(2,1)S(1)} %copy.35), channel_id=1, replica_groups=mesh['z_lo'=8,'y'=4,'core'=2,'x'=4,'z_hi'=2] {'y'}, dimensions={0} | all-to-all | bytes 1179648 | tf_op jit(solution)/shard_map/all_to_all | solution.py:139
  165.7 0.9 reduce_sum.101
  166.6 5.6 %all-to-all-start.4 = ((bf16[8,32,288]{2,1,0:T(8,128)(2,1)}), bf16[8,32,288]{2,1,0:T(8,128)(2,1)S(1)}, u32[]{:S(2)}, u32[]{:S(2)}) async-start(bf16[8,32,288]{2,1,0:T(8,128)(2,1)} %reduce_sum.101), calls=%async_computation.4 | async-start | bytes 393216 | tf_op jit(solution)/shard_map/all_to_all | solution.py:141
  172.2 1.0 constant_dynamic-slice_fusion
  173.3 11.4 %all-to-all-done.4 = bf16[8,32,288]{2,1,0:T(8,128)(2,1)S(1)} async-done(((bf16[8,32,288]{2,1,0:T(8,128)(2,1)}), bf16[8,32,288]{2,1,0:T(8,128)(2,1)S(1)}, u32[]{:S(2)}, u32[]{:S(2)}) %all-to-all-start.4) | async-done | bytes 147488 | tf_op jit(solution)/shard_map/all_to_all | solution.py:141
  184.7 0.7 multiply_subtract_fusion
  (48 shorter events, 1.8 us)
Async XLA Ops:
  1.8 38.2 %collective-permute-start = (bf16[512,256]{0,1:T(8,128)(2,1)S(1)}, bf16[512,256]{0,1:T(8,128)(2,1)S(1)}, u32[]{:S(2)}, u32[]{:S(2)}) collective-permute-start(bf16[512,256]{0,1:T(8,128)(2,1)S(1)} %bitcast.80), channel_id=1, source_target_pairs={{0,1},{1,0},{2,3},{3,2},{4,5},{5,4},{6,7},{7,6},{8,9},{9,8},{10,11... | collective-permute-start | bytes 786440 | tf_op jit(solution)/shard_map/ppermute | solution.py:24
  16.7 23.4 %collective-permute-start.1 = (bf16[512,256]{0,1:T(8,128)(2,1)S(1)}, bf16[512,256]{0,1:T(8,128)(2,1)S(1)}, u32[]{:S(2)}, u32[]{:S(2)}) collective-permute-start(bf16[512,256]{0,1:T(8,128)(2,1)S(1)} %bitcast.81), channel_id=1, source_target_pairs={{0,2},{2,4},{4,6},{6,0},{1,3},{3,5},{5,7},{7,1},{8,10},{10,12},{12... | collective-permute-start | bytes 786440 | tf_op jit(solution)/shard_map/ppermute | solution.py:24
  20.1 20.0 %collective-permute-start.2 = (bf16[512,256]{0,1:T(8,128)(2,1)S(1)}, bf16[512,256]{0,1:T(8,128)(2,1)S(1)}, u32[]{:S(2)}, u32[]{:S(2)}) collective-permute-start(bf16[512,256]{0,1:T(8,128)(2,1)S(1)} %bitcast.82), channel_id=1, source_target_pairs={{0,4},{2,6},{4,0},{6,2},{1,5},{3,7},{5,1},{7,3},{8,12},{10,14},{12... | collective-permute-start | bytes 786440 | tf_op jit(solution)/shard_map/ppermute | solution.py:24
  24.7 15.3 %collective-permute-start.3 = (bf16[512,256]{0,1:T(8,128)(2,1)S(1)}, bf16[512,256]{0,1:T(8,128)(2,1)S(1)}, u32[]{:S(2)}, u32[]{:S(2)}) collective-permute-start(bf16[512,256]{0,1:T(8,128)(2,1)S(1)} %bitcast.83), channel_id=1, source_target_pairs={{0,6},{2,0},{4,2},{6,4},{1,7},{3,1},{5,3},{7,5},{8,14},{10,8},{12,... | collective-permute-start | bytes 786440 | tf_op jit(solution)/shard_map/ppermute | solution.py:24
  29.4 7.1 %collective-permute-start.4 = (f32[1]{0:T(128)}, f32[1]{0:T(128)}, u32[]{:S(2)}, u32[]{:S(2)}) collective-permute-start(f32[1]{0:T(128)} %bitcast.2), channel_id=1, source_target_pairs={{0,8},{8,16},{16,24},{24,32},{32,40},{40,48},{48,56},{56,64},{64,7... | collective-permute-start | bytes 20 | tf_op jit(solution)/shard_map/ppermute | solution.py:24
  41.1 18.6 %all-to-all-start = ((bf16[4,512,256]{1,2,0:T(8,128)(2,1)}), bf16[4,512,256]{1,2,0:T(8,128)(2,1)S(1)}, u32[]{:S(2)}, u32[]{:S(2)}) async-start(bf16[4,512,256]{1,2,0:T(8,128)(2,1)} %broadcast_in_dim.14), calls=%async_computation | async-start | bytes 2097152 | tf_op jit(solution)/shard_map/all_to_all | solution.py:33
  45.6 32.0 %collective-permute-start.8 = (bf16[512,256]{0,1:T(8,128)(2,1)S(1)}, bf16[512,256]{0,1:T(8,128)(2,1)}, u32[]{:S(2)}, u32[]{:S(2)}) collective-permute-start(bf16[512,256]{0,1:T(8,128)(2,1)S(1)} %bitcast.85), channel_id=1, source_target_pairs={{0,1},{1,0},{2,3},{3,2},{4,5},{5,4},{6,7},{7,6},{8,9},{9,8},{10,11... | collective-permute-start | bytes 786440 | tf_op jit(solution)/shard_map/ppermute | solution.py:24
  59.7 1.3 copy-start.2
  59.8 1.3 copy-start.4
  59.8 2.0 %copy-start.6 = (bf16[2,512,288]{1,2,0:T(8,128)(2,1)S(1)}, bf16[2,512,288]{1,2,0:T(8,128)(2,1)}, u32[]{:S(2)}) copy-start(bf16[2,512,288]{1,2,0:T(8,128)(2,1)} %param.8) | copy-start | bytes 1769476
  59.8 2.4 %copy-start.8 = (bf16[2,512,288]{1,2,0:T(8,128)(2,1)S(1)}, bf16[2,512,288]{1,2,0:T(8,128)(2,1)}, u32[]{:S(2)}) copy-start(bf16[2,512,288]{1,2,0:T(8,128)(2,1)} %param.9) | copy-start | bytes 1769476
  60.1 3.0 %copy-start = (bf16[4,2,512,256]{2,3,1,0:T(8,128)(2,1)}, bf16[4,2,512,256]{2,3,1,0:T(8,128)(2,1)S(1)}, u32[]{:S(2)}) copy-start(bf16[4,2,512,256]{2,3,1,0:T(8,128)(2,1)S(1)} %maximum_select_fusion) | copy-start | bytes 6291460
  62.1 29.0 %copy-start.9 = (bf16[2,512,288]{1,2,0:T(8,128)(2,1)S(1)}, bf16[2,512,288]{1,2,0:T(8,128)(2,1)}, u32[]{:S(2)}) copy-start(bf16[2,512,288]{1,2,0:T(8,128)(2,1)} %param.9) | copy-start | bytes 1769476
  63.7 27.4 %all-to-all-start.1 = ((f32[8,3,512]{2,1,0:T(4,128)}), f32[8,3,512]{2,1,0:T(4,128)S(1)}, u32[]{:S(2)}, u32[]{:S(2)}) async-start(f32[8,3,512]{2,1,0:T(4,128)} %broadcast_in_dim.15), calls=%async_computation.1 | async-start | bytes 131072 | tf_op jit(solution)/shard_map/all_to_all | solution.py:33
  78.6 24.8 %collective-permute-start.10 = (bf16[2,512,256]{1,2,0:T(8,128)(2,1)S(1)}, bf16[2,512,256]{1,2,0:T(8,128)(2,1)S(1)}, u32[]{:S(2)}, u32[]{:S(2)}) collective-permute-start(bf16[2,512,256]{1,2,0:T(8,128)(2,1)S(1)} %maximum_select_fusion.1), channel_id=1, source_target_pairs={{0,4},{2,6},{4,0},{6,2},{1,5},{3,7},{5,1},{7,3},{8,12},{10,14},{12... | collective-permute-start | bytes 1572872 | tf_op jit(solution)/shard_map/ppermute | solution.py:24
  83.8 23.6 %collective-permute-start.9 = (bf16[2,512,256]{1,2,0:T(8,128)(2,1)S(1)}, bf16[2,512,256]{1,2,0:T(8,128)(2,1)}, u32[]{:S(2)}, u32[]{:S(2)}) collective-permute-start(bf16[2,512,256]{1,2,0:T(8,128)(2,1)S(1)} %maximum_select_fusion.1), channel_id=1, source_target_pairs={{0,2},{2,4},{4,6},{6,0},{1,3},{3,5},{5,7},{7,1},{8,10},{10,12},{12... | collective-permute-start | bytes 1572872 | tf_op jit(solution)/shard_map/ppermute | solution.py:24
  93.6 22.1 %copy-start.11 = (f32[2048,288]{0,1:T(8,128)}, f32[2048,288]{0,1:T(8,128)S(1)}, u32[]{:S(2)}) copy-start(f32[2048,288]{0,1:T(8,128)S(1)} %get-tuple-element.47) | copy-start | bytes 7077892
  93.6 19.6 %collective-permute-start.5 = (bf16[2048,288]{0,1:T(8,128)(2,1)S(1)}, bf16[2048,288]{0,1:T(8,128)(2,1)S(1)}, u32[]{:S(2)}, u32[]{:S(2)}) collective-permute-start(bf16[2048,288]{0,1:T(8,128)(2,1)S(1)} %get-tuple-element.46), channel_id=1, source_target_pairs={{0,8},{8,16},{16,24},{24,32},{32,40},{40,48},{48,56},{56,64},{64,7... | collective-permute-start | bytes 3538952 | tf_op jit(solution)/shard_map/ppermute | solution.py:24
  95.6 16.0 %collective-permute-start.11 = (bf16[2,512,256]{1,2,0:T(8,128)(2,1)S(1)}, bf16[2,512,256]{1,2,0:T(8,128)(2,1)S(1)}, u32[]{:S(2)}, u32[]{:S(2)}) collective-permute-start(bf16[2,512,256]{1,2,0:T(8,128)(2,1)S(1)} %maximum_select_fusion.1), channel_id=1, source_target_pairs={{0,6},{2,0},{4,2},{6,4},{1,7},{3,1},{5,3},{7,5},{8,14},{10,8},{12,... | collective-permute-start | bytes 1572872 | tf_op jit(solution)/shard_map/ppermute | solution.py:24
  98.6 13.1 %collective-permute-start.6 = (f32[1]{0:T(128)}, f32[1]{0:T(128)}, u32[]{:S(2)}, u32[]{:S(2)}) collective-permute-start(f32[1]{0:T(128)} %mul.138), channel_id=1, source_target_pairs={{0,16},{8,24},{16,32},{24,40},{32,48},{40,56},{48,64},{56,72},{64,... | collective-permute-start | bytes 20 | tf_op jit(solution)/shard_map/ppermute | solution.py:24
  107.6 5.7 %copy-start.3 = (bf16[2048,288]{0,1:T(8,128)(2,1)S(1)}, bf16[2048,288]{0,1:T(8,128)(2,1)}, u32[]{:S(2)}) copy-start(bf16[2048,288]{0,1:T(8,128)(2,1)} %param.11) | copy-start | bytes 3538948
  107.6 5.7 %copy-start.7 = (bf16[2,512,288]{1,2,0:T(8,128)(2,1)S(1)}, bf16[2,512,288]{1,2,0:T(8,128)(2,1)}, u32[]{:S(2)}) copy-start(bf16[2,512,288]{1,2,0:T(8,128)(2,1)} %param.8) | copy-start | bytes 1769476
  107.6 5.7 %copy-start.10 = (bf16[2,512,288]{1,2,0:T(8,128)(2,1)S(1)}, bf16[2,512,288]{1,2,0:T(8,128)(2,1)}, u32[]{:S(2)}) copy-start(bf16[2,512,288]{1,2,0:T(8,128)(2,1)} %param.9) | copy-start | bytes 1769476
  113.3 2.4 %copy-start.5 = (bf16[2048,288]{0,1:T(8,128)(2,1)}, bf16[2048,288]{0,1:T(8,128)(2,1)S(1)}, u32[]{:S(2)}) copy-start(bf16[2048,288]{0,1:T(8,128)(2,1)S(1)} %collective-permute-done.5) | copy-start | bytes 3538948
  116.3 23.2 %all-to-all-start.2 = ((f32[8,3,512]{2,1,0:T(4,128)}), f32[8,3,512]{2,1,0:T(4,128)S(1)}, u32[]{:S(2)}, u32[]{:S(2)}) async-start(f32[8,3,512]{2,1,0:T(4,128)} %broadcast_in_dim.20), calls=%async_computation.2 | async-start | bytes 131072 | tf_op jit(solution)/shard_map/all_to_all | solution.py:33
  125.5 5.5 %collective-permute-start.7 = (f32[1]{0:T(128)}, f32[1]{0:T(128)}, u32[]{:S(2)}, u32[]{:S(2)}) collective-permute-start(f32[1]{0:T(128)} %add.82), channel_id=1, source_target_pairs={{0,496},{8,504},{16,0},{24,8},{32,16},{40,24},{48,32},{56,40},{64,... | collective-permute-start | bytes 20 | tf_op jit(solution)/shard_map/ppermute | solution.py:24
  144.5 4.2 %collective-permute-start.12 = (bf16[8,4,32,288]{3,2,1,0:T(8,128)(2,1)S(1)}, bf16[8,4,32,288]{3,2,1,0:T(8,128)(2,1)S(1)}, u32[]{:S(2)}, u32[]{:S(2)}) collective-permute-start(bf16[8,4,32,288]{3,2,1,0:T(8,128)(2,1)S(1)} %select_bitcast_fusion), channel_id=1, source_target_pairs={{0,8},{8,0},{1,9},{9,1},{2,10},{10,2},{3,11},{11,3},{4,12},{12,4},... | collective-permute-start | bytes 1769480 | tf_op jit(solution)/shard_map/ppermute | solution.py:24
  149.0 35.7 %copy-start.1 = (f32[32,288]{1,0:T(8,128)S(1)}, f32[32,288]{1,0:T(8,128)}, u32[]{:S(2)}) copy-start(f32[32,288]{1,0:T(8,128)} %param.12) | copy-start | bytes 110596
  166.6 18.1 %all-to-all-start.4 = ((bf16[8,32,288]{2,1,0:T(8,128)(2,1)}), bf16[8,32,288]{2,1,0:T(8,128)(2,1)S(1)}, u32[]{:S(2)}, u32[]{:S(2)}) async-start(bf16[8,32,288]{2,1,0:T(8,128)(2,1)} %reduce_sum.101), calls=%async_computation.4 | async-start | bytes 393216 | tf_op jit(solution)/shard_map/all_to_all | solution.py:141

commit v10 on v9

--- a/solution.py
+++ b/solution.py
@@ -116,9 +116,9 @@
     weight_grad0 = contract_rows(gathered0, grad0)
 
     pushed = ((1.0 - share0) * weight_grad0).astype(BF16)
+    mass_in = shifted(leaving, REP, 2)
+    pushed, mass_in = lax.optimization_barrier((pushed, mass_in))
     incoming = shifted(pushed, REP, 1)
-    mass_in = shifted(leaving, REP, 2)
-    incoming, mass_in = lax.optimization_barrier((incoming, mass_in))
     step0 = share0 * weight_grad0 + incoming.astype(F32)
     quotient1 = (anchor - (LR / mass1[0]) * step0).astype(BF16)
     output1, sums1 = forward(gathered1, quotient1, residual[1], targets[1], gain)

time: 188 us -> 192 us (1.021)
  starting transfers between devices: 92.6 us -> 101 us
  waiting for transfers between devices: 46.1 us -> 42.8 us
    all_to_all x3, starting transfers between devices: 24.3 us -> 29 us  [to_all(): lax.all_to_all(jnp.broadcast_to(value[None], (count,) + value.shape), axi...]
    all_to_all x3, waiting for transfers between devices: 14.6 us -> 9.96 us  [to_all(): lax.all_to_all(jnp.broadcast_to(value[None], (count,) + value.shape), axi...]
    ppermute x13, starting transfers between devices: 62.7 us -> 65.8 us  [shifted(): lax.ppermute(value, axis, [(i, (i + steps) % count) for i in range(count)])]
  transfers between devices with their start and end apart: 17 -> 17, of which waited for: 12 -> 11; matrix products, arithmetic and copies ran while one was open for 5% -> 5% of each run, Pallas kernels for 0% -> 0%
where the time goes in v10:
time: 192 us; the launch traced here: 190 us
  starting transfers between devices  101 us (53%)
  waiting for transfers between devices  42.8 us (22%)
  blocking collectives  16.1 us (8%)
  local copies, waits for them, and re-layouts  10.7 us (6%)
  matrix products  9.66 us (5%)
  between operations  7.26 us (4%)
  other arithmetic  3.46 us (2%)
    ppermute x13, starting transfers between devices, shifted(): lax.ppermute(value, axis, [(i, (i + steps) % count) for i in range(count)])  65.8 us
    all_to_all x3, starting transfers between devices, to_all(): lax.all_to_all(jnp.broadcast_to(value[None], (count,) + value.shape), axi...  29 us
    ppermute x13, waiting for transfers between devices, shifted(): lax.ppermute(value, axis, [(i, (i + steps) % count) for i in range(count)])  21.5 us
    all_to_all x1, blocking collectives, body(): parts = lax.all_to_all(parts, 'y', 0, 0)  16.1 us
    all_to_all x1, waiting for transfers between devices, body(): parts = lax.all_to_all(total.astype(BF16), 'z_lo', 0, 0)  11.4 us
    all_to_all x3, waiting for transfers between devices, to_all(): lax.all_to_all(jnp.broadcast_to(value[None], (count,) + value.shape), axi...  9.96 us
    dot_general x2, matrix products, contract_rows(): lax.dot_general(left, right, (((0,), (0,)), ((), ())), preferred_element_...  6.34 us
    all_to_all x1, starting transfers between devices, body(): parts = lax.all_to_all(total.astype(BF16), 'z_lo', 0, 0)  5.65 us
  transfers between devices with their start and end apart: 17, of which 11 were waited for; matrix products, arithmetic and copies ran while one was open for 5% of the time, Pallas kernels for 0%

profile of v10, /device:TPU:32, one launch (start us, length us, event | category | flops | bytes accessed | tf_op | source)
XLA Modules:
  0.0 190.5 jit_solution(11528364847440150273)
XLA Ops:
  0.6 1.1 fusion.39
  1.8 14.8 %collective-permute-start = (bf16[512,256]{0,1:T(8,128)(2,1)S(1)}, bf16[512,256]{0,1:T(8,128)(2,1)S(1)}, u32[]{:S(2)}, u32[]{:S(2)}) collective-permute-start(bf16[512,256]{0,1:T(8,128)(2,1)S(1)} %bitcast.80), channel_id=1, source_target_pairs={{0,1},{1,0},{2,3},{3,2},{4,5},{5,4},{6,7},{7,6},{8,9},{9,8},{10,11... | collective-permute-start | bytes 786440 | tf_op jit(solution)/shard_map/ppermute | solution.py:24
  16.7 3.4 %collective-permute-start.1 = (bf16[512,256]{0,1:T(8,128)(2,1)S(1)}, bf16[512,256]{0,1:T(8,128)(2,1)S(1)}, u32[]{:S(2)}, u32[]{:S(2)}) collective-permute-start(bf16[512,256]{0,1:T(8,128)(2,1)S(1)} %bitcast.81), channel_id=1, source_target_pairs={{0,2},{2,4},{4,6},{6,0},{1,3},{3,5},{5,7},{7,1},{8,10},{10,12},{12... | collective-permute-start | bytes 786440 | tf_op jit(solution)/shard_map/ppermute | solution.py:24
  20.1 4.6 %collective-permute-start.2 = (bf16[512,256]{0,1:T(8,128)(2,1)S(1)}, bf16[512,256]{0,1:T(8,128)(2,1)S(1)}, u32[]{:S(2)}, u32[]{:S(2)}) collective-permute-start(bf16[512,256]{0,1:T(8,128)(2,1)S(1)} %bitcast.82), channel_id=1, source_target_pairs={{0,4},{2,6},{4,0},{6,2},{1,5},{3,7},{5,1},{7,3},{8,12},{10,14},{12... | collective-permute-start | bytes 786440 | tf_op jit(solution)/shard_map/ppermute | solution.py:24
  24.7 3.3 %collective-permute-start.3 = (bf16[512,256]{0,1:T(8,128)(2,1)S(1)}, bf16[512,256]{0,1:T(8,128)(2,1)S(1)}, u32[]{:S(2)}, u32[]{:S(2)}) collective-permute-start(bf16[512,256]{0,1:T(8,128)(2,1)S(1)} %bitcast.83), channel_id=1, source_target_pairs={{0,6},{2,0},{4,2},{6,4},{1,7},{3,1},{5,3},{7,5},{8,14},{10,8},{12,... | collective-permute-start | bytes 786440 | tf_op jit(solution)/shard_map/ppermute | solution.py:24
  28.1 1.3 fusion.40
  29.4 1.9 %collective-permute-start.4 = (f32[1]{0:T(128)}, f32[1]{0:T(128)}, u32[]{:S(2)}, u32[]{:S(2)}) collective-permute-start(f32[1]{0:T(128)} %bitcast.2), channel_id=1, source_target_pairs={{0,8},{8,16},{16,24},{24,32},{32,40},{40,48},{48,56},{56,64},{64,7... | collective-permute-start | bytes 20 | tf_op jit(solution)/shard_map/ppermute | solution.py:24
  32.0 4.5 %collective-permute-done.4 = f32[1]{0:T(128)} collective-permute-done((f32[1]{0:T(128)}, f32[1]{0:T(128)}, u32[]{:S(2)}, u32[]{:S(2)}) %collective-permute-start.4) | collective-permute-done | bytes 36 | tf_op jit(solution)/shard_map/ppermute | solution.py:24
  37.8 2.3 %collective-permute-done = bf16[512,256]{0,1:T(8,128)(2,1)S(1)} collective-permute-done((bf16[512,256]{0,1:T(8,128)(2,1)S(1)}, bf16[512,256]{0,1:T(8,128)(2,1)S(1)}, u32[]{:S(2)}, u32[]{:S(2)}) %collective-permute-start) | collective-permute-done | bytes 262176 | tf_op jit(solution)/shard_map/ppermute | solution.py:24
  40.1 1.1 broadcast_in_dim.14
  41.1 4.3 %all-to-all-start = ((bf16[4,512,256]{1,2,0:T(8,128)(2,1)}), bf16[4,512,256]{1,2,0:T(8,128)(2,1)S(1)}, u32[]{:S(2)}, u32[]{:S(2)}) async-start(bf16[4,512,256]{1,2,0:T(8,128)(2,1)} %broadcast_in_dim.14), calls=%async_computation | async-start | bytes 2097152 | tf_op jit(solution)/shard_map/all_to_all | solution.py:33
  45.6 12.1 %collective-permute-start.8 = (bf16[512,256]{0,1:T(8,128)(2,1)S(1)}, bf16[512,256]{0,1:T(8,128)(2,1)}, u32[]{:S(2)}, u32[]{:S(2)}) collective-permute-start(bf16[512,256]{0,1:T(8,128)(2,1)S(1)} %bitcast.85), channel_id=1, source_target_pairs={{0,1},{1,0},{2,3},{3,2},{4,5},{5,4},{6,7},{7,6},{8,9},{9,8},{10,11... | collective-permute-start | bytes 786440 | tf_op jit(solution)/shard_map/ppermute | solution.py:24
  57.9 1.9 all-to-all-done
  60.1 1.0 copy-done.2
  61.1 0.6 copy-done.6
  61.7 0.4 copy-done.8
  62.1 0.9 multiply_reduce_fusion.2
  63.1 0.6 broadcast_in_dim.15
  63.7 12.1 %all-to-all-start.1 = ((f32[8,3,512]{2,1,0:T(4,128)}), f32[8,3,512]{2,1,0:T(4,128)S(1)}, u32[]{:S(2)}, u32[]{:S(2)}) async-start(f32[8,3,512]{2,1,0:T(4,128)} %broadcast_in_dim.15), calls=%async_computation.1 | async-start | bytes 131072 | tf_op jit(solution)/shard_map/all_to_all | solution.py:33
  76.4 4.8 %collective-permute-start.5 = (f32[1]{0:T(128)}, f32[1]{0:T(128)}, u32[]{:S(2)}, u32[]{:S(2)}) collective-permute-start(f32[1]{0:T(128)} %mul.138), channel_id=1, source_target_pairs={{0,16},{8,24},{16,32},{24,40},{32,48},{40,56},{48,64},{56,72},{64,... | collective-permute-start | bytes 20 | tf_op jit(solution)/shard_map/ppermute | solution.py:24
  81.2 1.1 maximum_select_fusion.1
  82.3 5.4 %collective-permute-start.10 = (bf16[2,512,256]{1,2,0:T(8,128)(2,1)S(1)}, bf16[2,512,256]{1,2,0:T(8,128)(2,1)S(1)}, u32[]{:S(2)}, u32[]{:S(2)}) collective-permute-start(bf16[2,512,256]{1,2,0:T(8,128)(2,1)S(1)} %maximum_select_fusion.1), channel_id=1, source_target_pairs={{0,4},{2,6},{4,0},{6,2},{1,5},{3,7},{5,1},{7,3},{8,12},{10,14},{12... | collective-permute-start | bytes 1572872 | tf_op jit(solution)/shard_map/ppermute | solution.py:24
  87.7 2.5 %collective-permute-start.9 = (bf16[2,512,256]{1,2,0:T(8,128)(2,1)S(1)}, bf16[2,512,256]{1,2,0:T(8,128)(2,1)}, u32[]{:S(2)}, u32[]{:S(2)}) collective-permute-start(bf16[2,512,256]{1,2,0:T(8,128)(2,1)S(1)} %maximum_select_fusion.1), channel_id=1, source_target_pairs={{0,2},{2,4},{4,6},{6,0},{1,3},{3,5},{5,7},{7,1},{8,10},{10,12},{12... | collective-permute-start | bytes 1572872 | tf_op jit(solution)/shard_map/ppermute | solution.py:24
  90.2 0.9 all-to-all-done.1
  91.2 2.5 %multiply_convert_fusion.1 = (bf16[2048,288]{0,1:T(8,128)(2,1)S(1)}, f32[2048,288]{0,1:T(8,128)S(1)}) fusion(f32[]{:T(128)S(6)} %sub.56, bf16[512,2048]{0,1:T(8,128)(2,1)} %bitcast.79, f32[512,288]{0,1:T(8,128)S(1)} %get-tuple-element.45, f32[512]{0:T(512)S(1)} %bitcast.89, f32[512]{0:T(512)S(1)} %bitcast.88, f32[288]{0:T(512)S(1)} %copy-done.4, ...), kind=kOutput, calls=%fused_computation.4 | convolution fusion | flops 606486528 | bytes 6529028 | tf_op jit(solution)/shard_map/dot_general | solution.py:37
  93.7 1.9 %collective-permute-start.7 = (bf16[2048,288]{0,1:T(8,128)(2,1)S(1)}, bf16[2048,288]{0,1:T(8,128)(2,1)S(1)}, u32[]{:S(2)}, u32[]{:S(2)}) collective-permute-start(bf16[2048,288]{0,1:T(8,128)(2,1)S(1)} %get-tuple-element.24), channel_id=1, source_target_pairs={{0,8},{8,16},{16,24},{24,32},{32,40},{40,48},{48,56},{56,64},{64,7... | collective-permute-start | bytes 3538952 | tf_op jit(solution)/shard_map/ppermute | solution.py:24
  95.6 3.7 %collective-permute-start.11 = (bf16[2,512,256]{1,2,0:T(8,128)(2,1)S(1)}, bf16[2,512,256]{1,2,0:T(8,128)(2,1)S(1)}, u32[]{:S(2)}, u32[]{:S(2)}) collective-permute-start(bf16[2,512,256]{1,2,0:T(8,128)(2,1)S(1)} %maximum_select_fusion.1), channel_id=1, source_target_pairs={{0,6},{2,0},{4,2},{6,4},{1,7},{3,1},{5,3},{7,5},{8,14},{10,8},{12,... | collective-permute-start | bytes 1572872 | tf_op jit(solution)/shard_map/ppermute | solution.py:24
  99.4 1.4 collective-permute-done.10
  100.8 7.1 %collective-permute-done.9 = bf16[2,512,256]{1,2,0:T(8,128)(2,1)} collective-permute-done((bf16[2,512,256]{1,2,0:T(8,128)(2,1)S(1)}, bf16[2,512,256]{1,2,0:T(8,128)(2,1)}, u32[]{:S(2)}, u32[]{:S(2)}) %collective-permute-start.9) | collective-permute-done | bytes 524320 | tf_op jit(solution)/shard_map/ppermute | solution.py:24
  108.2 1.2 bitcast_dynamic-update-slice_fusion.1
  109.4 2.2 %collective-permute-done.11 = bf16[2,512,256]{1,2,0:T(8,128)(2,1)S(1)} collective-permute-done((bf16[2,512,256]{1,2,0:T(8,128)(2,1)S(1)}, bf16[2,512,256]{1,2,0:T(8,128)(2,1)S(1)}, u32[]{:S(2)}, u32[]{:S(2)}) %collective-permute-start.11) | collective-permute-done | bytes 524320 | tf_op jit(solution)/shard_map/ppermute | solution.py:24
  111.7 1.6 collective-permute-done.7
  113.3 2.4 %multiply_reduce_fusion = (f32[512]{0:T(512)S(1)}, f32[512]{0:T(512)S(1)}, f32[512]{0:T(512)S(1)}, f32[512,288]{0,1:T(8,128)}) fusion(f32[288]{0:T(512)S(1)} %copy-done.4, bf16[2,512,288]{1,2,0:T(8,128)(2,1)S(1)} %copy-done.10, bf16[512,2048]{0,1:T(8,128)(2,1)S(1)} %bitcast.76, bf16[2048,288]{0,1:T(8,128)(2,1)S(1)} %copy-done.3, ...), kind=kOutput, calls=%fused_computation.26 | convolution fusion | flops 609581568 | bytes 8002696 | tf_op jit(solution)/shard_map/dot_general | solution.py:72
  115.7 0.6 broadcast_in_dim.20
  116.4 12.7 %all-to-all-start.2 = ((f32[8,3,512]{2,1,0:T(4,128)}), f32[8,3,512]{2,1,0:T(4,128)S(1)}, u32[]{:S(2)}, u32[]{:S(2)}) async-start(f32[8,3,512]{2,1,0:T(4,128)} %broadcast_in_dim.20), calls=%async_computation.2 | async-start | bytes 131072 | tf_op jit(solution)/shard_map/all_to_all | solution.py:33
  130.3 5.3 %collective-permute-start.6 = (f32[1]{0:T(128)}, f32[1]{0:T(128)}, u32[]{:S(2)}, u32[]{:S(2)}) collective-permute-start(f32[1]{0:T(128)} %add.82), channel_id=1, source_target_pairs={{0,496},{8,504},{16,0},{24,8},{32,16},{40,24},{48,32},{56,40},{64,... | collective-permute-start | bytes 20 | tf_op jit(solution)/shard_map/ppermute | solution.py:24
  136.9 7.2 %all-to-all-done.2 = f32[8,3,512]{2,1,0:T(4,128)S(1)} async-done(((f32[8,3,512]{2,1,0:T(4,128)}), f32[8,3,512]{2,1,0:T(4,128)S(1)}, u32[]{:S(2)}, u32[]{:S(2)}) %all-to-all-start.2) | async-done | bytes 49184 | tf_op jit(solution)/shard_map/all_to_all | solution.py:33
  144.2 3.9 %multiply_convert_fusion = bf16[2048,288]{0,1:T(8,128)(2,1)S(1)} fusion(f32[]{:T(128)} %bitcast.18, bf16[512,2048]{0,1:T(8,128)(2,1)S(1)} %bitcast.77, f32[512,288]{0,1:T(8,128)} %get-tuple-element.48, bf16[2048,288]{0,1:T(8,128)(2,1)} %copy-done.5, f32[2048,288]{0,1:T(8,128)} %copy-done.11, f32[]{:T(128)} %bitcast.3, f32[512]{0:T(512)S(1)} %bitcast.87, ...), kind=kOutput, calls=%fused_computation.1 | convolution fusion | flops 608845824 | bytes 7707904 | tf_op jit(solution)/shard_map/dot_general | solution.py:37
  148.0 0.8 copy.34
  149.0 1.9 %collective-permute-start.12 = (bf16[8,4,32,288]{3,2,1,0:T(8,128)(2,1)S(1)}, bf16[8,4,32,288]{3,2,1,0:T(8,128)(2,1)S(1)}, u32[]{:S(2)}, u32[]{:S(2)}) collective-permute-start(bf16[8,4,32,288]{3,2,1,0:T(8,128)(2,1)S(1)} %select_bitcast_fusion), channel_id=1, source_target_pairs={{0,8},{8,0},{1,9},{9,1},{2,10},{10,2},{3,11},{11,3},{4,12},{12,4},... | collective-permute-start | bytes 1769480 | tf_op jit(solution)/shard_map/ppermute | solution.py:24
  150.9 2.3 %collective-permute-done.12 = bf16[8,4,32,288]{3,2,1,0:T(8,128)(2,1)S(1)} collective-permute-done((bf16[8,4,32,288]{3,2,1,0:T(8,128)(2,1)S(1)}, bf16[8,4,32,288]{3,2,1,0:T(8,128)(2,1)S(1)}, u32[]{:S(2)}, u32[]{:S(2)}) %collective-permute-start.12) | collective-permute-done | bytes 589856 | tf_op jit(solution)/shard_map/ppermute | solution.py:24
  153.2 0.3 fusion.3
  153.6 16.1 %all_to_all.25 = bf16[4,8,32,288]{3,2,1,0:T(8,128)(2,1)S(1)} all-to-all(bf16[4,8,32,288]{3,2,1,0:T(8,128)(2,1)S(1)} %copy.35), channel_id=1, replica_groups=mesh['z_lo'=8,'y'=4,'core'=2,'x'=4,'z_hi'=2] {'y'}, dimensions={0} | all-to-all | bytes 1179648 | tf_op jit(solution)/shard_map/all_to_all | solution.py:139
  169.7 0.9 reduce_sum.101
  170.5 5.6 %all-to-all-start.4 = ((bf16[8,32,288]{2,1,0:T(8,128)(2,1)}), bf16[8,32,288]{2,1,0:T(8,128)(2,1)S(1)}, u32[]{:S(2)}, u32[]{:S(2)}) async-start(bf16[8,32,288]{2,1,0:T(8,128)(2,1)} %reduce_sum.101), calls=%async_computation.4 | async-start | bytes 393216 | tf_op jit(solution)/shard_map/all_to_all | solution.py:141
  176.2 1.0 constant_dynamic-slice_fusion
  177.3 11.4 %all-to-all-done.4 = bf16[8,32,288]{2,1,0:T(8,128)(2,1)S(1)} async-done(((bf16[8,32,288]{2,1,0:T(8,128)(2,1)}), bf16[8,32,288]{2,1,0:T(8,128)(2,1)S(1)}, u32[]{:S(2)}, u32[]{:S(2)}) %all-to-all-start.4) | async-done | bytes 147488 | tf_op jit(solution)/shard_map/all_to_all | solution.py:141
  188.7 0.7 multiply_subtract_fusion
  (48 shorter events, 1.5 us)
Async XLA Ops:
  1.8 38.2 %collective-permute-start = (bf16[512,256]{0,1:T(8,128)(2,1)S(1)}, bf16[512,256]{0,1:T(8,128)(2,1)S(1)}, u32[]{:S(2)}, u32[]{:S(2)}) collective-permute-start(bf16[512,256]{0,1:T(8,128)(2,1)S(1)} %bitcast.80), channel_id=1, source_target_pairs={{0,1},{1,0},{2,3},{3,2},{4,5},{5,4},{6,7},{7,6},{8,9},{9,8},{10,11... | collective-permute-start | bytes 786440 | tf_op jit(solution)/shard_map/ppermute | solution.py:24
  16.7 23.4 %collective-permute-start.1 = (bf16[512,256]{0,1:T(8,128)(2,1)S(1)}, bf16[512,256]{0,1:T(8,128)(2,1)S(1)}, u32[]{:S(2)}, u32[]{:S(2)}) collective-permute-start(bf16[512,256]{0,1:T(8,128)(2,1)S(1)} %bitcast.81), channel_id=1, source_target_pairs={{0,2},{2,4},{4,6},{6,0},{1,3},{3,5},{5,7},{7,1},{8,10},{10,12},{12... | collective-permute-start | bytes 786440 | tf_op jit(solution)/shard_map/ppermute | solution.py:24
  20.1 20.0 %collective-permute-start.2 = (bf16[512,256]{0,1:T(8,128)(2,1)S(1)}, bf16[512,256]{0,1:T(8,128)(2,1)S(1)}, u32[]{:S(2)}, u32[]{:S(2)}) collective-permute-start(bf16[512,256]{0,1:T(8,128)(2,1)S(1)} %bitcast.82), channel_id=1, source_target_pairs={{0,4},{2,6},{4,0},{6,2},{1,5},{3,7},{5,1},{7,3},{8,12},{10,14},{12... | collective-permute-start | bytes 786440 | tf_op jit(solution)/shard_map/ppermute | solution.py:24
  24.7 15.3 %collective-permute-start.3 = (bf16[512,256]{0,1:T(8,128)(2,1)S(1)}, bf16[512,256]{0,1:T(8,128)(2,1)S(1)}, u32[]{:S(2)}, u32[]{:S(2)}) collective-permute-start(bf16[512,256]{0,1:T(8,128)(2,1)S(1)} %bitcast.83), channel_id=1, source_target_pairs={{0,6},{2,0},{4,2},{6,4},{1,7},{3,1},{5,3},{7,5},{8,14},{10,8},{12,... | collective-permute-start | bytes 786440 | tf_op jit(solution)/shard_map/ppermute | solution.py:24
  29.4 7.1 %collective-permute-start.4 = (f32[1]{0:T(128)}, f32[1]{0:T(128)}, u32[]{:S(2)}, u32[]{:S(2)}) collective-permute-start(f32[1]{0:T(128)} %bitcast.2), channel_id=1, source_target_pairs={{0,8},{8,16},{16,24},{24,32},{32,40},{40,48},{48,56},{56,64},{64,7... | collective-permute-start | bytes 20 | tf_op jit(solution)/shard_map/ppermute | solution.py:24
  41.1 18.6 %all-to-all-start = ((bf16[4,512,256]{1,2,0:T(8,128)(2,1)}), bf16[4,512,256]{1,2,0:T(8,128)(2,1)S(1)}, u32[]{:S(2)}, u32[]{:S(2)}) async-start(bf16[4,512,256]{1,2,0:T(8,128)(2,1)} %broadcast_in_dim.14), calls=%async_computation | async-start | bytes 2097152 | tf_op jit(solution)/shard_map/all_to_all | solution.py:33
  45.6 35.6 %collective-permute-start.8 = (bf16[512,256]{0,1:T(8,128)(2,1)S(1)}, bf16[512,256]{0,1:T(8,128)(2,1)}, u32[]{:S(2)}, u32[]{:S(2)}) collective-permute-start(bf16[512,256]{0,1:T(8,128)(2,1)S(1)} %bitcast.85), channel_id=1, source_target_pairs={{0,1},{1,0},{2,3},{3,2},{4,5},{5,4},{6,7},{7,6},{8,9},{9,8},{10,11... | collective-permute-start | bytes 786440 | tf_op jit(solution)/shard_map/ppermute | solution.py:24
  59.7 1.3 copy-start.2
  59.8 1.3 copy-start.4
  59.8 2.0 %copy-start.6 = (bf16[2,512,288]{1,2,0:T(8,128)(2,1)S(1)}, bf16[2,512,288]{1,2,0:T(8,128)(2,1)}, u32[]{:S(2)}) copy-start(bf16[2,512,288]{1,2,0:T(8,128)(2,1)} %param.8) | copy-start | bytes 1769476
  59.8 2.4 %copy-start.8 = (bf16[2,512,288]{1,2,0:T(8,128)(2,1)S(1)}, bf16[2,512,288]{1,2,0:T(8,128)(2,1)}, u32[]{:S(2)}) copy-start(bf16[2,512,288]{1,2,0:T(8,128)(2,1)} %param.9) | copy-start | bytes 1769476
  60.1 3.0 %copy-start = (bf16[4,2,512,256]{2,3,1,0:T(8,128)(2,1)}, bf16[4,2,512,256]{2,3,1,0:T(8,128)(2,1)S(1)}, u32[]{:S(2)}) copy-start(bf16[4,2,512,256]{2,3,1,0:T(8,128)(2,1)S(1)} %maximum_select_fusion) | copy-start | bytes 6291460
  62.1 29.0 %copy-start.9 = (bf16[2,512,288]{1,2,0:T(8,128)(2,1)S(1)}, bf16[2,512,288]{1,2,0:T(8,128)(2,1)}, u32[]{:S(2)}) copy-start(bf16[2,512,288]{1,2,0:T(8,128)(2,1)} %param.9) | copy-start | bytes 1769476
  63.7 27.4 %all-to-all-start.1 = ((f32[8,3,512]{2,1,0:T(4,128)}), f32[8,3,512]{2,1,0:T(4,128)S(1)}, u32[]{:S(2)}, u32[]{:S(2)}) async-start(f32[8,3,512]{2,1,0:T(4,128)} %broadcast_in_dim.15), calls=%async_computation.1 | async-start | bytes 131072 | tf_op jit(solution)/shard_map/all_to_all | solution.py:33
  76.4 17.3 %collective-permute-start.5 = (f32[1]{0:T(128)}, f32[1]{0:T(128)}, u32[]{:S(2)}, u32[]{:S(2)}) collective-permute-start(f32[1]{0:T(128)} %mul.138), channel_id=1, source_target_pairs={{0,16},{8,24},{16,32},{24,40},{32,48},{40,56},{48,64},{56,72},{64,... | collective-permute-start | bytes 20 | tf_op jit(solution)/shard_map/ppermute | solution.py:24
  82.3 18.5 %collective-permute-start.10 = (bf16[2,512,256]{1,2,0:T(8,128)(2,1)S(1)}, bf16[2,512,256]{1,2,0:T(8,128)(2,1)S(1)}, u32[]{:S(2)}, u32[]{:S(2)}) collective-permute-start(bf16[2,512,256]{1,2,0:T(8,128)(2,1)S(1)} %maximum_select_fusion.1), channel_id=1, source_target_pairs={{0,4},{2,6},{4,0},{6,2},{1,5},{3,7},{5,1},{7,3},{8,12},{10,14},{12... | collective-permute-start | bytes 1572872 | tf_op jit(solution)/shard_map/ppermute | solution.py:24
  87.7 20.2 %collective-permute-start.9 = (bf16[2,512,256]{1,2,0:T(8,128)(2,1)S(1)}, bf16[2,512,256]{1,2,0:T(8,128)(2,1)}, u32[]{:S(2)}, u32[]{:S(2)}) collective-permute-start(bf16[2,512,256]{1,2,0:T(8,128)(2,1)S(1)} %maximum_select_fusion.1), channel_id=1, source_target_pairs={{0,2},{2,4},{4,6},{6,0},{1,3},{3,5},{5,7},{7,1},{8,10},{10,12},{12... | collective-permute-start | bytes 1572872 | tf_op jit(solution)/shard_map/ppermute | solution.py:24
  93.6 22.1 %copy-start.11 = (f32[2048,288]{0,1:T(8,128)}, f32[2048,288]{0,1:T(8,128)S(1)}, u32[]{:S(2)}) copy-start(f32[2048,288]{0,1:T(8,128)S(1)} %get-tuple-element.47) | copy-start | bytes 7077892
  93.7 19.6 %collective-permute-start.7 = (bf16[2048,288]{0,1:T(8,128)(2,1)S(1)}, bf16[2048,288]{0,1:T(8,128)(2,1)S(1)}, u32[]{:S(2)}, u32[]{:S(2)}) collective-permute-start(bf16[2048,288]{0,1:T(8,128)(2,1)S(1)} %get-tuple-element.24), channel_id=1, source_target_pairs={{0,8},{8,16},{16,24},{24,32},{32,40},{40,48},{48,56},{56,64},{64,7... | collective-permute-start | bytes 3538952 | tf_op jit(solution)/shard_map/ppermute | solution.py:24
  95.6 16.0 %collective-permute-start.11 = (bf16[2,512,256]{1,2,0:T(8,128)(2,1)S(1)}, bf16[2,512,256]{1,2,0:T(8,128)(2,1)S(1)}, u32[]{:S(2)}, u32[]{:S(2)}) collective-permute-start(bf16[2,512,256]{1,2,0:T(8,128)(2,1)S(1)} %maximum_select_fusion.1), channel_id=1, source_target_pairs={{0,6},{2,0},{4,2},{6,4},{1,7},{3,1},{5,3},{7,5},{8,14},{10,8},{12,... | collective-permute-start | bytes 1572872 | tf_op jit(solution)/shard_map/ppermute | solution.py:24
  108.1 5.2 %copy-start.3 = (bf16[2048,288]{0,1:T(8,128)(2,1)S(1)}, bf16[2048,288]{0,1:T(8,128)(2,1)}, u32[]{:S(2)}) copy-start(bf16[2048,288]{0,1:T(8,128)(2,1)} %param.11) | copy-start | bytes 3538948
  108.1 5.2 %copy-start.7 = (bf16[2,512,288]{1,2,0:T(8,128)(2,1)S(1)}, bf16[2,512,288]{1,2,0:T(8,128)(2,1)}, u32[]{:S(2)}) copy-start(bf16[2,512,288]{1,2,0:T(8,128)(2,1)} %param.8) | copy-start | bytes 1769476
  108.1 5.2 %copy-start.10 = (bf16[2,512,288]{1,2,0:T(8,128)(2,1)S(1)}, bf16[2,512,288]{1,2,0:T(8,128)(2,1)}, u32[]{:S(2)}) copy-start(bf16[2,512,288]{1,2,0:T(8,128)(2,1)} %param.9) | copy-start | bytes 1769476
  113.3 2.4 %copy-start.5 = (bf16[2048,288]{0,1:T(8,128)(2,1)}, bf16[2048,288]{0,1:T(8,128)(2,1)S(1)}, u32[]{:S(2)}) copy-start(bf16[2048,288]{0,1:T(8,128)(2,1)S(1)} %collective-permute-done.7) | copy-start | bytes 3538948
  116.4 27.8 %all-to-all-start.2 = ((f32[8,3,512]{2,1,0:T(4,128)}), f32[8,3,512]{2,1,0:T(4,128)S(1)}, u32[]{:S(2)}, u32[]{:S(2)}) async-start(f32[8,3,512]{2,1,0:T(4,128)} %broadcast_in_dim.20), calls=%async_computation.2 | async-start | bytes 131072 | tf_op jit(solution)/shard_map/all_to_all | solution.py:33
  130.3 6.0 %collective-permute-start.6 = (f32[1]{0:T(128)}, f32[1]{0:T(128)}, u32[]{:S(2)}, u32[]{:S(2)}) collective-permute-start(f32[1]{0:T(128)} %add.82), channel_id=1, source_target_pairs={{0,496},{8,504},{16,0},{24,8},{32,16},{40,24},{48,32},{56,40},{64,... | collective-permute-start | bytes 20 | tf_op jit(solution)/shard_map/ppermute | solution.py:24
  149.0 4.2 %collective-permute-start.12 = (bf16[8,4,32,288]{3,2,1,0:T(8,128)(2,1)S(1)}, bf16[8,4,32,288]{3,2,1,0:T(8,128)(2,1)S(1)}, u32[]{:S(2)}, u32[]{:S(2)}) collective-permute-start(bf16[8,4,32,288]{3,2,1,0:T(8,128)(2,1)S(1)} %select_bitcast_fusion), channel_id=1, source_target_pairs={{0,8},{8,0},{1,9},{9,1},{2,10},{10,2},{3,11},{11,3},{4,12},{12,4},... | collective-permute-start | bytes 1769480 | tf_op jit(solution)/shard_map/ppermute | solution.py:24
  153.6 35.1 %copy-start.1 = (f32[32,288]{1,0:T(8,128)S(1)}, f32[32,288]{1,0:T(8,128)}, u32[]{:S(2)}) copy-start(f32[32,288]{1,0:T(8,128)} %param.12) | copy-start | bytes 110596
  170.5 18.1 %all-to-all-start.4 = ((bf16[8,32,288]{2,1,0:T(8,128)(2,1)}), bf16[8,32,288]{2,1,0:T(8,128)(2,1)S(1)}, u32[]{:S(2)}, u32[]{:S(2)}) async-start(bf16[8,32,288]{2,1,0:T(8,128)(2,1)} %reduce_sum.101), calls=%async_computation.4 | async-start | bytes 393216 | tf_op jit(solution)/shard_map/all_to_all | solution.py:141
